TPU v7x, 32 devices: a whole 2x2x4 slice. The times are simulated.
32 devices in a mesh: dp: 16 (over z, y, core), mp: 2 (over x).
Axes of the slice: x: 2, y: 2, z: 4, core: 2. Of those that a mesh axis runs over, the one named last changes fastest.
Arguments:
- upper_first: bfloat16 [4096, 4096], P('dp'), may hold values from -6 to 6
- upper_second: bfloat16 [4096, 4096], P('dp'), may hold values from -24 to 24
- grad_first: bfloat16 [4096, 4096], P('dp'), may hold values from -6 to 6
- grad_second: bfloat16 [4096, 4096], P('dp'), may hold values from -6 to 6
- norm_gain: bfloat16 [4096], replicated, may hold values from 0.25 to 1.75
- up_weight: bfloat16 [4096, 11264], P('dp', 'mp'), may hold values from -0.09375 to 0.09375
- down_weight: bfloat16 [4096, 11264], P('dp', 'mp'), may hold values from -0.0546875 to 0.0546875
- adapter_down: bfloat16 [4096, 64], replicated, may hold values from -0.09375 to 0.09375
- adapter_up: bfloat16 [64, 4096], replicated, may hold values from -0.75 to 0.75
Outputs:
- lower_first: bfloat16 [4096, 4096], P('dp', 'mp')
- lower_second: bfloat16 [4096, 4096], P('dp', 'mp')
- input_grad_first: bfloat16 [4096, 4096], P('dp', 'mp')
- input_grad_second: bfloat16 [4096, 4096], P('dp')
- adapter_down_grad: float32 [4096, 64], P('mp')
- adapter_up_grad: float32 [64, 4096], P(None, 'mp')
All inputs are finite; a program needn't handle non-finite values.
Results may differ from a plain program's by a relative error of at most 0.009.
Values may be sent and summed in bfloat16 or wider, within the bound.
No kernel may reach another device: no remote copies, remote signals or barrier semaphores. Data moves between devices by JAX's collectives and lax.ppermute only.
A program may use at most 192 MiB of HBM per device.

v0:
```python
import math

import jax
import jax.numpy as jnp
from jax import lax
from jax.sharding import PartitionSpec as P

coupling = 0.5


def silu_slope(argument):
    sigmoid_value = jax.nn.sigmoid(argument)
    return sigmoid_value * (1.0 + argument * (1.0 - sigmoid_value))


def on_device(
    upper_first,
    upper_second,
    grad_first,
    grad_second,
    norm_gain,
    up_weight,
    down_weight,
    adapter_down,
    adapter_up,
):
    groups = lax.axis_size("mp")
    mp_rank = lax.axis_index("mp")
    model_width = upper_first.shape[1]
    share_width = model_width // groups
    offset = mp_rank * share_width
    tokens_all = upper_first.shape[0] * lax.axis_size("dp")
    grad_scale = 1.0 / math.sqrt(tokens_all)
    up_full = lax.all_gather(up_weight, "dp", axis=0, tiled=True)
    pre_adapter = jnp.dot(upper_first, adapter_down, preferred_element_type=jnp.float32)
    squashed = jax.nn.silu(pre_adapter).astype(jnp.bfloat16)
    adapted = jnp.dot(squashed, adapter_up, preferred_element_type=jnp.float32)
    lower_full = (upper_second.astype(jnp.float32) - adapted).astype(jnp.bfloat16)
    lower_value = lower_full.astype(jnp.float32)
    inverse_rms = lax.rsqrt(jnp.mean(lower_value * lower_value, axis=1, keepdims=True) + 1e-05)
    gain_full = norm_gain.astype(jnp.float32)
    normed = (lower_value * inverse_rms * gain_full).astype(jnp.bfloat16)
    hidden_pre = jnp.dot(normed, up_full, preferred_element_type=jnp.float32)
    activated = jax.nn.silu(hidden_pre).astype(jnp.bfloat16)
    down_full = lax.all_gather(down_weight, "dp", axis=0, tiled=True)
    partial_out = lax.dot_general(
        activated, down_full, (((1,), (1,)), ((), ())), preferred_element_type=jnp.float32
    )
    frozen_share = lax.psum_scatter(
        partial_out.astype(jnp.bfloat16), "mp", scatter_dimension=1, tiled=True
    ).astype(jnp.float32)
    upper_slice = lax.dynamic_slice_in_dim(upper_first, offset, share_width, 1)
    lower_first = ((upper_slice.astype(jnp.float32) - frozen_share) / coupling).astype(jnp.bfloat16)
    adapter_slope = jnp.einsum(
        "td,rd->tr", grad_second, adapter_up, preferred_element_type=jnp.float32
    )
    adapter_pre_grad = (adapter_slope * silu_slope(pre_adapter)).astype(jnp.bfloat16)
    back_adapter = jnp.einsum(
        "tr,dr->td", adapter_pre_grad, adapter_down, preferred_element_type=jnp.float32
    )
    carried = (grad_first.astype(jnp.float32) + back_adapter).astype(jnp.bfloat16)
    carried_slice = lax.dynamic_slice_in_dim(carried, offset, share_width, 1)
    input_grad_first = (coupling * carried_slice.astype(jnp.float32)).astype(jnp.bfloat16)
    down_grad_part = (
        jnp.einsum("td,tr->dr", upper_slice, adapter_pre_grad, preferred_element_type=jnp.float32)
        * grad_scale
    )
    second_slice = lax.dynamic_slice_in_dim(grad_second, offset, share_width, 1)
    up_grad_part = (
        jnp.einsum("tr,td->rd", squashed, second_slice, preferred_element_type=jnp.float32)
        * grad_scale
    )
    adapter_down_grad, adapter_up_grad = lax.psum((down_grad_part, up_grad_part), "dp")
    act_grad = jnp.dot(carried, down_full, preferred_element_type=jnp.float32)
    pre_grad = (act_grad * silu_slope(hidden_pre)).astype(jnp.bfloat16)
    normed_part = lax.dot_general(
        pre_grad, up_full, (((1,), (1,)), ((), ())), preferred_element_type=jnp.float32
    )
    stat_part = jnp.sum(hidden_pre * pre_grad.astype(jnp.float32), axis=1)
    stat_tiled = jnp.broadcast_to(stat_part[:, None], (stat_part.shape[0], groups))
    normed_share, curvature = (
        lax.psum_scatter(normed_part, "mp", scatter_dimension=1, tiled=True),
        lax.psum_scatter(stat_tiled, "mp", scatter_dimension=1, tiled=True),
    )
    gain_share = lax.dynamic_slice_in_dim(gain_full, offset, share_width, 0)
    lower_share = lax.dynamic_slice_in_dim(lower_value, offset, share_width, 1)
    correction = lower_share * inverse_rms * inverse_rms * curvature / model_width
    second_share = (
        second_slice.astype(jnp.float32) + inverse_rms * gain_share * normed_share - correction
    ).astype(jnp.bfloat16)
    input_grad_second = lax.all_gather(second_share, "mp", axis=1, tiled=True)
    lower_second = lax.dynamic_slice_in_dim(lower_full, offset, share_width, 1)
    return (
        lower_first,
        lower_second,
        input_grad_first,
        input_grad_second,
        adapter_down_grad,
        adapter_up_grad,
    )


def solution(mesh):
    return jax.shard_map(
        on_device,
        mesh=mesh,
        in_specs=(
            P("dp", None),
            P("dp", None),
            P("dp", None),
            P("dp", None),
            P(),
            P("dp", "mp"),
            P("dp", "mp"),
            P(),
            P(),
        ),
        out_specs=(
            P("dp", "mp"),
            P("dp", "mp"),
            P("dp", "mp"),
            P("dp", None),
            P("mp", None),
            P(None, "mp"),
        ),
        check_vma=False,
    )
```

profile of v0, /device:TPU:0, one launch (start us, length us, event | category | flops | bytes accessed | tf_op | source)
XLA Modules:
  0.0 745.0 jit_solution(4005912032443671779)
XLA Ops:
  7.2 0.0 copy-start
  7.2 0.0 copy-start.9
  7.2 0.0 copy-start.6
  7.2 0.0 copy-start.3
  7.2 0.0 all-gather.4.cloned.1.call-start
  7.3 0.7 all-gather.4.cloned.1.call-update
  7.9 0.0 all-gather.6.cloned.1.call-start
  8.0 0.7 all-gather.6.cloned.1.call-update
  8.7 0.0 reduce-scatter.5.cloned.1.call-start
  8.7 0.0 copy-done.9
  8.8 0.0 copy-done.6
  8.8 0.2 copy-done.3
  9.0 0.8 fusion.14
  9.8 0.0 copy-done
  9.8 0.0 copy-start.2
  9.8 0.0 copy-start.5
  9.8 3.9 multiply_reduce_fusion.1
  13.7 0.0 copy-done.2
  13.7 0.8 fusion.8
  14.5 0.0 copy-done.5
  14.5 2.0 fusion.2
  16.5 223.2 %all-gather.4.cloned.1.call-done = bf16[4096,5632]{1,0:T(8,128)(2,1)} async-done(((bf16[256,5632]{1,0:T(8,128)(2,1)}), bf16[4096,5632]{1,0:T(8,128)(2,1)}) %all-gather.4.cloned.1.call-update) | async-done | bytes 46137360 | tf_op jit(solution)/shard_map/all_gather | solution.py:34
  239.7 25.5 %fusion.4 = f32[256,5632]{1,0:T(8,128)} fusion(bf16[4096,5632]{1,0:T(8,128)(2,1)} %all-gather.4.cloned.1.call-done, f32[4096]{0:T(1024)S(1)} %convert_element_type.65, f32[256]{0:T(256)S(1)} %add_rsqrt_fusion, bf16[256,4096]{1,0:T(8,128)(2,1)} %get-tuple-element.9), kind=kOutput, calls=%fused_computation.15 | convolution fusion | flops 11815354368 | bytes 54019072 | tf_op jit(solution)/shard_map/dot_general | solution.py:43
  265.2 203.5 %all-gather.6.cloned.1.call-done = bf16[4096,5632]{1,0:T(8,128)(2,1)} async-done(((bf16[256,5632]{1,0:T(8,128)(2,1)}), bf16[4096,5632]{1,0:T(8,128)(2,1)}) %all-gather.6.cloned.1.call-update) | async-done | bytes 46137360 | tf_op jit(solution)/shard_map/all_gather | solution.py:45
  468.7 23.2 %multiply_reduce_fusion = (f32[256]{0:T(256)S(1)}, bf16[256,5632]{1,0:T(8,128)(2,1)}) fusion(f32[256,5632]{1,0:T(8,128)} %fusion.4, bf16[256,4096]{1,0:T(8,128)(2,1)} %fusion.2, bf16[4096,5632]{1,0:T(8,128)(2,1)} %all-gather.6.cloned.1.call-done), kind=kOutput, calls=%fused_computation.2 | convolution fusion | flops 11828461568 | bytes 56886272 | tf_op jit(solution)/shard_map/dot_general | solution.py:74
  491.9 21.0 %fusion.15 = f32[256,4096]{1,0:T(8,128)} fusion(bf16[256,5632]{1,0:T(8,128)(2,1)} %get-tuple-element.11, bf16[4096,5632]{1,0:T(8,128)(2,1)} %all-gather.4.cloned.1.call-done), kind=kOutput, calls=%fused_computation.35 | convolution fusion | flops 11811160064 | bytes 53215232 | tf_op jit(solution)/shard_map/dot_general | solution.py:76
  512.9 0.0 reduce-scatter.5.cloned.1.call-update
  512.9 0.0 reduce-scatter.3.cloned.1.call-start
  512.9 22.2 %convolution_convert_fusion = bf16[256,4096]{1,0:T(8,128)(2,1)} fusion(bf16[4096,5632]{1,0:T(8,128)(2,1)} %all-gather.6.cloned.1.call-done, f32[256,5632]{1,0:T(8,128)} %fusion.4), kind=kOutput, calls=%fused_computation.9 | convolution fusion | flops 11819417600 | bytes 54001664 | tf_op jit(solution)/shard_map/dot_general | solution.py:46
  535.2 0.0 reduce-scatter.3.cloned.1.call-update
  535.2 0.0 all-gather.8.cloned.1.call-start
  535.3 0.0 copy-start.10
  535.3 4.0 convert_element_type.64
  539.3 0.0 copy-done.10
  539.3 0.6 dynamic-slice
  539.9 5.0 all-reduce
  544.9 0.7 constant_dynamic-slice_fusion.1
  545.5 21.9 %reduce-scatter.5.cloned.1.call-done = f32[256,2048]{1,0:T(8,128)} async-done(((f32[256,4096]{1,0:T(8,128)}), f32[256,2048]{1,0:T(8,128)}) %reduce-scatter.5.cloned.1.call-update) | async-done | bytes 2097168 | tf_op jit(solution)/shard_map/reduce_scatter | solution.py:82
  567.4 4.0 subtract_convert_fusion
  571.4 0.0 all-gather.8.cloned.1.call-update
  571.4 0.0 all-reduce.4.cloned.1.call-start
  571.5 2.3 convolution_multiply_fusion.1
  573.8 1.1 convolution_multiply_fusion.2
  574.9 0.0 copy-start.4
  574.9 0.0 all-reduce.4.cloned.1.call-update
  574.9 2.7 constant_dynamic-slice_fusion
  577.7 2.4 multiply_convert_fusion.4
  580.1 21.4 %reduce-scatter.3.cloned.1.call-done = bf16[256,2048]{1,0:T(8,128)(2,1)} async-done(((bf16[256,4096]{1,0:T(8,128)(2,1)}), bf16[256,2048]{1,0:T(8,128)(2,1)}) %reduce-scatter.3.cloned.1.call-update) | async-done | bytes 1048592 | tf_op jit(solution)/shard_map/reduce_scatter | solution.py:49
  601.5 0.0 copy-done.4
  601.5 2.6 multiply_convert_fusion.5
  604.1 32.0 %all-gather.8.cloned.1.call-done = bf16[256,4096]{1,0:T(8,128)(2,1)} async-done(((bf16[256,2048]{1,0:T(8,128)(2,1)}), bf16[256,4096]{1,0:T(8,128)(2,1)}) %all-gather.8.cloned.1.call-update) | async-done | bytes 2097168 | tf_op jit(solution)/shard_map/all_gather | solution.py:91
  636.0 97.3 %all-reduce.4.cloned.1.call-done = (f32[2048,64]{0,1:T(8,128)}, f32[64,2048]{1,0:T(8,128)}) async-done(((f32[2048,64]{0,1:T(8,128)}, f32[64,2048]{1,0:T(8,128)}), (f32[2048,64]{0,1:T(8,128)}, f32[64,2048]{1,0:T(8,128)})) %all-reduce.4.cloned.1.call-update) | async-done | bytes 1048592 | tf_op jit(solution)/shard_map/psum | solution.py:73
  733.3 0.0 copy-start.8
  733.3 0.0 copy-start.7
  733.3 0.0 copy-start.1
  733.3 3.2 copy.18
  736.6 0.0 copy-done.8
  736.6 0.8 copy.19
  737.4 0.0 copy-done.7
  737.4 0.8 copy.20
  738.2 0.0 copy-done.1
  (4 shorter events, 0.0 us)
Async XLA Ops:
  7.2 2.6 copy-start
  7.2 1.6 copy-start.9
  7.2 1.6 copy-start.6
  7.2 1.8 copy-start.3
  7.2 232.5 %all-gather.4.cloned.1.call-start = ((), (), s32[]{:S(2)}) async-start(), calls=%async_computation.2 | async-start | bytes 49020928 | tf_op jit(solution)/shard_map/all_gather | solution.py:34
  7.9 460.7 %all-gather.6.cloned.1.call-start = ((), (), s32[]{:S(2)}) async-start(), calls=%async_computation.3 | async-start | bytes 49020928 | tf_op jit(solution)/shard_map/all_gather | solution.py:45
  8.7 558.7 %reduce-scatter.5.cloned.1.call-start = ((), (), s32[]{:S(2)}) async-start(), calls=%async_computation.5 | async-start | bytes 6291456 | tf_op jit(solution)/shard_map/reduce_scatter | solution.py:82
  9.8 4.0 copy-start.2
  9.8 4.7 copy-start.5
  512.9 88.6 %reduce-scatter.3.cloned.1.call-start = ((), (), s32[]{:S(2)}) async-start(), calls=%async_computation.4 | async-start | bytes 3145728 | tf_op jit(solution)/shard_map/reduce_scatter | solution.py:49
  535.2 100.8 %all-gather.8.cloned.1.call-start = ((), (), s32[]{:S(2)}) async-start(), calls=%async_computation.6 | async-start | bytes 3145728 | tf_op jit(solution)/shard_map/all_gather | solution.py:91
  535.3 4.1 copy-start.10
  571.4 161.9 %all-reduce.4.cloned.1.call-start = ((), (), s32[]{:S(2)}) async-start(), calls=%async_computation.7 | async-start | bytes 2097152 | tf_op jit(solution)/shard_map/psum | solution.py:73
  574.9 26.6 %copy-start.4 = (bf16[256,4096]{1,0:T(8,128)(2,1)S(1)}, bf16[256,4096]{1,0:T(8,128)(2,1)}, u32[]{:S(2)}) copy-start(bf16[256,4096]{1,0:T(8,128)(2,1)} %param.9) | copy-start | bytes 6291460
  733.3 3.3 copy-start.8
  733.3 4.0 copy-start.7
  733.3 4.8 copy-start.1
Sparse Core Ops, SparseCore 0:
  9.6 230.0 all-gather.3
  241.3 227.3 all-gather.5
  513.0 54.3 reduce-scatter.4
  569.6 31.8 reduce-scatter.2
  602.9 33.1 all-gather.7
  640.0 93.2 all-reduce.3
where the time goes:
time: 745 us
  waiting for transfers between devices  601 us (81%)
  matrix products  103 us (14%)
  between operations  14.2 us (2%)
  other arithmetic  13 us (2%)
  local copies, waits for them, and re-layouts  9.11 us (1%)
    all_gather x1, waiting for transfers between devices, on_device(): up_full = lax.all_gather(up_weight, 'dp', axis=0, tiled=True)  223 us
    all_gather x1, waiting for transfers between devices, on_device(): down_full = lax.all_gather(down_weight, 'dp', axis=0, tiled=True)  203 us
    psum x1, waiting for transfers between devices, on_device(): lax.psum((down_grad_part, up_grad_part), 'dp')  97.3 us
    all_gather x1, waiting for transfers between devices, on_device(): input_grad_second = lax.all_gather(second_share, 'mp', axis=1, tiled=True)  32 us
    dot_general x1, matrix products, on_device(): hidden_pre = jnp.dot(normed, up_full, preferred_element_type=jnp.float32)  25.5 us
    dot_general x1, matrix products, on_device(): act_grad = jnp.dot(carried, down_full, preferred_element_type=jnp.float32)  23.2 us
    dot_general x1, matrix products, on_device(): lax.dot_general(activated, down_full, (((1,), (1,)), ((), ())), preferred...  22.2 us
    reduce_scatter x1, waiting for transfers between devices, on_device(): lax.psum_scatter(normed_part, 'mp', scatter_dimension=1, tiled=True)  21.9 us
  transfers between devices with their start and end apart: 6, of which 6 were waited for; matrix products, arithmetic and copies ran while one was open for 10% of the time, Pallas kernels for 0%

commit v1 on v0

v1 whole, which is shorter than its diff:
```python
import math

import jax
import jax.numpy as jnp
from jax import lax
from jax.experimental import pallas as pl
from jax.experimental.pallas import tpu as pltpu
from jax.sharding import PartitionSpec as P

coupling = 0.5


def silu_slope(argument):
    sigmoid_value = jax.nn.sigmoid(argument)
    return sigmoid_value * (1.0 + argument * (1.0 - sigmoid_value))


def after(value, *earlier):
    return lax.optimization_barrier((value, *earlier))[0]


def hop(value, bits):
    size = lax.axis_size("dp")
    return lax.ppermute(value, "dp", [(i, i ^ bits) for i in range(size)])


def swap_mp(value):
    return lax.ppermute(value, "mp", [(0, 1), (1, 0)])


def relative_order(blocks):
    return [(r & ~3) | ((r & 1) << 1) | ((r >> 1) & 1) for r in range(blocks)]


def reorder_body(orders, width, me_ref, *refs):
    count = len(refs) // (1 + len(orders))
    me = me_ref[0]
    for at in range(count):
        source = refs[at]
        for which, (order, flip) in enumerate(orders):
            target = refs[count + at * len(orders) + which]
            for place, block in enumerate(order):
                start = pl.multiple_of((block ^ flip ^ me) * width, width)
                target[:, place * width : (place + 1) * width] = source[:, pl.ds(start, width)]


def reorder(me, arrays, flips, blocks, inverse=False):
    rows, columns = arrays[0].shape
    width = columns // blocks
    order = relative_order(blocks)
    orders = [(order, flip) for flip in flips]
    body = reorder_body
    if inverse:
        body = restore_body
    vmem = pl.BlockSpec(memory_space=pltpu.VMEM)
    return pl.pallas_call(
        lambda *refs: body(orders, width, *refs),
        out_shape=[
            jax.ShapeDtypeStruct(a.shape, a.dtype) for a in arrays for _ in flips
        ],
        in_specs=[pl.BlockSpec(memory_space=pltpu.SMEM)] + [vmem] * len(arrays),
        out_specs=[vmem] * (len(arrays) * len(flips)),
        compiler_params=pltpu.CompilerParams(vmem_limit_bytes=40 * 1024 * 1024),
    )(jnp.reshape(me, (1,)).astype(jnp.int32), *arrays)


def restore_body(orders, width, me_ref, *refs):
    count = len(refs) // 2
    me = me_ref[0]
    for at in range(count):
        for place, block in enumerate(orders[0][0]):
            start = pl.multiple_of((block ^ me) * width, width)
            refs[count + at][:, pl.ds(start, width)] = refs[at][
                :, place * width : (place + 1) * width
            ]


def dot(left, right):
    return jnp.dot(left, right, preferred_element_type=jnp.float32)


def dot_t(left, right):
    return lax.dot_general(
        left, right, (((1,), (1,)), ((), ())), preferred_element_type=jnp.float32
    )


def on_device(
    upper_first,
    upper_second,
    grad_first,
    grad_second,
    norm_gain,
    up_weight,
    down_weight,
    adapter_down,
    adapter_up,
):
    size = lax.axis_size("dp")
    groups = lax.axis_size("mp")
    me = lax.axis_index("dp")
    mp_rank = lax.axis_index("mp")
    tokens, model_width = upper_first.shape
    layers = size // 4
    chunk = model_width // layers
    share_width = model_width // groups
    offset = mp_rank * share_width
    grad_scale = 1.0 / math.sqrt(tokens * size)
    parity = (me >> 2) & 1
    quarter = up_weight.shape[1] // 2

    def halves(weight):
        mine = lax.dynamic_slice_in_dim(weight, parity * quarter, quarter, 1)
        other = lax.dynamic_slice_in_dim(weight, (1 - parity) * quarter, quarter, 1)
        return mine, other

    up_mine, up_other = halves(up_weight)
    down_mine, down_other = halves(down_weight)

    up_z = [up_mine] + [None] * (layers - 1)
    up_y = [None] * layers
    down_z = [down_mine] + [None] * (layers - 1)
    down_y = [None] * layers

    up_z[2] = hop(up_mine, 2 << 2)
    up_z[1] = hop(up_other, 1 << 2)
    up_y[0] = hop(up_mine, 2)
    for s in range(3, layers):
        gate = up_y[0] if s == 3 else up_z[s - 2]
        up_z[s] = hop(after(up_other if s & 1 else up_mine, gate), s << 2)
    for s in range(1, layers):
        up_y[s] = hop(up_z[s], 2)
    down_z[1] = hop(after(down_other, up_z[1], up_y[0]), 1 << 2)
    down_y[0] = hop(after(down_mine, up_y[1]), 2)
    for s in range(2, layers):
        gate = up_z[layers - 2 + (s & 1)] if s < 4 else down_z[s - 2]
        down_z[s] = hop(after(down_other if s & 1 else down_mine, gate), s << 2)
    for s in range(1, layers):
        down_y[s] = hop(down_z[s], 2)

    def whole_chunk(piece, piece_y):
        pair = jnp.concatenate([piece, piece_y], axis=0)
        return jnp.concatenate([pair, hop(pair, 1)], axis=0)

    pre_adapter = dot(upper_first, adapter_down)
    squashed = jax.nn.silu(pre_adapter).astype(jnp.bfloat16)
    adapted = dot(squashed, adapter_up)
    lower_full = (upper_second.astype(jnp.float32) - adapted).astype(jnp.bfloat16)
    lower_value = lower_full.astype(jnp.float32)
    inverse_rms = lax.rsqrt(jnp.mean(lower_value * lower_value, axis=1, keepdims=True) + 1e-05)
    gain_full = norm_gain.astype(jnp.float32)
    normed = (lower_value * inverse_rms * gain_full).astype(jnp.bfloat16)
    adapter_slope = dot_t(grad_second, adapter_up)
    adapter_pre_grad = (adapter_slope * silu_slope(pre_adapter)).astype(jnp.bfloat16)
    back_adapter = dot_t(adapter_pre_grad, adapter_down)
    carried = (grad_first.astype(jnp.float32) + back_adapter).astype(jnp.bfloat16)

    normed_own, normed_send, carried_own, carried_send = reorder(
        me, [normed, carried], [0, 4], size
    )

    def partner_tokens(send):
        part = hop(lax.dynamic_slice_in_dim(send, offset, share_width, 1), 4)
        if groups == 2:
            other = swap_mp(part)
            first = jnp.where(mp_rank == 0, part, other)
            second = jnp.where(mp_rank == 0, other, part)
            return jnp.concatenate([first, second], axis=1)
        return lax.all_gather(part, "mp", axis=1, tiled=True)

    normed_both = jnp.concatenate([normed_own, partner_tokens(normed_send)], axis=0)
    carried_both = jnp.concatenate([carried_own, partner_tokens(carried_send)], axis=0)

    hidden_pre = None
    up_chunks = []
    for s in range(layers):
        up_chunks.append(whole_chunk(up_z[s], up_y[s]))
        term = dot(normed_both[:, s * chunk : (s + 1) * chunk], up_chunks[s])
        hidden_pre = term if s == 0 else hidden_pre + term
    activated = jax.nn.silu(hidden_pre).astype(jnp.bfloat16)

    def summed_pair(parts):
        got = [hop(p[tokens:].astype(jnp.bfloat16), 4) for p in parts]
        return [parts[i][:tokens] + got[i ^ 1].astype(jnp.float32) for i in range(2)]

    act_grad = None
    out_parts = []
    out_sums = []
    for s in range(layers):
        down_chunk = whole_chunk(down_z[s], down_y[s])
        term = dot(carried_both[:, s * chunk : (s + 1) * chunk], down_chunk)
        act_grad = term if s == 0 else act_grad + term
        out_parts.append(dot_t(activated, down_chunk))
        if s & 1:
            out_sums += summed_pair(out_parts[s - 1 : s + 1])
    pre_grad = (act_grad * silu_slope(hidden_pre)).astype(jnp.bfloat16)
    stat_part = jnp.sum(hidden_pre * pre_grad.astype(jnp.float32), axis=1)
    stat_pair = stat_part[:tokens] + hop(stat_part[tokens:], 4)
    curvature = stat_pair + swap_mp(stat_pair) if groups == 2 else lax.psum(stat_pair, "mp")

    grad_sums = []
    for s in range(0, layers, 2):
        pair = summed_pair([dot_t(pre_grad, up_chunks[s]), dot_t(pre_grad, up_chunks[s + 1])])
        for part in pair:
            part = part.astype(jnp.bfloat16)
            if groups == 2:
                total = part.astype(jnp.float32) + swap_mp(part).astype(jnp.float32)
            else:
                total = lax.psum(part.astype(jnp.float32), "mp")
            grad_sums.append(total)

    (out_whole,) = reorder(
        me, [jnp.concatenate(out_sums, axis=1).astype(jnp.bfloat16)], [0], size, inverse=True
    )
    if groups == 2:
        out_keep = lax.dynamic_slice_in_dim(out_whole, offset, share_width, 1)
        out_give = lax.dynamic_slice_in_dim(out_whole, share_width - offset, share_width, 1)
        frozen_share = out_keep.astype(jnp.float32) + swap_mp(out_give).astype(jnp.float32)
    else:
        frozen_share = lax.psum_scatter(
            out_whole.astype(jnp.float32), "mp", scatter_dimension=1, tiled=True
        )
    upper_slice = lax.dynamic_slice_in_dim(upper_first, offset, share_width, 1)
    lower_first = ((upper_slice.astype(jnp.float32) - frozen_share) / coupling).astype(jnp.bfloat16)

    (normed_grad,) = reorder(
        me, [jnp.concatenate(grad_sums, axis=1)], [0], size, inverse=True
    )
    correction = lower_value * inverse_rms * inverse_rms * curvature[:, None] / model_width
    input_grad_second = (
        grad_second.astype(jnp.float32) + inverse_rms * gain_full * normed_grad - correction
    ).astype(jnp.bfloat16)

    lower_second = lax.dynamic_slice_in_dim(lower_full, offset, share_width, 1)
    carried_slice = lax.dynamic_slice_in_dim(carried, offset, share_width, 1)
    input_grad_first = (coupling * carried_slice.astype(jnp.float32)).astype(jnp.bfloat16)

    second_slice = lax.dynamic_slice_in_dim(grad_second, offset, share_width, 1)
    down_grad_part = (
        jnp.einsum("tr,td->rd", adapter_pre_grad, upper_slice, preferred_element_type=jnp.float32)
        * grad_scale
    )
    up_grad_part = (
        jnp.einsum("tr,td->rd", squashed, second_slice, preferred_element_type=jnp.float32)
        * grad_scale
    )
    rank = down_grad_part.shape[0]
    is_core, is_y = (me & 1) == 1, (me & 2) == 2
    keep = jnp.where(is_core, up_grad_part, down_grad_part)
    give = jnp.where(is_core, down_grad_part, up_grad_part)
    keep = keep + hop(give, 1)
    low, high = keep[: rank // 2], keep[rank // 2 :]
    share = jnp.where(is_y, high, low) + hop(jnp.where(is_y, low, high), 2)
    bit = 4
    while bit < size:
        share = share + hop(share, bit)
        bit *= 2
    other = hop(share, 2)
    half = jnp.concatenate(
        [jnp.where(is_y, other, share), jnp.where(is_y, share, other)], axis=0
    )
    other = hop(half, 1)
    adapter_down_grad = jnp.where(is_core, other, half).T
    adapter_up_grad = jnp.where(is_core, half, other)
    return (
        lower_first,
        lower_second,
        input_grad_first,
        input_grad_second,
        adapter_down_grad,
        adapter_up_grad,
    )


def solution(mesh):
    return jax.shard_map(
        on_device,
        mesh=mesh,
        in_specs=(
            P("dp", None),
            P("dp", None),
            P("dp", None),
            P("dp", None),
            P(),
            P("dp", "mp"),
            P("dp", "mp"),
            P(),
            P(),
        ),
        out_specs=(
            P("dp", "mp"),
            P("dp", "mp"),
            P("dp", "mp"),
            P("dp", None),
            P("mp", None),
            P(None, "mp"),
        ),
        check_vma=False,
    )
```

time: 745 us -> 646 us (0.87)
  waiting for transfers between devices: 601 us -> 369 us
  starting transfers between devices: 0.24 us -> 55.8 us
  other arithmetic: 13 us -> 52.1 us
  local copies, waits for them, and re-layouts: 9.11 us -> 45.2 us
  between operations: 14.2 us -> 2.02 us
  matrix products: 103 us -> 113 us
    all_gather x3 -> x0, waiting for transfers between devices: 459 us -> none  [the longest x1 223 us: on_device(): up_full = lax.all_gather(up_weight, 'dp', axis=0, tiled=True)]
    ppermute x0 -> x47, waiting for transfers between devices: none -> 369 us  [the longest x39 345 us: hop(): return lax.ppermute(value, 'dp', [(i, i ^ bits) for i in range(size)])]
    psum x1 -> x0, waiting for transfers between devices: 97.3 us -> none  [on_device(): lax.psum((down_grad_part, up_grad_part), 'dp')]
    ppermute x0 -> x47, starting transfers between devices: none -> 55.8 us  [the longest x39 48.9 us: hop(): return lax.ppermute(value, 'dp', [(i, i ^ bits) for i in range(size)])]
    reduce_scatter x2 -> x0, waiting for transfers between devices: 43.3 us -> none  [the longest x1 21.9 us: on_device(): lax.psum_scatter(normed_part, 'mp', scatter_dimension=1, tiled=True)]
    concatenate x0 -> x13, other arithmetic: none -> 38 us  [the longest x8 15.7 us: whole_chunk(): pair = jnp.concatenate([piece, piece_y], axis=0)]
    unnamed x27 -> x84, local copies, waits for them, and re-layouts: 6.36 us -> 23.3 us
    concatenate x0 -> x6, local copies, waits for them, and re-layouts: none -> 14.6 us  [whole_chunk(): return jnp.concatenate([pair, hop(pair, 1)], axis=0)]
  transfers between devices with their start and end apart: 6 -> 47, of which waited for: 6 -> 22; matrix products, arithmetic and copies ran while one was open for 10% -> 23% of each run, Pallas kernels for 0% -> 0%
where the time goes in v1:
time: 646 us; the launch traced here: 640 us
  waiting for transfers between devices  369 us (57%)
  matrix products  113 us (17%)
  starting transfers between devices  55.8 us (9%)
  other arithmetic  52.1 us (8%)
  local copies, waits for them, and re-layouts  45.2 us (7%)
    ppermute x39, waiting for transfers between devices, hop(): return lax.ppermute(value, 'dp', [(i, i ^ bits) for i in range(size)])  345 us
    dot_general x10, matrix products, dot(): return jnp.dot(left, right, preferred_element_type=jnp.float32)  67.2 us
    ppermute x39, starting transfers between devices, hop(): return lax.ppermute(value, 'dp', [(i, i ^ bits) for i in range(size)])  48.9 us
    dot_general x10, matrix products, dot_t(): lax.dot_general(left, right, (((1,), (1,)), ((), ())), preferred_element_...  43.4 us
    ppermute x8, waiting for transfers between devices, swap_mp(): return lax.ppermute(value, 'mp', [(0, 1), (1, 0)])  24.5 us
    unnamed x84, local copies, waits for them, and re-layouts  23.3 us
    concatenate x8, other arithmetic, whole_chunk(): pair = jnp.concatenate([piece, piece_y], axis=0)  15.7 us
    concatenate x6, local copies, waits for them, and re-layouts, whole_chunk(): return jnp.concatenate([pair, hop(pair, 1)], axis=0)  14.6 us
  transfers between devices with their start and end apart: 47, of which 22 were waited for; matrix products, arithmetic and copies ran while one was open for 23% of the time, Pallas kernels for 0%

profile of v1, /device:TPU:0, one launch (start us, length us, event | category | flops | bytes accessed | tf_op | source)
XLA Modules:
  0.0 639.8 jit_solution(7401666580616627624)
XLA Ops:
  0.7 2.6 fusion.49
  3.3 2.4 fusion.14
  5.9 2.5 broadcast_select_fusion.5
  8.9 2.7 fusion.9
  19.4 2.5 collective-permute-start
  27.3 5.4 collective-permute-done.42
  34.0 2.0 collective-permute-start.29
  36.0 2.6 collective-permute-start.7
  38.5 44.1 %collective-permute-done.43 = f32[32,2048]{1,0:T(8,128)S(1)} collective-permute-done((f32[32,2048]{1,0:T(8,128)S(1)}, f32[32,2048]{1,0:T(8,128)S(1)}, u32[]{:S(2)}, u32[]{:S(2)}) %collective-permute-start.43) | collective-permute-done | bytes 262176 | tf_op jit(solution)/shard_map/ppermute | solution.py:24
  84.4 4.7 collective-permute-start.44
  91.4 13.9 %collective-permute-done.29 = bf16[256,2048]{1,0:T(8,128)(2,1)} collective-permute-done((bf16[256,2048]{1,0:T(8,128)(2,1)}, bf16[256,2048]{1,0:T(8,128)(2,1)}, u32[]{:S(2)}, u32[]{:S(2)}) %collective-permute-start.29) | collective-permute-done | bytes 1048608 | tf_op jit(solution)/shard_map/ppermute | solution.py:24
  105.3 2.0 collective-permute-start.1
  107.3 33.3 %collective-permute-done.44 = f32[32,2048]{1,0:T(8,128)S(1)} collective-permute-done((f32[32,2048]{1,0:T(8,128)S(1)}, f32[32,2048]{1,0:T(8,128)S(1)}, u32[]{:S(2)}, u32[]{:S(2)}) %collective-permute-start.44) | collective-permute-done | bytes 262176 | tf_op jit(solution)/shard_map/ppermute | solution.py:24
  143.9 2.0 pad_maximum_fusion.3
  146.0 2.5 collective-permute-start.10
  148.5 2.5 constant_dynamic-update-slice_fusion.5
  151.1 2.7 constant_dynamic-update-slice_fusion.2
  153.8 2.5 collective-permute-start.20
  158.3 10.4 %maximum_maximum_fusion = bf16[512,4096]{1,0:T(8,128)(2,1)S(1)} fusion(bf16[256,2048]{1,0:T(8,128)(2,1)S(1)} %get-tuple-element.33, bf16[256,2048]{1,0:T(8,128)(2,1)S(1)} %get-tuple-element.32, bf16[256,4096]{1,0:T(8,128)(2,1)S(1)} %copy-done.5), kind=kLoop, calls=%fused_computation.21 | loop fusion | flops 12582912 | bytes 8388608 | tf_op jit(solution)/shard_map/concatenate | solution.py:171
  173.4 11.3 %maximum_maximum_fusion.1 = bf16[512,4096]{1,0:T(8,128)(2,1)} fusion(bf16[256,2048]{1,0:T(8,128)(2,1)S(1)} %get-tuple-element.31, bf16[256,2048]{1,0:T(8,128)(2,1)S(1)} %get-tuple-element.30, bf16[256,4096]{1,0:T(8,128)(2,1)S(1)} %copy-done.3), kind=kLoop, calls=%fused_computation.22 | loop fusion | flops 12582912 | bytes 8388608 | tf_op jit(solution)/shard_map/concatenate | solution.py:172
  184.7 6.4 collective-permute-done.8
  192.7 28.1 %collective-permute-done.5 = bf16[256,2816]{1,0:T(8,128)(2,1)S(1)} collective-permute-done((bf16[256,2816]{1,0:T(8,128)(2,1)}, bf16[256,2816]{1,0:T(8,128)(2,1)S(1)}, u32[]{:S(2)}, u32[]{:S(2)}) %collective-permute-start.5) | collective-permute-done | bytes 1441824 | tf_op jit(solution)/shard_map/ppermute | solution.py:24
  221.3 53.3 %collective-permute-done.20 = bf16[256,2816]{1,0:T(8,128)(2,1)S(1)} collective-permute-done((bf16[256,2816]{1,0:T(8,128)(2,1)S(1)}, bf16[256,2816]{1,0:T(8,128)(2,1)S(1)}, u32[]{:S(2)}, u32[]{:S(2)}) %collective-permute-start.20) | collective-permute-done | bytes 1441824 | tf_op jit(solution)/shard_map/ppermute | solution.py:24
  277.4 3.2 pad_maximum_fusion.4
  281.7 2.5 collective-permute-start.23
  289.0 20.1 %collective-permute-done.21 = bf16[256,2816]{1,0:T(8,128)(2,1)S(1)} collective-permute-done((bf16[256,2816]{1,0:T(8,128)(2,1)S(1)}, bf16[256,2816]{1,0:T(8,128)(2,1)S(1)}, u32[]{:S(2)}, u32[]{:S(2)}) %collective-permute-start.21) | collective-permute-done | bytes 1441824 | tf_op jit(solution)/shard_map/ppermute | solution.py:24
  310.9 6.3 collective-permute-done.23
  321.2 18.8 %collective-permute-done.16 = bf16[256,2816]{1,0:T(8,128)(2,1)S(1)} collective-permute-done((bf16[256,2816]{1,0:T(8,128)(2,1)S(1)}, bf16[256,2816]{1,0:T(8,128)(2,1)S(1)}, u32[]{:S(2)}, u32[]{:S(2)}) %collective-permute-start.16) | collective-permute-done | bytes 1441824 | tf_op jit(solution)/shard_map/ppermute | solution.py:24
  343.4 27.5 %collective-permute-done.13 = bf16[256,2816]{1,0:T(8,128)(2,1)S(1)} collective-permute-done((bf16[256,2816]{1,0:T(8,128)(2,1)S(1)}, bf16[256,2816]{1,0:T(8,128)(2,1)S(1)}, u32[]{:S(2)}, u32[]{:S(2)}) %collective-permute-start.13) | collective-permute-done | bytes 1441824 | tf_op jit(solution)/shard_map/ppermute | solution.py:24
  373.2 5.4 fusion.13
  378.6 22.3 %collective-permute-done.24 = bf16[256,2816]{1,0:T(8,128)(2,1)S(1)} collective-permute-done((bf16[256,2816]{1,0:T(8,128)(2,1)S(1)}, bf16[256,2816]{1,0:T(8,128)(2,1)S(1)}, u32[]{:S(2)}, u32[]{:S(2)}) %collective-permute-start.24) | collective-permute-done | bytes 1441824 | tf_op jit(solution)/shard_map/ppermute | solution.py:24
  404.9 3.6 constant_dynamic-update-slice_fusion
  408.5 7.5 %fusion.36 = f32[512,2816]{1,0:T(8,128)} fusion(bf16[1024,2816]{1,0:T(8,128)(2,1)} %constant_dynamic-update-slice_fusion.3, bf16[512,4096]{1,0:T(8,128)(2,1)S(1)} %maximum_maximum_fusion), kind=kOutput, calls=%fused_computation.76 | convolution fusion | flops 2952790016 | bytes 12582912 | tf_op jit(solution)/shard_map/dot_general | solution.py:79
  417.3 7.6 %fusion.38 = f32[512,2816]{1,0:T(8,128)} fusion(bf16[1024,2816]{1,0:T(8,128)(2,1)} %constant_dynamic-update-slice_fusion, bf16[512,4096]{1,0:T(8,128)(2,1)S(1)} %maximum_maximum_fusion), kind=kOutput, calls=%fused_computation.78 | convolution fusion | flops 2952790016 | bytes 12582912 | tf_op jit(solution)/shard_map/dot_general | solution.py:79
  425.1 3.5 constant_dynamic-update-slice_fusion.12
  431.9 7.9 %fusion.23 = f32[512,2816]{1,0:T(8,128)} fusion(bf16[1024,2816]{1,0:T(8,128)(2,1)} %constant_dynamic-update-slice_fusion.12, bf16[512,4096]{1,0:T(8,128)(2,1)S(1)} %copy-done.16), kind=kOutput, calls=%fused_computation.57 | convolution fusion | flops 2952790016 | bytes 12582912 | tf_op jit(solution)/shard_map/dot_general | solution.py:79
  439.8 7.5 %fusion.10 = f32[512,2816]{1,0:T(8,128)} fusion(bf16[512,2816]{1,0:T(8,128)(2,1)} %collective-permute-done.14, bf16[256,2816]{1,0:T(8,128)(2,1)S(1)} %copy-done.23, bf16[256,2816]{1,0:T(8,128)(2,1)S(1)} %copy-done.15, bf16[512,4096]{1,0:T(8,128)(2,1)S(1)} %copy-done.16), kind=kOutput, calls=%fused_computation.32 | convolution fusion | flops 2970091520 | bytes 12582912 | tf_op jit(solution)/shard_map/dot_general | solution.py:79
  447.3 5.1 fusion.25
  452.4 8.2 %add_add_fusion = f32[512,2816]{1,0:T(8,128)} fusion(f32[512,2816]{1,0:T(8,128)} %fusion.36, f32[512,2816]{1,0:T(8,128)S(1)} %fusion.13, f32[512,2816]{1,0:T(8,128)} %fusion.38, bf16[1024,2816]{1,0:T(8,128)(2,1)S(1)} %constant_dynamic-update-slice_fusion.6, bf16[512,4096]{1,0:T(8,128)(2,1)S(1)} %maximum_maximum_fusion), kind=kOutput, calls=%fused_computation.6 | convolution fusion | flops 2957115392 | bytes 29884416 | tf_op jit(solution)/shard_map/dot_general | solution.py:79
  460.6 3.7 constant_dynamic-update-slice_fusion.15
  465.1 12.6 %multiply_reduce_fusion = (f32[512]{0:T(512)S(1)}, bf16[512,2816]{1,0:T(8,128)(2,1)}, bf16[512,2816]{1,0:T(8,128)(2,1)}) fusion(f32[512,2816]{1,0:T(8,128)S(1)} %copy-done.14, bf16[1024,2816]{1,0:T(8,128)(2,1)} %constant_dynamic-update-slice_fusion.15, bf16[512,4096]{1,0:T(8,128)(2,1)} %maximum_maximum_fusion.1, f32[512,2816]{1,0:T(8,128)} %fusion.23, ...), kind=kOutput, calls=%fused_computation.2 | convolution fusion | flops 2977299968 | bytes 35653632 | tf_op jit(solution)/shard_map/dot_general | solution.py:79
  477.7 6.2 fusion.52
  483.9 5.2 fusion.51
  489.2 5.6 fusion.50
  494.8 3.2 fusion.55
  498.0 3.2 fusion.54
  501.2 5.4 fusion.53
  506.6 8.2 %collective-permute-start.27 = (bf16[256,1024]{1,0:T(8,128)(2,1)S(1)}, bf16[256,1024]{1,0:T(8,128)(2,1)S(1)}, u32[]{:S(2)}, u32[]{:S(2)}) collective-permute-start(bf16[256,1024]{1,0:T(8,128)(2,1)S(1)} %slice.207), channel_id=1, source_target_pairs={{0,8},{2,10},{4,12},{6,14},{8,0},{10,2},{12,4},{14,6},{16,24},{18,... | collective-permute-start | bytes 1572872 | tf_op jit(solution)/shard_map/ppermute | solution.py:24
  515.0 2.0 collective-permute-start.39
  517.0 4.9 fusion.11
  522.2 2.0 collective-permute-start.18
  524.2 14.7 %collective-permute-done.39 = f32[256]{0:T(256)S(1)} collective-permute-done((f32[256]{0:T(256)S(1)}, f32[256]{0:T(256)S(1)}, u32[]{:S(2)}, u32[]{:S(2)}) %collective-permute-start.39) | collective-permute-done | bytes 1056 | tf_op jit(solution)/shard_map/ppermute | solution.py:24
  539.5 6.6 %fusion.12 = f32[512,1024]{1,0:T(8,128)S(1)} fusion(bf16[512,2816]{1,0:T(8,128)(2,1)} %get-tuple-element.40, bf16[512,2816]{1,0:T(8,128)(2,1)} %collective-permute-done.3, bf16[256,2816]{1,0:T(8,128)(2,1)} %collective-permute-done.2, bf16[256,2816]{1,0:T(8,128)(2,1)} %get-tuple-element.29), kind=kOutput, calls=%fused_computation.34 | convolution fusion | flops 2970091520 | bytes 10747904 | tf_op jit(solution)/shard_map/dot_general | solution.py:83
  546.4 2.0 collective-permute-start.37
  548.7 2.0 collective-permute-start.33
  552.2 9.1 %collective-permute-done.18 = bf16[256,1024]{1,0:T(8,128)(2,1)S(1)} collective-permute-done((bf16[256,1024]{1,0:T(8,128)(2,1)S(1)}, bf16[256,1024]{1,0:T(8,128)(2,1)S(1)}, u32[]{:S(2)}, u32[]{:S(2)}) %collective-permute-start.18) | collective-permute-done | bytes 524320 | tf_op jit(solution)/shard_map/ppermute | solution.py:24
  562.7 9.9 %collective-permute-done.37 = bf16[256,1024]{1,0:T(8,128)(2,1)S(1)} collective-permute-done((bf16[256,1024]{1,0:T(8,128)(2,1)S(1)}, bf16[256,1024]{1,0:T(8,128)(2,1)S(1)}, u32[]{:S(2)}, u32[]{:S(2)}) %collective-permute-start.37) | collective-permute-done | bytes 524320 | tf_op jit(solution)/shard_map/ppermute | solution.py:24
  573.3 10.5 %collective-permute-done.35 = bf16[256,1024]{1,0:T(8,128)(2,1)S(1)} collective-permute-done((bf16[256,1024]{1,0:T(8,128)(2,1)S(1)}, bf16[256,1024]{1,0:T(8,128)(2,1)S(1)}, u32[]{:S(2)}, u32[]{:S(2)}) %collective-permute-start.35) | collective-permute-done | bytes 524320 | tf_op jit(solution)/shard_map/ppermute | solution.py:24
  584.6 10.5 %collective-permute-done.33 = bf16[256,1024]{1,0:T(8,128)(2,1)S(1)} collective-permute-done((bf16[256,1024]{1,0:T(8,128)(2,1)S(1)}, bf16[256,1024]{1,0:T(8,128)(2,1)S(1)}, u32[]{:S(2)}, u32[]{:S(2)}) %collective-permute-start.33) | collective-permute-done | bytes 524320 | tf_op jit(solution)/shard_map/ppermute | solution.py:24
  595.8 10.3 %collective-permute-done.31 = bf16[256,1024]{1,0:T(8,128)(2,1)S(1)} collective-permute-done((bf16[256,1024]{1,0:T(8,128)(2,1)S(1)}, bf16[256,1024]{1,0:T(8,128)(2,1)S(1)}, u32[]{:S(2)}, u32[]{:S(2)}) %collective-permute-start.31) | collective-permute-done | bytes 524320 | tf_op jit(solution)/shard_map/ppermute | solution.py:24
  607.1 3.6 collective-permute-done.36
  610.9 11.1 %collective-permute-done.34 = bf16[256,1024]{1,0:T(8,128)(2,1)S(1)} collective-permute-done((bf16[256,1024]{1,0:T(8,128)(2,1)S(1)}, bf16[256,1024]{1,0:T(8,128)(2,1)S(1)}, u32[]{:S(2)}, u32[]{:S(2)}) %collective-permute-start.34) | collective-permute-done | bytes 524320 | tf_op jit(solution)/shard_map/ppermute | solution.py:28
  622.1 9.8 %collective-permute-done.32 = bf16[256,1024]{1,0:T(8,128)(2,1)S(1)} collective-permute-done((bf16[256,1024]{1,0:T(8,128)(2,1)S(1)}, bf16[256,1024]{1,0:T(8,128)(2,1)S(1)}, u32[]{:S(2)}, u32[]{:S(2)}) %collective-permute-start.32) | collective-permute-done | bytes 524320 | tf_op jit(solution)/shard_map/ppermute | solution.py:28
  634.8 3.0 fusion.8
  (204 shorter events, 73.0 us)
Async XLA Ops:
  0.6 5.0 copy-start.11
  5.9 5.7 copy-start.28
  8.5 13.5 %collective-permute-start.41 = (f32[64,2048]{1,0:T(8,128)}, f32[64,2048]{1,0:T(8,128)}, u32[]{:S(2)}, u32[]{:S(2)}) collective-permute-start(f32[64,2048]{1,0:T(8,128)} %get-tuple-element.41), channel_id=1, source_target_pairs={{0,2},{2,0},{4,6},{6,4},{8,10},{10,8},{12,14},{14,12},{16,18},{18,... | collective-permute-start | bytes 1572872 | tf_op jit(solution)/shard_map/ppermute | solution.py:24
  19.4 65.0 %collective-permute-start = (bf16[256,2048]{1,0:T(8,128)(2,1)}, bf16[256,2048]{1,0:T(8,128)(2,1)}, u32[]{:S(2)}, u32[]{:S(2)}) collective-permute-start(bf16[256,2048]{1,0:T(8,128)(2,1)} %constant_dynamic-slice_fusion.7), channel_id=1, source_target_pairs={{0,8},{2,10},{4,12},{6,14},{8,0},{10,2},{12,4},{14,6},{16,24},{18,... | collective-permute-start | bytes 3145736 | tf_op jit(solution)/shard_map/ppermute | solution.py:24
  23.4 9.5 %copy-start.7 = (bf16[256,4096]{1,0:T(8,128)(2,1)S(1)}, bf16[256,4096]{1,0:T(8,128)(2,1)}, u32[]{:S(2)}) copy-start(bf16[256,4096]{1,0:T(8,128)(2,1)} %copy-done.6) | copy-start | bytes 6291460
  23.5 59.2 %copy-start.18 = (bf16[256,5632]{1,0:T(8,128)(2,1)S(1)}, bf16[256,5632]{1,0:T(8,128)(2,1)}, u32[]{:S(2)}) copy-start(bf16[256,5632]{1,0:T(8,128)(2,1)} %param.15) | copy-start | bytes 8650756
  23.5 9.3 %collective-permute-start.42 = (f32[32,2048]{1,0:T(8,128)S(1)}, f32[32,2048]{1,0:T(8,128)S(1)}, u32[]{:S(2)}, u32[]{:S(2)}) collective-permute-start(f32[32,2048]{1,0:T(8,128)S(1)} %slice_select_fusion), channel_id=1, source_target_pairs={{0,4},{2,6},{4,0},{6,2},{8,12},{10,14},{12,8},{14,10},{16,20},{18,... | collective-permute-start | bytes 786440 | tf_op jit(solution)/shard_map/ppermute | solution.py:24
  26.7 115.4 %collective-permute-start.2 = (bf16[256,2816]{1,0:T(8,128)(2,1)}, bf16[256,2816]{1,0:T(8,128)(2,1)}, u32[]{:S(2)}, u32[]{:S(2)}) collective-permute-start(bf16[256,2816]{1,0:T(8,128)(2,1)} %get-tuple-element.29), channel_id=1, source_target_pairs={{0,4},{2,6},{4,0},{6,2},{8,12},{10,14},{12,8},{14,10},{16,20},{18,... | collective-permute-start | bytes 4325384 | tf_op jit(solution)/shard_map/ppermute | solution.py:24
  32.8 49.8 %collective-permute-start.43 = (f32[32,2048]{1,0:T(8,128)S(1)}, f32[32,2048]{1,0:T(8,128)S(1)}, u32[]{:S(2)}, u32[]{:S(2)}) collective-permute-start(f32[32,2048]{1,0:T(8,128)S(1)} %select_add_fusion.1), channel_id=1, source_target_pairs={{0,8},{2,10},{4,12},{6,14},{8,0},{10,2},{12,4},{14,6},{16,24},{18,... | collective-permute-start | bytes 786440 | tf_op jit(solution)/shard_map/ppermute | solution.py:24
  32.9 56.2 %copy-start.9 = (bf16[256,4096]{1,0:T(8,128)(2,1)S(1)}, bf16[256,4096]{1,0:T(8,128)(2,1)}, u32[]{:S(2)}) copy-start(bf16[256,4096]{1,0:T(8,128)(2,1)} %copy-done.8) | copy-start | bytes 6291460
  34.0 71.3 %collective-permute-start.29 = (bf16[256,2048]{1,0:T(8,128)(2,1)}, bf16[256,2048]{1,0:T(8,128)(2,1)}, u32[]{:S(2)}, u32[]{:S(2)}) collective-permute-start(bf16[256,2048]{1,0:T(8,128)(2,1)} %constant_dynamic-slice_fusion), channel_id=1, source_target_pairs={{0,8},{2,10},{4,12},{6,14},{8,0},{10,2},{12,4},{14,6},{16,24},{18,... | collective-permute-start | bytes 3145736 | tf_op jit(solution)/shard_map/ppermute | solution.py:24
  36.0 109.9 %collective-permute-start.7 = (bf16[256,2816]{1,0:T(8,128)(2,1)}, bf16[256,2816]{1,0:T(8,128)(2,1)}, u32[]{:S(2)}, u32[]{:S(2)}) collective-permute-start(bf16[256,2816]{1,0:T(8,128)(2,1)} %get-tuple-element.29), channel_id=1, source_target_pairs={{0,16},{2,18},{4,20},{6,22},{8,24},{10,26},{12,28},{14,30},{16,0},... | collective-permute-start | bytes 4325384 | tf_op jit(solution)/shard_map/ppermute | solution.py:24
  82.6 63.4 %collective-permute-start.4 = (bf16[256,2816]{1,0:T(8,128)(2,1)}, bf16[256,2816]{1,0:T(8,128)(2,1)}, u32[]{:S(2)}, u32[]{:S(2)}) collective-permute-start(bf16[256,2816]{1,0:T(8,128)(2,1)} %get-tuple-element.17), channel_id=1, source_target_pairs={{0,8},{2,10},{4,12},{6,14},{8,0},{10,2},{12,4},{14,6},{16,24},{18,... | collective-permute-start | bytes 4325384 | tf_op jit(solution)/shard_map/ppermute | solution.py:24
  84.4 56.2 %collective-permute-start.44 = (f32[32,2048]{1,0:T(8,128)S(1)}, f32[32,2048]{1,0:T(8,128)S(1)}, u32[]{:S(2)}, u32[]{:S(2)}) collective-permute-start(f32[32,2048]{1,0:T(8,128)S(1)} %add.164), channel_id=1, source_target_pairs={{0,16},{2,18},{4,20},{6,22},{8,24},{10,26},{12,28},{14,30},{16,0},... | collective-permute-start | bytes 786440 | tf_op jit(solution)/shard_map/ppermute | solution.py:24
  105.3 51.0 %collective-permute-start.1 = (bf16[256,2048]{1,0:T(8,128)(2,1)}, bf16[256,2048]{1,0:T(8,128)(2,1)S(1)}, u32[]{:S(2)}, u32[]{:S(2)}) collective-permute-start(bf16[256,2048]{1,0:T(8,128)(2,1)} %collective-permute-done), channel_id=1, source_target_pairs={{0,1},{1,0},{2,3},{3,2},{4,5},{5,4},{6,7},{7,6},{8,9},{9,8},{10,11... | collective-permute-start | bytes 3145736 | tf_op jit(solution)/shard_map/ppermute | solution.py:28
  140.6 28.1 %collective-permute-start.30 = (bf16[256,2048]{1,0:T(8,128)(2,1)}, bf16[256,2048]{1,0:T(8,128)(2,1)S(1)}, u32[]{:S(2)}, u32[]{:S(2)}) collective-permute-start(bf16[256,2048]{1,0:T(8,128)(2,1)} %collective-permute-done.29), channel_id=1, source_target_pairs={{0,1},{1,0},{2,3},{3,2},{4,5},{5,4},{6,7},{7,6},{8,9},{9,8},{10,11... | collective-permute-start | bytes 3145736 | tf_op jit(solution)/shard_map/ppermute | solution.py:28
  142.1 11.6 %collective-permute-start.45 = (f32[32,2048]{1,0:T(8,128)S(1)}, f32[32,2048]{1,0:T(8,128)S(1)}, u32[]{:S(2)}, u32[]{:S(2)}) collective-permute-start(f32[32,2048]{1,0:T(8,128)S(1)} %add.165), channel_id=1, source_target_pairs={{0,4},{2,6},{4,0},{6,2},{8,12},{10,14},{12,8},{14,10},{16,20},{18,... | collective-permute-start | bytes 786440 | tf_op jit(solution)/shard_map/ppermute | solution.py:24
  145.9 7.9 %copy-start.15 = (bf16[256,2816]{1,0:T(8,128)(2,1)S(1)}, bf16[256,2816]{1,0:T(8,128)(2,1)}, u32[]{:S(2)}) copy-start(bf16[256,2816]{1,0:T(8,128)(2,1)} %get-tuple-element.18) | copy-start | bytes 4325380
  145.9 227.0 %collective-permute-start.3 = (bf16[512,2816]{1,0:T(8,128)(2,1)S(1)}, bf16[512,2816]{1,0:T(8,128)(2,1)}, u32[]{:S(2)}, u32[]{:S(2)}) collective-permute-start(bf16[512,2816]{1,0:T(8,128)(2,1)S(1)} %pad_maximum_fusion.3), channel_id=1, source_target_pairs={{0,2},{2,0},{4,6},{6,4},{8,10},{10,8},{12,14},{14,12},{16,18},{18,... | collective-permute-start | bytes 8650760 | tf_op jit(solution)/shard_map/ppermute | solution.py:24
  146.0 46.7 %collective-permute-start.10 = (bf16[256,2816]{1,0:T(8,128)(2,1)}, bf16[256,2816]{1,0:T(8,128)(2,1)S(1)}, u32[]{:S(2)}, u32[]{:S(2)}) collective-permute-start(bf16[256,2816]{1,0:T(8,128)(2,1)} %get-tuple-element.17), channel_id=1, source_target_pairs={{0,24},{2,26},{4,28},{6,30},{8,16},{10,18},{12,20},{14,22},{16,8},... | collective-permute-start | bytes 4325384 | tf_op jit(solution)/shard_map/ppermute | solution.py:24
  151.1 7.2 %copy-start.5 = (bf16[256,4096]{1,0:T(8,128)(2,1)S(1)}, bf16[256,4096]{1,0:T(8,128)(2,1)}, u32[]{:S(2)}) copy-start(bf16[256,4096]{1,0:T(8,128)(2,1)} %copy-done.4) | copy-start | bytes 6291460
  153.8 120.9 %collective-permute-start.20 = (bf16[256,2816]{1,0:T(8,128)(2,1)S(1)}, bf16[256,2816]{1,0:T(8,128)(2,1)S(1)}, u32[]{:S(2)}, u32[]{:S(2)}) collective-permute-start(bf16[256,2816]{1,0:T(8,128)(2,1)S(1)} %copy-done.15), channel_id=1, source_target_pairs={{0,16},{2,18},{4,20},{6,22},{8,24},{10,26},{12,28},{14,30},{16,0},... | collective-permute-start | bytes 4325384 | tf_op jit(solution)/shard_map/ppermute | solution.py:24
  156.3 34.7 %collective-permute-start.8 = (bf16[256,2816]{1,0:T(8,128)(2,1)}, bf16[256,2816]{1,0:T(8,128)(2,1)S(1)}, u32[]{:S(2)}, u32[]{:S(2)}) collective-permute-start(bf16[256,2816]{1,0:T(8,128)(2,1)} %collective-permute-done.7), channel_id=1, source_target_pairs={{0,4},{2,6},{4,0},{6,2},{8,12},{10,14},{12,8},{14,10},{16,20},{18,... | collective-permute-start | bytes 4325384 | tf_op jit(solution)/shard_map/ppermute | solution.py:24
  168.7 4.8 copy-start.3
  168.7 2.0 collective-permute-start.46
  170.7 50.2 %collective-permute-start.5 = (bf16[256,2816]{1,0:T(8,128)(2,1)}, bf16[256,2816]{1,0:T(8,128)(2,1)S(1)}, u32[]{:S(2)}, u32[]{:S(2)}) collective-permute-start(bf16[256,2816]{1,0:T(8,128)(2,1)} %collective-permute-done.4), channel_id=1, source_target_pairs={{0,4},{2,6},{4,0},{6,2},{8,12},{10,14},{12,8},{14,10},{16,20},{18,... | collective-permute-start | bytes 4325384 | tf_op jit(solution)/shard_map/ppermute | solution.py:24
  191.1 90.7 %collective-permute-start.15 = (bf16[256,2816]{1,0:T(8,128)(2,1)}, bf16[256,2816]{1,0:T(8,128)(2,1)S(1)}, u32[]{:S(2)}, u32[]{:S(2)}) collective-permute-start(bf16[256,2816]{1,0:T(8,128)(2,1)} %get-tuple-element.19), channel_id=1, source_target_pairs={{0,8},{2,10},{4,12},{6,14},{8,0},{10,2},{12,4},{14,6},{16,24},{18,... | collective-permute-start | bytes 4325384 | tf_op jit(solution)/shard_map/ppermute | solution.py:24
  192.7 210.0 %collective-permute-start.9 = (bf16[512,2816]{1,0:T(8,128)(2,1)S(1)}, bf16[512,2816]{1,0:T(8,128)(2,1)S(1)}, u32[]{:S(2)}, u32[]{:S(2)}) collective-permute-start(bf16[512,2816]{1,0:T(8,128)(2,1)S(1)} %pad_maximum_fusion.5), channel_id=1, source_target_pairs={{0,2},{2,0},{4,6},{6,4},{8,10},{10,8},{12,14},{14,12},{16,18},{18,... | collective-permute-start | bytes 8650760 | tf_op jit(solution)/shard_map/ppermute | solution.py:24
  220.9 64.6 %collective-permute-start.11 = (bf16[256,2816]{1,0:T(8,128)(2,1)S(1)}, bf16[256,2816]{1,0:T(8,128)(2,1)S(1)}, u32[]{:S(2)}, u32[]{:S(2)}) collective-permute-start(bf16[256,2816]{1,0:T(8,128)(2,1)S(1)} %collective-permute-done.10), channel_id=1, source_target_pairs={{0,4},{2,6},{4,0},{6,2},{8,12},{10,14},{12,8},{14,10},{16,20},{18,... | collective-permute-start | bytes 4325384 | tf_op jit(solution)/shard_map/ppermute | solution.py:24
  274.7 34.4 %collective-permute-start.21 = (bf16[256,2816]{1,0:T(8,128)(2,1)S(1)}, bf16[256,2816]{1,0:T(8,128)(2,1)S(1)}, u32[]{:S(2)}, u32[]{:S(2)}) collective-permute-start(bf16[256,2816]{1,0:T(8,128)(2,1)S(1)} %collective-permute-done.20), channel_id=1, source_target_pairs={{0,4},{2,6},{4,0},{6,2},{8,12},{10,14},{12,8},{14,10},{16,20},{18,... | collective-permute-start | bytes 4325384 | tf_op jit(solution)/shard_map/ppermute | solution.py:24
  281.7 35.4 %collective-permute-start.23 = (bf16[256,2816]{1,0:T(8,128)(2,1)}, bf16[256,2816]{1,0:T(8,128)(2,1)S(1)}, u32[]{:S(2)}, u32[]{:S(2)}) collective-permute-start(bf16[256,2816]{1,0:T(8,128)(2,1)} %get-tuple-element.19), channel_id=1, source_target_pairs={{0,24},{2,26},{4,28},{6,30},{8,16},{10,18},{12,20},{14,22},{16,8},... | collective-permute-start | bytes 4325384 | tf_op jit(solution)/shard_map/ppermute | solution.py:24
  285.5 54.5 %collective-permute-start.16 = (bf16[256,2816]{1,0:T(8,128)(2,1)S(1)}, bf16[256,2816]{1,0:T(8,128)(2,1)S(1)}, u32[]{:S(2)}, u32[]{:S(2)}) collective-permute-start(bf16[256,2816]{1,0:T(8,128)(2,1)S(1)} %collective-permute-done.15), channel_id=1, source_target_pairs={{0,4},{2,6},{4,0},{6,2},{8,12},{10,14},{12,8},{14,10},{16,20},{18,... | collective-permute-start | bytes 4325384 | tf_op jit(solution)/shard_map/ppermute | solution.py:24
  309.1 95.8 %collective-permute-start.6 = (bf16[512,2816]{1,0:T(8,128)(2,1)}, bf16[512,2816]{1,0:T(8,128)(2,1)}, u32[]{:S(2)}, u32[]{:S(2)}) collective-permute-start(bf16[512,2816]{1,0:T(8,128)(2,1)} %pad_maximum_fusion.4), channel_id=1, source_target_pairs={{0,2},{2,0},{4,6},{6,4},{8,10},{10,8},{12,14},{14,12},{16,18},{18,... | collective-permute-start | bytes 8650760 | tf_op jit(solution)/shard_map/ppermute | solution.py:24
  317.1 53.8 %collective-permute-start.13 = (bf16[256,2816]{1,0:T(8,128)(2,1)S(1)}, bf16[256,2816]{1,0:T(8,128)(2,1)S(1)}, u32[]{:S(2)}, u32[]{:S(2)}) collective-permute-start(bf16[256,2816]{1,0:T(8,128)(2,1)S(1)} %copy-done.15), channel_id=1, source_target_pairs={{0,4},{2,6},{4,0},{6,2},{8,12},{10,14},{12,8},{14,10},{16,20},{18,... | collective-permute-start | bytes 4325384 | tf_op jit(solution)/shard_map/ppermute | solution.py:24
  340.0 60.9 %collective-permute-start.24 = (bf16[256,2816]{1,0:T(8,128)(2,1)S(1)}, bf16[256,2816]{1,0:T(8,128)(2,1)S(1)}, u32[]{:S(2)}, u32[]{:S(2)}) collective-permute-start(bf16[256,2816]{1,0:T(8,128)(2,1)S(1)} %collective-permute-done.23), channel_id=1, source_target_pairs={{0,4},{2,6},{4,0},{6,2},{8,12},{10,14},{12,8},{14,10},{16,20},{18,... | collective-permute-start | bytes 4325384 | tf_op jit(solution)/shard_map/ppermute | solution.py:24
  370.9 54.0 %collective-permute-start.12 = (bf16[512,2816]{1,0:T(8,128)(2,1)}, bf16[512,2816]{1,0:T(8,128)(2,1)S(1)}, u32[]{:S(2)}, u32[]{:S(2)}) collective-permute-start(bf16[512,2816]{1,0:T(8,128)(2,1)} %pad_maximum_fusion.6), channel_id=1, source_target_pairs={{0,2},{2,0},{4,6},{6,4},{8,10},{10,8},{12,14},{14,12},{16,18},{18,... | collective-permute-start | bytes 8650760 | tf_op jit(solution)/shard_map/ppermute | solution.py:24
  373.0 52.1 %collective-permute-start.22 = (bf16[512,2816]{1,0:T(8,128)(2,1)}, bf16[512,2816]{1,0:T(8,128)(2,1)}, u32[]{:S(2)}, u32[]{:S(2)}) collective-permute-start(bf16[512,2816]{1,0:T(8,128)(2,1)} %pad_maximum_fusion.9), channel_id=1, source_target_pairs={{0,2},{2,0},{4,6},{6,4},{8,10},{10,8},{12,14},{14,12},{16,18},{18,... | collective-permute-start | bytes 8650760 | tf_op jit(solution)/shard_map/ppermute | solution.py:24
  378.6 24.1 %copy-start.19 = (bf16[512,2816]{1,0:T(8,128)(2,1)S(1)}, bf16[512,2816]{1,0:T(8,128)(2,1)}, u32[]{:S(2)}) copy-start(bf16[512,2816]{1,0:T(8,128)(2,1)} %pad_maximum_fusion.8) | copy-start | bytes 8650756
  400.9 38.9 %collective-permute-start.14 = (bf16[512,2816]{1,0:T(8,128)(2,1)}, bf16[512,2816]{1,0:T(8,128)(2,1)}, u32[]{:S(2)}, u32[]{:S(2)}) collective-permute-start(bf16[512,2816]{1,0:T(8,128)(2,1)} %pad_maximum_fusion.7), channel_id=1, source_target_pairs={{0,2},{2,0},{4,6},{6,4},{8,10},{10,8},{12,14},{14,12},{16,18},{18,... | collective-permute-start | bytes 8650760 | tf_op jit(solution)/shard_map/ppermute | solution.py:24
  402.7 25.9 %collective-permute-start.17 = (bf16[512,2816]{1,0:T(8,128)(2,1)S(1)}, bf16[512,2816]{1,0:T(8,128)(2,1)S(1)}, u32[]{:S(2)}, u32[]{:S(2)}) collective-permute-start(bf16[512,2816]{1,0:T(8,128)(2,1)S(1)} %copy-done.19), channel_id=1, source_target_pairs={{0,2},{2,0},{4,6},{6,4},{8,10},{10,8},{12,14},{14,12},{16,18},{18,... | collective-permute-start | bytes 8650760 | tf_op jit(solution)/shard_map/ppermute | solution.py:24
  404.9 55.7 %collective-permute-start.25 = (bf16[512,2816]{1,0:T(8,128)(2,1)}, bf16[512,2816]{1,0:T(8,128)(2,1)}, u32[]{:S(2)}, u32[]{:S(2)}) collective-permute-start(bf16[512,2816]{1,0:T(8,128)(2,1)} %pad_maximum_fusion.10), channel_id=1, source_target_pairs={{0,2},{2,0},{4,6},{6,4},{8,10},{10,8},{12,14},{14,12},{16,18},{18,... | collective-permute-start | bytes 8650760 | tf_op jit(solution)/shard_map/ppermute | solution.py:24
  431.9 8.0 %copy-start.23 = (bf16[256,2816]{1,0:T(8,128)(2,1)S(1)}, bf16[256,2816]{1,0:T(8,128)(2,1)}, u32[]{:S(2)}) copy-start(bf16[256,2816]{1,0:T(8,128)(2,1)} %copy-done.22) | copy-start | bytes 4325380
  431.9 15.5 %slice-start.2 = ((s8[5767168]{0:T(1024)(128)(4,1)}), s8[4194304]{0:T(1024)(128)(4,1)S(1)}, s32[]{:S(2)}) async-start(s8[5767168]{0:T(1024)(128)(4,1)} %bitcast.33), calls=%async_computation.2 | async-start | bytes 8388608
  439.8 7.5 %slice-start.3 = ((s8[5767168]{0:T(1024)(128)(4,1)}), s8[1572864]{0:T(1024)(128)(4,1)S(1)}, s32[]{:S(2)}) async-start(s8[5767168]{0:T(1024)(128)(4,1)} %bitcast.33), calls=%async_computation.3 | async-start | bytes 3145728
  477.7 6.3 copy-start.30
  489.1 5.7 copy-start.29
  489.2 8.8 %slice-start = ((s8[5767168]{0:T(1024)(128)(4,1)}), s8[4194304]{0:T(1024)(128)(4,1)S(1)}, s32[]{:S(2)}) async-start(s8[5767168]{0:T(1024)(128)(4,1)} %bitcast.31), calls=%async_computation | async-start | bytes 8388608
  501.2 15.8 %copy-start.31 = (bf16[512,2816]{1,0:T(8,128)(2,1)S(1)}, bf16[512,2816]{1,0:T(8,128)(2,1)}, u32[]{:S(2)}) copy-start(bf16[512,2816]{1,0:T(8,128)(2,1)} %get-tuple-element.25) | copy-start | bytes 8650756
  506.6 41.8 %collective-permute-start.27 = (bf16[256,1024]{1,0:T(8,128)(2,1)S(1)}, bf16[256,1024]{1,0:T(8,128)(2,1)S(1)}, u32[]{:S(2)}, u32[]{:S(2)}) collective-permute-start(bf16[256,1024]{1,0:T(8,128)(2,1)S(1)} %slice.207), channel_id=1, source_target_pairs={{0,8},{2,10},{4,12},{6,14},{8,0},{10,2},{12,4},{14,6},{16,24},{18,... | collective-permute-start | bytes 1572872 | tf_op jit(solution)/shard_map/ppermute | solution.py:24
  514.9 33.8 %collective-permute-start.26 = (bf16[256,1024]{1,0:T(8,128)(2,1)S(1)}, bf16[256,1024]{1,0:T(8,128)(2,1)S(1)}, u32[]{:S(2)}, u32[]{:S(2)}) collective-permute-start(bf16[256,1024]{1,0:T(8,128)(2,1)S(1)} %slice.208), channel_id=1, source_target_pairs={{0,8},{2,10},{4,12},{6,14},{8,0},{10,2},{12,4},{14,6},{16,24},{18,... | collective-permute-start | bytes 1572872 | tf_op jit(solution)/shard_map/ppermute | solution.py:24
  515.0 23.9 %collective-permute-start.39 = (f32[256]{0:T(256)S(1)}, f32[256]{0:T(256)S(1)}, u32[]{:S(2)}, u32[]{:S(2)}) collective-permute-start(f32[256]{0:T(256)S(1)} %slice.117), channel_id=1, source_target_pairs={{0,8},{2,10},{4,12},{6,14},{8,0},{10,2},{12,4},{14,6},{16,24},{18,... | collective-permute-start | bytes 3080 | tf_op jit(solution)/shard_map/ppermute | solution.py:24
  522.0 28.9 %collective-permute-start.19 = (bf16[256,1024]{1,0:T(8,128)(2,1)S(1)}, bf16[256,1024]{1,0:T(8,128)(2,1)S(1)}, u32[]{:S(2)}, u32[]{:S(2)}) collective-permute-start(bf16[256,1024]{1,0:T(8,128)(2,1)S(1)} %slice.209), channel_id=1, source_target_pairs={{0,8},{2,10},{4,12},{6,14},{8,0},{10,2},{12,4},{14,6},{16,24},{18,... | collective-permute-start | bytes 1572872 | tf_op jit(solution)/shard_map/ppermute | solution.py:24
  522.2 39.2 %collective-permute-start.18 = (bf16[256,1024]{1,0:T(8,128)(2,1)S(1)}, bf16[256,1024]{1,0:T(8,128)(2,1)S(1)}, u32[]{:S(2)}, u32[]{:S(2)}) collective-permute-start(bf16[256,1024]{1,0:T(8,128)(2,1)S(1)} %slice.210), channel_id=1, source_target_pairs={{0,8},{2,10},{4,12},{6,14},{8,0},{10,2},{12,4},{14,6},{16,24},{18,... | collective-permute-start | bytes 1572872 | tf_op jit(solution)/shard_map/ppermute | solution.py:24
  538.9 7.5 %collective-permute-start.40 = (f32[256]{0:T(256)S(1)}, f32[256]{0:T(256)S(1)}, u32[]{:S(2)}, u32[]{:S(2)}) collective-permute-start(f32[256]{0:T(256)S(1)} %slice_add_fusion.8), channel_id=1, source_target_pairs={{0,1},{1,0},{2,3},{3,2},{4,5},{5,4},{6,7},{7,6},{8,9},{9,8},{10,11... | collective-permute-start | bytes 3080 | tf_op jit(solution)/shard_map/ppermute | solution.py:28
  546.4 26.2 %collective-permute-start.37 = (bf16[256,1024]{1,0:T(8,128)(2,1)S(1)}, bf16[256,1024]{1,0:T(8,128)(2,1)S(1)}, u32[]{:S(2)}, u32[]{:S(2)}) collective-permute-start(bf16[256,1024]{1,0:T(8,128)(2,1)S(1)} %slice.203), channel_id=1, source_target_pairs={{0,8},{2,10},{4,12},{6,14},{8,0},{10,2},{12,4},{14,6},{16,24},{18,... | collective-permute-start | bytes 1572872 | tf_op jit(solution)/shard_map/ppermute | solution.py:24
  548.4 35.4 %collective-permute-start.35 = (bf16[256,1024]{1,0:T(8,128)(2,1)S(1)}, bf16[256,1024]{1,0:T(8,128)(2,1)S(1)}, u32[]{:S(2)}, u32[]{:S(2)}) collective-permute-start(bf16[256,1024]{1,0:T(8,128)(2,1)S(1)} %slice.204), channel_id=1, source_target_pairs={{0,8},{2,10},{4,12},{6,14},{8,0},{10,2},{12,4},{14,6},{16,24},{18,... | collective-permute-start | bytes 1572872 | tf_op jit(solution)/shard_map/ppermute | solution.py:24
  548.7 46.4 %collective-permute-start.33 = (bf16[256,1024]{1,0:T(8,128)(2,1)S(1)}, bf16[256,1024]{1,0:T(8,128)(2,1)S(1)}, u32[]{:S(2)}, u32[]{:S(2)}) collective-permute-start(bf16[256,1024]{1,0:T(8,128)(2,1)S(1)} %slice.205), channel_id=1, source_target_pairs={{0,8},{2,10},{4,12},{6,14},{8,0},{10,2},{12,4},{14,6},{16,24},{18,... | collective-permute-start | bytes 1572872 | tf_op jit(solution)/shard_map/ppermute | solution.py:24
  550.9 55.3 %collective-permute-start.31 = (bf16[256,1024]{1,0:T(8,128)(2,1)S(1)}, bf16[256,1024]{1,0:T(8,128)(2,1)S(1)}, u32[]{:S(2)}, u32[]{:S(2)}) collective-permute-start(bf16[256,1024]{1,0:T(8,128)(2,1)S(1)} %slice.206), channel_id=1, source_target_pairs={{0,8},{2,10},{4,12},{6,14},{8,0},{10,2},{12,4},{14,6},{16,24},{18,... | collective-permute-start | bytes 1572872 | tf_op jit(solution)/shard_map/ppermute | solution.py:24
  562.1 75.7 %collective-permute-start.28 = (bf16[256,2048]{1,0:T(8,128)(2,1)S(1)}, bf16[256,2048]{1,0:T(8,128)(2,1)S(1)}, u32[]{:S(2)}, u32[]{:S(2)}) collective-permute-start(bf16[256,2048]{1,0:T(8,128)(2,1)S(1)} %constant_dynamic-slice_fusion.2), channel_id=1, source_target_pairs={{0,1},{1,0},{2,3},{3,2},{4,5},{5,4},{6,7},{7,6},{8,9},{9,8},{10,11... | collective-permute-start | bytes 3145736 | tf_op jit(solution)/shard_map/ppermute | solution.py:28
  572.8 34.1 %collective-permute-start.38 = (bf16[256,1024]{1,0:T(8,128)(2,1)S(1)}, bf16[256,1024]{1,0:T(8,128)(2,1)S(1)}, u32[]{:S(2)}, u32[]{:S(2)}) collective-permute-start(bf16[256,1024]{1,0:T(8,128)(2,1)S(1)} %fusion.15), channel_id=1, source_target_pairs={{0,1},{1,0},{2,3},{3,2},{4,5},{5,4},{6,7},{7,6},{8,9},{9,8},{10,11... | collective-permute-start | bytes 1572872 | tf_op jit(solution)/shard_map/ppermute | solution.py:28
  584.0 26.7 %collective-permute-start.36 = (bf16[256,1024]{1,0:T(8,128)(2,1)S(1)}, bf16[256,1024]{1,0:T(8,128)(2,1)S(1)}, u32[]{:S(2)}, u32[]{:S(2)}) collective-permute-start(bf16[256,1024]{1,0:T(8,128)(2,1)S(1)} %fusion.16), channel_id=1, source_target_pairs={{0,1},{1,0},{2,3},{3,2},{4,5},{5,4},{6,7},{7,6},{8,9},{9,8},{10,11... | collective-permute-start | bytes 1572872 | tf_op jit(solution)/shard_map/ppermute | solution.py:28
  595.2 26.7 %collective-permute-start.34 = (bf16[256,1024]{1,0:T(8,128)(2,1)S(1)}, bf16[256,1024]{1,0:T(8,128)(2,1)S(1)}, u32[]{:S(2)}, u32[]{:S(2)}) collective-permute-start(bf16[256,1024]{1,0:T(8,128)(2,1)S(1)} %fusion.17), channel_id=1, source_target_pairs={{0,1},{1,0},{2,3},{3,2},{4,5},{5,4},{6,7},{7,6},{8,9},{9,8},{10,11... | collective-permute-start | bytes 1572872 | tf_op jit(solution)/shard_map/ppermute | solution.py:28
  606.3 25.6 %collective-permute-start.32 = (bf16[256,1024]{1,0:T(8,128)(2,1)S(1)}, bf16[256,1024]{1,0:T(8,128)(2,1)S(1)}, u32[]{:S(2)}, u32[]{:S(2)}) collective-permute-start(bf16[256,1024]{1,0:T(8,128)(2,1)S(1)} %fusion.18), channel_id=1, source_target_pairs={{0,1},{1,0},{2,3},{3,2},{4,5},{5,4},{6,7},{7,6},{8,9},{9,8},{10,11... | collective-permute-start | bytes 1572872 | tf_op jit(solution)/shard_map/ppermute | solution.py:28
  634.8 4.5 copy-start.1
  (19 other events, 45.8 us)

commit v2 on v0

v2 whole, which is shorter than its diff:
```python
import functools
import math

import jax
import jax.numpy as jnp
from jax import lax
from jax.experimental import pallas as pl
from jax.experimental.pallas import tpu as pltpu
from jax.sharding import PartitionSpec as P

coupling = 0.5
SMEM = pl.BlockSpec(memory_space=pltpu.SMEM)
FREE = pl.CostEstimate(flops=0, bytes_accessed=0, transcendentals=0)
PARAMS = pltpu.CompilerParams(vmem_limit_bytes=56 * 1024 * 1024)


def silu_slope(argument):
    sigmoid_value = jax.nn.sigmoid(argument)
    return sigmoid_value * (1.0 + argument * (1.0 - sigmoid_value))


def after(value, *earlier):
    return lax.optimization_barrier((value, *earlier))[0]


def together(*values):
    return lax.optimization_barrier(values)


def hop(value, bits):
    size = lax.axis_size("dp")
    return lax.ppermute(value, "dp", [(i, i ^ bits) for i in range(size)])


def swap_mp(value):
    return lax.ppermute(value, "mp", [(0, 1), (1, 0)])


def place_of(block, me):
    relative = block ^ (me & ~1)
    return (relative & ~3) | ((relative & 1) << 1) | ((relative >> 1) & 1)


def block_at(place, me):
    return ((place & ~3) | ((place & 1) << 1) | ((place >> 1) & 1)) ^ (me & ~1)


def dot(left, right):
    return jnp.dot(left, right, preferred_element_type=jnp.float32)


def dot_t(left, right):
    return lax.dot_general(
        left, right, (((1,), (1,)), ((), ())), preferred_element_type=jnp.float32
    )


def call(body, cost=FREE, **settings):
    return pl.pallas_call(body, compiler_params=PARAMS, cost_estimate=cost, **settings)


def head_body(blocks, groups, at, uf, us, gf, gs, gain, down_t, up, *outs):
    (squashed_o, apg_o, inverse_o, lower_o, lower_share, input_share) = outs[:6]
    normed_own, normed_send, carried_own, carried_send = outs[6:]
    me, rank = at[0], at[1]
    width = uf.shape[1]
    column = width // blocks
    share = width // groups
    pre = dot_t(uf[...], down_t[...])
    squashed = (pre * jax.nn.sigmoid(pre)).astype(jnp.bfloat16)
    squashed_o[...] = squashed
    lower = (us[...].astype(jnp.float32) - dot(squashed, up[...])).astype(jnp.bfloat16)
    lower_o[...] = lower
    value = lower.astype(jnp.float32)
    inverse = lax.rsqrt(jnp.mean(value * value, axis=1, keepdims=True) + 1e-05)
    inverse_o[...] = jnp.broadcast_to(inverse, inverse_o.shape)
    normed = (value * inverse * gain[...].astype(jnp.float32)).astype(jnp.bfloat16)
    apg = (dot_t(gs[...], up[...]) * silu_slope(pre)).astype(jnp.bfloat16)
    apg_o[...] = apg
    carried = (gf[...].astype(jnp.float32) + dot(apg, down_t[...])).astype(jnp.bfloat16)
    for group in range(groups):

        @pl.when(rank == group)
        def _():
            part = slice(group * share, (group + 1) * share)
            lower_share[...] = lower[:, part]
            input_share[...] = (coupling * carried[:, part].astype(jnp.float32)).astype(
                jnp.bfloat16
            )

    for block in range(blocks):
        part = slice(block * column, (block + 1) * column)
        own = pl.multiple_of(place_of(block, me) * column, column)
        normed_own[:, pl.ds(own, column)] = normed[:, part]
        carried_own[:, pl.ds(own, column)] = carried[:, part]
        place = place_of(block, me ^ 4) * column - rank * share

        @pl.when((place >= 0) & (place < share))
        def _():
            to = pl.multiple_of(place, column)
            normed_send[:, pl.ds(to, column)] = normed[:, part]
            carried_send[:, pl.ds(to, column)] = carried[:, part]


def head(at, blocks, groups, uf, us, gf, gs, gain, down_t, up):
    tokens, width = uf.shape
    rank = up.shape[0]
    share = width // groups
    step = 64 if tokens % 64 == 0 else tokens
    row = lambda columns: pl.BlockSpec((step, columns), lambda i: (i, 0))
    whole = lambda a: pl.BlockSpec(a.shape, lambda i: (0, 0))
    outs = [rank, rank, 128, width, share, share, width, share, width, share]
    types = [jnp.bfloat16, jnp.bfloat16, jnp.float32] + [jnp.bfloat16] * 7
    return call(
        functools.partial(head_body, blocks, groups),
        grid=(tokens // step,),
        in_specs=[SMEM] + [row(width)] * 4 + [whole(gain), whole(down_t), whole(up)],
        out_specs=[row(c) for c in outs],
        out_shape=[jax.ShapeDtypeStruct((tokens, c), t) for c, t in zip(outs, types)],
    )(at, uf, us, gf, gs, gain, down_t, up)


def both_body(at, own, part, other, out):
    tokens, share = part.shape
    out[:tokens] = own[...]
    for group in range(2):
        place = group * share

        @pl.when(at[1] == group)
        def _():
            out[tokens:, place : place + share] = part[...]
            out[tokens:, share - place : 2 * share - place] = other[...]


def both_tokens(at, own, part, other):
    tokens, width = own.shape
    return call(
        both_body,
        in_specs=[SMEM] + [pl.BlockSpec(memory_space=pltpu.VMEM)] * 3,
        out_specs=pl.BlockSpec(memory_space=pltpu.VMEM),
        out_shape=jax.ShapeDtypeStruct((2 * tokens, width), own.dtype),
    )(at, own, part, other)


def stack(*units):
    columns, dtype = units[0][0].shape[1], units[0][0].dtype
    arrays = []
    for array, _, _ in units:
        if not any(array is a for a in arrays):
            arrays.append(array)
    which = [next(k for k, a in enumerate(arrays) if a is u[0]) for u in units]
    total = sum(u[2] for u in units)

    def body(*refs):
        out, held, got, put = refs[-4:]
        reads, writes, at = [], [], 0
        for i, (_, first, rows) in enumerate(units):
            here = held.at[pl.ds(at, rows)]
            reads.append(
                pltpu.make_async_copy(refs[which[i]].at[pl.ds(first, rows)], here, got.at[i])
            )
            writes.append(pltpu.make_async_copy(here, out.at[pl.ds(at, rows)], put.at[i]))
            at += rows
        for read in reads:
            read.start()
        for read, write in zip(reads, writes):
            read.wait()
            write.start()
        for write in writes:
            write.wait()

    anywhere = pl.BlockSpec(memory_space=pl.ANY)
    return call(
        body,
        in_specs=[anywhere] * len(arrays),
        out_specs=anywhere,
        out_shape=jax.ShapeDtypeStruct((total, columns), dtype),
        scratch_shapes=[
            pltpu.VMEM((total, columns), dtype),
            pltpu.SemaphoreType.DMA((len(units),)),
            pltpu.SemaphoreType.DMA((len(units),)),
        ],
    )(*arrays)


ANY = pl.BlockSpec(memory_space=pl.ANY)


def fetch(units, refs, held, sems):
    copies, at = [], 0
    for i, (_, first, rows) in enumerate(units):
        copies.append(
            pltpu.make_async_copy(
                refs[i].at[pl.ds(first, rows)], held.at[pl.ds(at, rows)], sems.at[i]
            )
        )
        at += rows
    for copy in copies:
        copy.start()
    for copy in copies:
        copy.wait()


def held_scratch(units):
    array = units[0][0]
    return [
        pltpu.VMEM((sum(u[2] for u in units), array.shape[1]), array.dtype),
        pltpu.SemaphoreType.DMA((len(units),)),
    ]


def both_halves(tokens, step, columns, use):
    for which in range(2):

        @pl.when(step == which)
        def _():
            use(tokens[which][:, columns])


def hidden_body(units, *refs):
    count = len(units)
    tokens, refs = refs[:2], refs[2:]
    hidden, slope, activated, held, sems = refs[count:]
    step = pl.program_id(0)

    @pl.when(step == 0)
    def _():
        fetch(units, refs, held, sems)

    def use(left):
        total = dot(left, held[...])
        hidden[...] = total
        sigmoid_value = jax.nn.sigmoid(total)
        slope[...] = sigmoid_value * (1.0 + total * (1.0 - sigmoid_value))
        activated[...] = (total * sigmoid_value).astype(jnp.bfloat16)

    both_halves(tokens, step, slice(None), use)


def hidden_kernel(tokens, units):
    count, width = tokens[0].shape
    columns = units[0][0].shape[1]
    whole = pl.BlockSpec((count, width), lambda i: (0, 0))
    out = pl.BlockSpec((count, columns), lambda i: (i, 0))
    return call(
        functools.partial(hidden_body, units),
        cost=work(4 * count * columns * width),
        grid=(2,),
        in_specs=[whole, whole] + [ANY] * len(units),
        out_specs=[out] * 3,
        out_shape=[
            jax.ShapeDtypeStruct((2 * count, columns), t)
            for t in (jnp.float32, jnp.float32, jnp.bfloat16)
        ],
        scratch_shapes=held_scratch(units),
    )(*tokens, *[u[0] for u in units])


def act_body(units, spans, extras, slope_given, *refs):
    count = len(units)
    tokens, refs = refs[:2], refs[2:]
    outs, (held, sems) = refs[count + extras : -2], refs[-2:]
    step = pl.program_id(0)

    @pl.when(step == 0)
    def _():
        fetch(units, refs, held, sems)

    for which in range(2):
        out = outs[which % len(outs)]

        @pl.when(step == which)
        def _():
            total, at = None, 0
            for first, depth in spans:
                term = dot(tokens[which][:, first : first + depth], held[at : at + depth])
                total = term if total is None else total + term
                at += depth
            if extras > slope_given:
                total = total + refs[count][...]
            if slope_given:
                total = total * refs[count + extras - 1][...]
            out[...] = total.astype(out.dtype)


def work(flops):
    return pl.CostEstimate(flops=flops // 4, bytes_accessed=0, transcendentals=0)


def act_kernel(tokens, spans, partial, slope=None):
    count, width = tokens[0].shape
    merged = []
    for first, us in spans:
        depth = sum(u[2] for u in us)
        if merged and sum(merged[-1]) == first:
            merged[-1] = (merged[-1][0], merged[-1][1] + depth)
        else:
            merged.append((first, depth))
    units = [u for _, us in spans for u in us]
    columns = units[0][0].shape[1]
    whole = pl.BlockSpec((count, width), lambda i: (0, 0))
    out = pl.BlockSpec((count, columns), lambda i: (i, 0))
    extra = [a for a in (partial, slope) if a is not None]
    half = pl.BlockSpec((count, columns), lambda i: (0, 0))
    if slope is None:
        out_specs, out_shape = out, jax.ShapeDtypeStruct((2 * count, columns), jnp.float32)
    else:
        out_specs = [half, half]
        out_shape = [jax.ShapeDtypeStruct((count, columns), jnp.bfloat16)] * 2
    return call(
        functools.partial(act_body, units, merged, len(extra), int(slope is not None)),
        cost=work(4 * count * columns * sum(d for _, d in merged)),
        grid=(2,),
        in_specs=[whole, whole] + [ANY] * len(units) + [out] * len(extra),
        out_specs=out_specs,
        out_shape=out_shape,
        scratch_shapes=held_scratch(units),
    )(*tokens, *[u[0] for u in units], *extra)


def stat_body(hidden, pre_grad, out):
    out[...] = jnp.sum(hidden[...] * pre_grad[...].astype(jnp.float32), axis=1, keepdims=True)


def stat_kernel(hidden, pre_grad):
    count, columns = hidden.shape
    step = count // 4
    block = pl.BlockSpec((step, columns), lambda i: (i, 0))
    return call(
        stat_body,
        grid=(4,),
        in_specs=[block, block],
        out_specs=pl.BlockSpec((step, 1), lambda i: (i, 0)),
        out_shape=jax.ShapeDtypeStruct((count, 1), jnp.float32),
    )(hidden, pre_grad)


def out_body(units, left, *refs):
    own, other, held, sems = refs[len(units) :]
    step = pl.program_id(0)

    @pl.when(step == 0)
    def _():
        fetch(units, refs, held, sems)
        own[...] = dot_t(left[...], held[...])

    @pl.when(step == 1)
    def _():
        other[...] = dot_t(left[...], held[...]).astype(jnp.bfloat16)


def out_kernel(left, units):
    count, depth = left.shape
    columns = sum(u[2] for u in units)
    out = pl.BlockSpec((count // 2, columns), lambda i: (0, 0))
    return call(
        functools.partial(out_body, units),
        cost=work(2 * count * columns * depth),
        grid=(2,),
        in_specs=[pl.BlockSpec((count // 2, depth), lambda i: (i, 0))] + [ANY] * len(units),
        out_specs=[out, out],
        out_shape=[
            jax.ShapeDtypeStruct((count // 2, columns), jnp.float32),
            jax.ShapeDtypeStruct((count // 2, columns), jnp.bfloat16),
        ],
        scratch_shapes=held_scratch(units),
    )(left, *[u[0] for u in units])


def final_body(blocks, layers, at, gs, lower, gain, inverse, curvature, *refs):
    mine, got, out = refs[:layers], refs[layers:-1], refs[-1]
    me = at[0]
    width = out.shape[1]
    column = width // blocks
    scale = inverse[...][:, :1]
    drop = scale * scale * curvature[...] / width
    for place in range(blocks):
        layer, inner = divmod(place * column, mine[0].shape[1])
        part = slice(inner, inner + column)
        grad = mine[layer][:, part].astype(jnp.float32) + got[layer][:, part].astype(jnp.float32)
        spot = pl.ds(pl.multiple_of(block_at(place, me) * column, column), column)
        out[:, spot] = (
            gs[:, spot].astype(jnp.float32)
            + scale * gain[:, spot].astype(jnp.float32) * grad
            - lower[:, spot].astype(jnp.float32) * drop
        ).astype(jnp.bfloat16)


def final_kernel(at, blocks, gs, lower, gain, inverse, curvature, mine, got):
    tokens, width = gs.shape
    step = 64 if tokens % 64 == 0 else tokens
    row = lambda a: pl.BlockSpec((step, a.shape[1]), lambda i: (i, 0))
    return call(
        functools.partial(final_body, blocks, len(mine)),
        grid=(tokens // step,),
        in_specs=[SMEM, row(gs), row(lower), pl.BlockSpec(gain.shape, lambda i: (0, 0))]
        + [row(a) for a in [inverse, curvature, *mine, *got]],
        out_specs=row(gs),
        out_shape=jax.ShapeDtypeStruct(gs.shape, jnp.bfloat16),
    )(at, gs, lower, gain, inverse, curvature, *mine, *got)


def restore_body(blocks, layers, at, *refs):
    out = refs[layers]
    column = out.shape[1] // blocks
    for place in range(blocks):
        layer, inner = divmod(place * column, refs[0].shape[1])
        spot = pl.multiple_of(block_at(place, at[0]) * column, column)
        out[:, pl.ds(spot, column)] = refs[layer][:, inner : inner + column]


def restore(at, blocks, arrays):
    vmem = pl.BlockSpec(memory_space=pltpu.VMEM)
    tokens, chunk = arrays[0].shape
    return call(
        functools.partial(restore_body, blocks, len(arrays)),
        in_specs=[SMEM] + [vmem] * len(arrays),
        out_specs=vmem,
        out_shape=jax.ShapeDtypeStruct((tokens, chunk * len(arrays)), arrays[0].dtype),
    )(at, *arrays)


def first_body(blocks, at, upper, *refs):
    sums, got, out = refs[:4], refs[4:8], refs[8]
    me, rank = at[0], at[1]
    share = out.shape[1]
    chunk = share // 2
    column = 2 * share // blocks
    pair = (rank ^ (me >> 3)) & 1
    for which in range(2):

        @pl.when(pair == which)
        def _():
            for place in range(which * blocks // 2, (which + 1) * blocks // 2):
                layer, part = divmod(place * column, chunk)
                block = block_at(place, me)
                spot = pl.multiple_of(block * column, column)
                to = pl.multiple_of(block * column - rank * share, column)
                columns = slice(part, part + column)
                frozen = sums[layer][:, columns].astype(jnp.float32) + got[layer][
                    :, columns
                ].astype(jnp.float32)
                out[:, pl.ds(to, column)] = (
                    (upper[:, pl.ds(spot, column)].astype(jnp.float32) - frozen) / coupling
                ).astype(jnp.bfloat16)


def first_kernel(at, blocks, upper, sums, got):
    tokens, width = upper.shape
    step = 64 if tokens % 64 == 0 else tokens
    row = lambda columns: pl.BlockSpec((step, columns), lambda i: (i, 0))
    return call(
        functools.partial(first_body, blocks),
        grid=(tokens // step,),
        in_specs=[SMEM, row(width)] + [row(a.shape[1]) for a in [*sums, *got]],
        out_specs=row(width // 2),
        out_shape=jax.ShapeDtypeStruct((tokens, width // 2), jnp.bfloat16),
    )(at, upper, *sums, *got)


def on_device(
    upper_first,
    upper_second,
    grad_first,
    grad_second,
    norm_gain,
    up_weight,
    down_weight,
    adapter_down,
    adapter_up,
):
    size = lax.axis_size("dp")
    groups = lax.axis_size("mp")
    me = lax.axis_index("dp")
    mp_rank = lax.axis_index("mp")
    at = jnp.stack([me, mp_rank]).astype(jnp.int32)
    tokens, model_width = upper_first.shape
    layers = size // 4
    share_width = model_width // groups
    offset = mp_rank * share_width
    grad_scale = 1.0 / math.sqrt(tokens * size)
    parity = (me >> 2) & 1
    quarter = up_weight.shape[1] // 2
    gain = norm_gain.reshape(1, model_width)
    paired = groups == 2 and layers == 4

    rows = up_weight.shape[0]
    chunk = 4 * rows
    far = range(3, layers)
    eighth = quarter // 2
    core = me & 1

    def cut(weight):
        mine = lax.dynamic_slice_in_dim(weight, core * quarter, quarter, 1)
        other = lax.dynamic_slice_in_dim(weight, (1 - core) * quarter, quarter, 1)
        return mine, other

    def by_parity(own, got):
        first = jnp.where(core == 0, own, got)
        pair = jnp.concatenate([first, jnp.where(core == 0, got, own)], axis=0)
        mine = lax.dynamic_slice_in_dim(pair, parity * eighth, eighth, 1)
        other = lax.dynamic_slice_in_dim(pair, (1 - parity) * eighth, eighth, 1)
        return mine, other

    def of_z(pair, s):
        return pair[s & 1]

    def units_of(piece, piece_y, first=0, count=2):
        return [(a, u * rows, rows) for u in range(first, first + count) for a in (piece, piece_y)]

    up_own, up_send = cut(up_weight)
    down_own, down_send = cut(down_weight)
    up_got = hop(up_send, 1)
    down_got = hop(down_send, 1)
    up = by_parity(up_own, up_got)
    (up, (down_own, down_got, upper_first, upper_second, grad_first, grad_second, adapter_up)) = (
        together(
            up,
            (down_own, down_got, upper_first, upper_second, grad_first, grad_second, adapter_up),
        )
    )

    uz, uy, dz, dy = [[None] * layers for _ in range(4)]
    uz[0] = up[0]
    uz[2] = hop(up[0], 2 << 2)
    uz[1] = hop(up[1], 1 << 2)
    uy[0] = hop(up[0], 2)
    down = by_parity(down_own, down_got)
    dz[0] = down[0]
    dy[0] = hop(down[0], 2)
    (
        squashed,
        adapter_pre_grad,
        inverse_rms,
        lower_full,
        lower_second,
        input_grad_first,
        normed_own,
        normed_send,
        carried_own,
        carried_send,
    ) = head(
        at,
        size,
        groups,
        upper_first,
        upper_second,
        grad_first,
        grad_second,
        gain,
        adapter_down.T,
        adapter_up,
    )
    up, down, uz, uy, dz, dy, normed_send, carried_send, adapter_pre_grad, squashed = together(
        up, down, uz, uy, dz, dy, normed_send, carried_send, adapter_pre_grad, squashed
    )

    for s in far:
        uz[s] = hop(of_z(up, s), s << 2)
    normed_part = hop(normed_send, 4)
    uy[2] = hop(uz[2], 2)
    uy[1] = hop(uz[1], 2)
    upper_slice = lax.dynamic_slice_in_dim(upper_first, offset, share_width, 1)
    second_slice = lax.dynamic_slice_in_dim(grad_second, offset, share_width, 1)
    down_grad_part = (
        jnp.einsum("tr,td->rd", adapter_pre_grad, upper_slice, preferred_element_type=jnp.float32)
        * grad_scale
    )
    up_grad_part = (
        jnp.einsum("tr,td->rd", squashed, second_slice, preferred_element_type=jnp.float32)
        * grad_scale
    )
    rank = down_grad_part.shape[0]
    is_core, is_y = (me & 1) == 1, (me & 2) == 2
    keep = jnp.where(is_core, up_grad_part, down_grad_part)
    give = jnp.where(is_core, down_grad_part, up_grad_part)
    uz, uy, normed_part, down, carried_send, keep, give = together(
        uz, uy, normed_part, down, carried_send, keep, give
    )

    low_rows, high_rows = slice(0, rows), slice(rows, 2 * rows)
    dzp = [[None, None] for _ in range(layers)]
    dyp = [[None, None] for _ in range(layers)]
    dzp[2][0] = hop(down[0][low_rows], 2 << 2)
    carried_part = hop(carried_send, 4)
    for s in far:
        uy[s] = hop(uz[s], 2)
    normed_other = swap_mp(normed_part) if groups == 2 else normed_part
    keep = keep + hop(give, 1)
    low, high = keep[: rank // 2], keep[rank // 2 :]
    share, give = jnp.where(is_y, high, low), jnp.where(is_y, low, high)
    dzp, uz, uy, carried_part, normed_part, normed_other, down, normed_own, carried_own, share, give = (
        together(
            dzp, uz, uy, carried_part, normed_part, normed_other, down, normed_own, carried_own,
            share, give,
        )
    )

    dzp[2][1] = hop(down[0][high_rows], 2 << 2)
    dzp[1][0] = hop(down[1][low_rows], 1 << 2)
    dyp[2][0] = hop(dzp[2][0], 2)
    carried_other = swap_mp(carried_part) if groups == 2 else carried_part

    def pair_tokens(own, piece, other):
        if groups == 2:
            return both_tokens(at, own, piece, other)
        return jnp.concatenate([own, lax.all_gather(piece, "mp", axis=1, tiled=True)], axis=0)

    up_units = sum([units_of(uz[s], uy[s]) for s in range(layers)], [])
    normed_both = pair_tokens(normed_own, normed_part, normed_other)
    hidden_pre, slope, activated = hidden_kernel([normed_both, hop(normed_both, 1)], up_units)
    dzp, dyp, carried_part, carried_other, hidden_pre, slope, activated, down, uz, uy, dz, dy = (
        together(
            dzp, dyp, carried_part, carried_other, hidden_pre, slope, activated, down, uz, uy, dz,
            dy,
        )
    )

    for s in far:
        dzp[s][0] = hop(of_z(down, s)[low_rows], s << 2)
    dyp[1][0] = hop(dzp[1][0], 2)
    dzp[1][1] = hop(down[1][high_rows], 1 << 2)
    dyp[2][1] = hop(dzp[2][1], 2)
    carried_both = pair_tokens(carried_own, carried_part, carried_other)
    carried_both = [carried_both, hop(carried_both, 1)]
    out_parts = [None] * layers
    zero = units_of(dz[0], dy[0])
    out_parts[0] = out_kernel(activated, zero)
    partial = act_kernel(carried_both, [(0, zero)], None)
    dzp, dyp, carried_both, out_parts, partial, uz, uy = together(
        dzp, dyp, carried_both, out_parts, partial, uz, uy
    )

    def unit(s, u):
        return [(dzp[s][u], 0, rows), (dyp[s][u], 0, rows)]

    def core_sum(parts):
        own, other = parts
        total = own + hop(other, 1).astype(jnp.float32)
        return total[:tokens], total[tokens:].astype(jnp.bfloat16)

    for s in far:
        dzp[s][1] = hop(of_z(down, s)[high_rows], s << 2)
        dyp[s][0] = hop(dzp[s][0], 2)
    dyp[1][1] = hop(dzp[1][1], 2)
    core_parts, got = [None] * layers, [None] * layers
    core_parts[0] = core_sum(out_parts[0])
    got[1] = hop(core_parts[0][1], 4)
    two = unit(2, 0) + unit(2, 1)
    out_parts[2] = out_kernel(activated, two)
    partial = act_kernel(
        carried_both, [(chunk, unit(1, 0)), (2 * chunk, two)], partial
    )
    up_chunks = [stack(*units_of(uz[s], uy[s])) for s in range(layers)]
    dzp, dyp, core_parts, got, out_parts, partial, up_chunks, hidden_pre, slope, share, give = (
        together(
            dzp, dyp, core_parts, got, out_parts, partial, up_chunks, hidden_pre, slope, share,
            give,
        )
    )

    for s in far:
        dyp[s][1] = hop(dzp[s][1], 2)
    core_parts[2] = core_sum(out_parts[2])
    got[3] = hop(core_parts[2][1], 4)
    one = unit(1, 0) + unit(1, 1)
    out_parts[1] = out_kernel(activated, one)
    partial = act_kernel(
        carried_both,
        [(chunk + chunk // 2, unit(1, 1))] + [(s * chunk, unit(s, 0)) for s in far],
        partial,
    )
    dyp, got, core_parts, out_parts, partial, share, give = together(
        dyp, got, core_parts, out_parts, partial, share, give
    )

    pre_own, pre_other = act_kernel(
        carried_both, [(s * chunk + chunk // 2, unit(s, 1)) for s in far], partial, slope
    )
    core_parts[1] = core_sum(out_parts[1])
    got[0] = hop(core_parts[1][1], 4)
    share = share + hop(give, 2)
    pre_own, pre_other, core_parts, got, hidden_pre, share = together(
        pre_own, pre_other, core_parts, got, hidden_pre, share
    )

    def out_sum(s):
        return (core_parts[s][0] + got[s].astype(jnp.float32)).astype(jnp.bfloat16)

    def to_holder(s):
        moves = []
        for i in range(size):
            holder = ((i >> 3) ^ (s >> 1)) & 1
            moves.append((2 * i + 1 - holder, 2 * i + holder))
        return lax.ppermute(out_sums[s], ("dp", "mp"), moves)

    def product(s):
        other = dot_t(pre_other, up_chunks[s]).astype(jnp.bfloat16)
        return core_sum((dot_t(pre_own, up_chunks[s]), other))

    def share_mp(piece):
        if groups == 2:
            return swap_mp(piece)
        whole = lax.psum(piece.astype(jnp.float32), "mp")
        return whole - piece.astype(jnp.float32)

    out_sums = [None] * layers
    other = half = None
    out_sums[0], out_sums[1] = out_sum(0), out_sum(1)
    sent = [None] * layers
    grads = [None] * layers
    grad_in = [None] * layers
    grad_mine = [None] * layers
    grad_got = [None] * layers
    grads[0] = product(0)
    if paired:
        sent[0] = to_holder(0)
    (grads, out_sums, sent, pre_own, pre_other, share) = together(
        grads, out_sums, sent, pre_own, pre_other, share
    )
    for step in range(layers + 1):
        if step < layers:
            grad_in[step ^ 1] = hop(grads[step][1], 4)
        if step:
            s = (step - 1) ^ 1
            grad_mine[s] = (grads[s][0] + grad_in[s].astype(jnp.float32)).astype(jnp.bfloat16)
            grad_got[s] = share_mp(grad_mine[s])
        if step + 1 < layers:
            grads[step + 1] = product(step + 1)
        if step == 0:
            if paired:
                sent[1] = to_holder(1)
            stat = jnp.concatenate(
                [
                    jnp.sum(hidden_pre[: 2 * tokens] * pre_own.astype(jnp.float32), axis=1),
                    jnp.sum(hidden_pre[2 * tokens :] * pre_other.astype(jnp.float32), axis=1),
                ]
            )[:, None]
            share = share + hop(share, 4)
        if step == 1:
            stat = stat[: 2 * tokens] + hop(stat[2 * tokens :], 1)
            bit = 8
            while bit < size:
                share = share + hop(share, bit)
                bit *= 2
        if step == 2:
            stat = stat[:tokens] + hop(stat[tokens:], 4)
            other = hop(share, 2)
            half = jnp.concatenate(
                [jnp.where(is_y, other, share), jnp.where(is_y, share, other)], axis=0
            )
        if step == 3:
            stat = stat + swap_mp(stat) if groups == 2 else lax.psum(stat, "mp")
            other = hop(half, 1)
        if step == max(layers - 2, 0):
            for s in far:
                out_parts[s] = out_kernel(activated, unit(s, 0) + unit(s, 1))
                core_parts[s] = core_sum(out_parts[s])
        if step == layers - 1:
            out_sums[3] = out_sum(3)
            if paired:
                sent[3] = to_holder(3)
        if step == layers:
            for s in far:
                got[s ^ 1] = hop(core_parts[s][1], 4)
        state = (
            grads, grad_in, grad_mine, grad_got, out_sums, sent, core_parts, got, stat, share,
            other, pre_own, pre_other, hidden_pre,
        )
        (
            grads, grad_in, grad_mine, grad_got, out_sums, sent, core_parts, got, stat, share,
            other, pre_own, pre_other, hidden_pre,
        ) = together(*state)
    curvature = stat
    out_sums = [out_sum(s) if out_sums[s] is None else out_sums[s] for s in range(layers)]
    adapter_down_grad = jnp.where(is_core, other, half).T
    adapter_up_grad = jnp.where(is_core, half, other)

    input_grad_second = final_kernel(
        at,
        size,
        grad_second,
        lower_full,
        gain,
        inverse_rms,
        curvature,
        grad_mine,
        grad_got,
    )

    if paired:
        sent[2] = to_holder(2)
        lower_first = first_kernel(at, size, upper_first, out_sums, sent)
    else:
        out_whole = restore(at, size, out_sums)
        frozen_share = lax.psum_scatter(
            out_whole.astype(jnp.float32), "mp", scatter_dimension=1, tiled=True
        )
        lower_first = ((upper_slice.astype(jnp.float32) - frozen_share) / coupling).astype(
            jnp.bfloat16
        )
    return (
        lower_first,
        lower_second,
        input_grad_first,
        input_grad_second,
        adapter_down_grad,
        adapter_up_grad,
    )


def solution(mesh):
    return jax.shard_map(
        on_device,
        mesh=mesh,
        in_specs=(
            P("dp", None),
            P("dp", None),
            P("dp", None),
            P("dp", None),
            P(),
            P("dp", "mp"),
            P("dp", "mp"),
            P(),
            P(),
        ),
        out_specs=(
            P("dp", "mp"),
            P("dp", "mp"),
            P("dp", "mp"),
            P("dp", None),
            P("mp", None),
            P(None, "mp"),
        ),
        check_vma=False,
    )
```

time: 745 us -> 522 us (0.70)
  waiting for transfers between devices: 601 us -> 240 us
  Pallas kernels: 0 us -> 151 us
  matrix products: 103 us -> 26 us
  starting transfers between devices: 0.24 us -> 59.6 us
  between operations: 14.2 us -> 2.25 us
  other arithmetic: 13 us -> 21.9 us
    all_gather x3 -> x0, waiting for transfers between devices: 459 us -> none  [the longest x1 223 us: on_device(): up_full = lax.all_gather(up_weight, 'dp', axis=0, tiled=True)]
    ppermute x0 -> x61, waiting for transfers between devices: none -> 240 us  [the longest x50 189 us: hop(): return lax.ppermute(value, 'dp', [(i, i ^ bits) for i in range(size)])]
    pallas_call x0 -> x18, Pallas kernels: none -> 151 us  [the longest x4 46.6 us: act_kernel(): call(functools.partial(act_body, units, merged, len(extra), int(slope is...]
    psum x1 -> x0, waiting for transfers between devices: 97.3 us -> none  [on_device(): lax.psum((down_grad_part, up_grad_part), 'dp')]
    dot_general x9, matrix products: 102 us -> 24.4 us  [the longest x8 22 us: dot_t(): lax.dot_general(left, right, (((1,), (1,)), ((), ())), preferred_element_...]
    ppermute x0 -> x61, starting transfers between devices: none -> 59.6 us  [the longest x50 40.4 us: hop(): return lax.ppermute(value, 'dp', [(i, i ^ bits) for i in range(size)])]
    reduce_scatter x2 -> x0, waiting for transfers between devices: 43.3 us -> none  [the longest x1 21.9 us: on_device(): lax.psum_scatter(normed_part, 'mp', scatter_dimension=1, tiled=True)]
    convert_element_type x5 -> x8, other arithmetic: 13 us -> 3.04 us  [the longest x4 2.44 us: on_device(): (grads[s][0] + grad_in[s].astype(jnp.float32)).astype(jnp.bfloat16)]
  transfers between devices with their start and end apart: 6 -> 61, of which waited for: 6 -> 29; matrix products, arithmetic and copies ran while one was open for 10% -> 9% of each run, Pallas kernels for 0% -> 26%
where the time goes in v2:
time: 522 us; the launch traced here: 517 us
  waiting for transfers between devices  240 us (46%)
  Pallas kernels  151 us (29%)
  starting transfers between devices  59.6 us (11%)
  matrix products  26 us (5%)
  other arithmetic  21.9 us (4%)
  local copies, waits for them, and re-layouts  16.5 us (3%)
    ppermute x50, waiting for transfers between devices, hop(): return lax.ppermute(value, 'dp', [(i, i ^ bits) for i in range(size)])  189 us
    pallas_call x4, Pallas kernels, act_kernel(): call(functools.partial(act_body, units, merged, len(extra), int(slope is...  46.6 us
    ppermute x50, starting transfers between devices, hop(): return lax.ppermute(value, 'dp', [(i, i ^ bits) for i in range(size)])  40.4 us
    ppermute x7, waiting for transfers between devices, swap_mp(): return lax.ppermute(value, 'mp', [(0, 1), (1, 0)])  38.1 us
    pallas_call x4, Pallas kernels, out_kernel(): call(functools.partial(out_body, units), cost=work(2 * count * columns *...  35.1 us
    pallas_call x1, Pallas kernels, hidden_kernel(): call(functools.partial(hidden_body, units), cost=work(4 * count * columns...  24.9 us
    dot_general x8, matrix products, dot_t(): lax.dot_general(left, right, (((1,), (1,)), ((), ())), preferred_element_...  22 us
    ppermute x4, waiting for transfers between devices, to_holder(): return lax.ppermute(out_sums[s], ('dp', 'mp'), moves)  12.8 us
  transfers between devices with their start and end apart: 61, of which 29 were waited for; matrix products, arithmetic and copies ran while one was open for 9% of the time, Pallas kernels for 26%

profile of v2, /device:TPU:0, one launch (start us, length us, event | category | flops | bytes accessed | tf_op | source)
XLA Modules:
  0.0 516.9 jit_solution(14168728372492051348)
XLA Ops:
  2.6 3.1 constant_dynamic-slice_fusion
  5.8 2.3 broadcast_select_fusion.2
  8.0 2.0 fusion.2
  13.1 3.0 collective-permute-start.5
  16.1 2.6 collective-permute-start.3
  21.7 11.8 %shard_map.136 = (bf16[256,64]{1,0:T(8,128)(2,1)}, bf16[256,64]{1,0:T(8,128)(2,1)}, f32[256,128]{1,0:T(8,128)}, bf16[256,4096]{1,0:T(8,128)(2,1)}, bf16[256,2048...) custom-call(s32[2]{0:T(128)} %pad_add_fusion.at, ...), custom_call_target="tpu_custom_call" | custom-call | tf_op jit(solution)/shard_map/pallas_call | solution.py:114
  33.5 15.0 %collective-permute-done.5.refs_1_.refs_3_.refs_5_ = bf16[512,1408]{1,0:T(8,128)(2,1)S(1)} collective-permute-done((bf16[512,1408]{1,0:T(8,128)(2,1)S(1)}, bf16[512,1408]{1,0:T(8,128)(2,1)S(1)}, u32[]{:S(2)}, u32[]{:S(2)}) %collective-permute-start.5) | collective-permute-done | bytes 1441824 | tf_op jit(solution)/shard_map/ppermute | solution.py:32
  48.5 33.1 %collective-permute-done.3.refs_10_.refs_12_.refs_0_ = bf16[512,1408]{1,0:T(8,128)(2,1)} collective-permute-done((bf16[512,1408]{1,0:T(8,128)(2,1)}, bf16[512,1408]{1,0:T(8,128)(2,1)}, u32[]{:S(2)}, u32[]{:S(2)}) %collective-permute-start.3) | collective-permute-done | bytes 1441824 | tf_op jit(solution)/shard_map/ppermute | solution.py:32
  82.3 2.4 collective-permute-start.6
  88.3 2.4 broadcast_select_fusion.5
  90.7 48.4 %collective-permute-done.9.part = bf16[256,2048]{1,0:T(8,128)(2,1)} collective-permute-done((bf16[256,2048]{1,0:T(8,128)(2,1)}, bf16[256,2048]{1,0:T(8,128)(2,1)}, u32[]{:S(2)}, u32[]{:S(2)}) %collective-permute-start.9) | collective-permute-done | bytes 1048608 | tf_op jit(solution)/shard_map/ppermute | solution.py:32
  139.2 9.8 %collective-permute-done.8.refs_11_.refs_13_.refs_1_ = bf16[512,1408]{1,0:T(8,128)(2,1)} collective-permute-done((bf16[512,1408]{1,0:T(8,128)(2,1)}, bf16[512,1408]{1,0:T(8,128)(2,1)}, u32[]{:S(2)}, u32[]{:S(2)}) %collective-permute-start.8) | collective-permute-done | bytes 1441824 | tf_op jit(solution)/shard_map/ppermute | solution.py:32
  155.2 32.1 %collective-permute-done.10.refs_0_.refs_4_ = bf16[256,1408]{1,0:T(8,128)(2,1)} collective-permute-done((bf16[256,1408]{1,0:T(8,128)(2,1)}, bf16[256,1408]{1,0:T(8,128)(2,1)}, u32[]{:S(2)}, u32[]{:S(2)}) %collective-permute-start.10) | collective-permute-done | bytes 720928 | tf_op jit(solution)/shard_map/ppermute | solution.py:32
  188.6 5.4 %shard_map.137.refs_0_ = bf16[512,4096]{1,0:T(8,128)(2,1)} custom-call(s32[2]{0:T(128)} %pad_add_fusion.at, bf16[256,4096]{1,0:T(8,128)(2,1)} %get-tuple-element.298.own, bf16[256,2048]{1,0:T(8,128)(2,1)} %collective-permute-done.9.part, bf16[256,2048]{1,0:T(8,128)(2,1)} %collective-permute-done.13.other), custom_call_target="tpu_custom_call" | custom-call | tf_op jit(solution)/shard_map/pallas_call | solution.py:137
  198.5 3.0 collective-permute-done.19.refs_1_
  201.5 24.9 %shard_map.138 = (f32[1024,1408]{1,0:T(8,128)}, f32[1024,1408]{1,0:T(8,128)}, bf16[1024,1408]{1,0:T(8,128)(2,1)}) custom-call(bf16[512,4096]{1,0:T(8,128)(2,1)} %shard_map.137.refs_0_, bf16[512,4096]{1,0:T(8,128)(2,1)} %collective-permute-done.19.refs_1_, bf16[512,1408]{1,0:T(8,128)(2,1)} %get-tuple-element.350.refs_2_.refs_4_.refs_0_, ...), custom_call_target="tpu_custom_call" | custom-call | flops 2952790016 | tf_op jit(solution)/shard_map/pallas_call | solution.py:245
  226.5 2.5 collective-permute-done.15.refs_2_.refs_0_
  231.5 4.5 shard_map.139.refs_0_
  237.5 2.2 collective-permute-start.21
  241.7 8.7 %shard_map.140 = (f32[512,1024]{1,0:T(8,128)}, bf16[512,1024]{1,0:T(8,128)(2,1)}) custom-call(bf16[1024,1408]{1,0:T(8,128)(2,1)} %get-tuple-element.322.left, bf16[512,1408]{1,0:T(8,128)(2,1)} %copy-done.1, bf16[512,1408]{1,0:T(8,128)(2,1)} %copy-done.2, bf16[512,1408]{1,0:T(8,128)(2,1)} %copy-done.1, bf16[512,1408]{1,0:T(8,128)(2,1)} %copy-done.2), custom_call_target="tpu_custom_call" | custom-call | flops 738197504 | tf_op jit(solution)/shard_map/pallas_call | solution.py:356
  250.5 2.0 copy-done
  252.4 10.5 %shard_map.141.refs_8_ = f32[1024,1408]{1,0:T(8,128)} custom-call(bf16[512,4096]{1,0:T(8,128)(2,1)} %shard_map.139.refs_0_, bf16[512,4096]{1,0:T(8,128)(2,1)} %copy-done, bf16[512,1408]{1,0:T(8,128)(2,1)} %copy-done.1, bf16[512,1408]{1,0:T(8,128)(2,1)} %copy-done.2, bf16[512,1408]{1,0:T(8,128)(2,1)} %copy-done.1, bf16[512,1408]{1,0:T(8,128)(2,1)} %copy-done.2), custom_call_target="tpu_custom_call" | custom-call | flops 738197504 | tf_op jit(solution)/shard_map/pallas_call | solution.py:310
  262.9 9.3 %collective-permute-done.21.refs_4_.refs_0_ = bf16[256,1408]{1,0:T(8,128)(2,1)S(1)} collective-permute-done((bf16[256,1408]{1,0:T(8,128)(2,1)}, bf16[256,1408]{1,0:T(8,128)(2,1)S(1)}, u32[]{:S(2)}, u32[]{:S(2)}) %collective-permute-start.21) | collective-permute-done | bytes 720928 | tf_op jit(solution)/shard_map/ppermute | solution.py:32
  277.0 2.0 convert_add_fusion.7
  279.4 3.1 shard_map.147
  282.6 2.8 shard_map.146
  285.4 2.8 shard_map.145
  288.1 2.8 shard_map.144
  290.9 8.6 %shard_map.142 = (f32[512,1024]{1,0:T(8,128)}, bf16[512,1024]{1,0:T(8,128)(2,1)}) custom-call(bf16[1024,1408]{1,0:T(8,128)(2,1)} %get-tuple-element.322.left, bf16[256,1408]{1,0:T(8,128)(2,1)} %collective-permute-done.10.refs_0_.refs_4_, bf16[256,1408]{1,0:T(8,128)(2,1)} %copy-done.18, bf16[256,1408]{1,0:T(8,128)(2,1)} %copy-done.17, ...), custom_call_target="tpu_custom_call" | custom-call | flops 738197504 | tf_op jit(solution)/shard_map/pallas_call | solution.py:356
  299.6 13.7 %shard_map.143.refs_6_ = f32[1024,1408]{1,0:T(8,128)} custom-call(bf16[512,4096]{1,0:T(8,128)(2,1)} %shard_map.139.refs_0_, bf16[512,4096]{1,0:T(8,128)(2,1)} %copy-done, bf16[256,1408]{1,0:T(8,128)(2,1)} %copy-done.14, bf16[256,1408]{1,0:T(8,128)(2,1)} %copy-done.19, bf16[256,1408]{1,0:T(8,128)(2,1)} %collective-permute-done.10.refs_0_.refs_4_, ...), custom_call_target="tpu_custom_call" | custom-call | flops 1107296256 | tf_op jit(solution)/shard_map/pallas_call | solution.py:310
  313.5 1.6 collective-permute-start.30
  318.1 9.0 %shard_map.148 = (f32[512,1024]{1,0:T(8,128)}, bf16[512,1024]{1,0:T(8,128)(2,1)}) custom-call(bf16[1024,1408]{1,0:T(8,128)(2,1)} %get-tuple-element.322.left, bf16[256,1408]{1,0:T(8,128)(2,1)} %copy-done.14, bf16[256,1408]{1,0:T(8,128)(2,1)} %copy-done.19, bf16[256,1408]{1,0:T(8,128)(2,1)} %copy-done.16, bf16[256,1408]{1,0:T(8,128)(2,1)} %copy-done.20), custom_call_target="tpu_custom_call" | custom-call | flops 738197504 | tf_op jit(solution)/shard_map/pallas_call | solution.py:356
  327.1 11.6 %shard_map.149.refs_4_ = f32[1024,1408]{1,0:T(8,128)} custom-call(bf16[512,4096]{1,0:T(8,128)(2,1)} %shard_map.139.refs_0_, bf16[512,4096]{1,0:T(8,128)(2,1)} %copy-done, bf16[256,1408]{1,0:T(8,128)(2,1)} %copy-done.16, bf16[256,1408]{1,0:T(8,128)(2,1)} %copy-done.20, bf16[256,1408]{1,0:T(8,128)(2,1)} %copy-done.13, bf16[256,1408]{1,0:T(8,128)(2,1)} %copy-done.15, ...), custom_call_target="tpu_custom_call" | custom-call | flops 738197504 | tf_op jit(solution)/shard_map/pallas_call | solution.py:310
  338.8 2.6 collective-permute-done.33
  344.1 10.9 %shard_map.150 = (bf16[512,1408]{1,0:T(8,128)(2,1)}, bf16[512,1408]{1,0:T(8,128)(2,1)}) custom-call(bf16[512,4096]{1,0:T(8,128)(2,1)} %shard_map.139.refs_0_, bf16[512,4096]{1,0:T(8,128)(2,1)} %copy-done, bf16[256,1408]{1,0:T(8,128)(2,1)} %copy-done.26, bf16[256,1408]{1,0:T(8,128)(2,1)} %copy-done.27, f32[1024,1408]{1,0:T(8,128)} %shard_map.149.refs_4_, ...), custom_call_target="tpu_custom_call" | custom-call | flops 369098752 | tf_op jit(solution)/shard_map/pallas_call | solution.py:310
  356.8 3.3 convolution_convert_fusion.3
  362.9 1.8 convert_add_fusion.4
  365.7 11.0 %collective-permute-done.37.refs_4_ = bf16[256,1024]{1,0:T(8,128)(2,1)S(1)} collective-permute-done((bf16[256,1024]{1,0:T(8,128)(2,1)S(1)}, bf16[256,1024]{1,0:T(8,128)(2,1)S(1)}, u32[]{:S(2)}, u32[]{:S(2)}) %collective-permute-start.37) | collective-permute-done | bytes 524320 | tf_op jit(solution)/shard_map/ppermute | solution.py:695
  376.7 2.8 convolution_convert_fusion.2
  379.5 8.8 %shard_map.151 = (f32[512,1024]{1,0:T(8,128)}, bf16[512,1024]{1,0:T(8,128)(2,1)}) custom-call(bf16[1024,1408]{1,0:T(8,128)(2,1)} %get-tuple-element.322.left, bf16[256,1408]{1,0:T(8,128)(2,1)} %copy-done.13, bf16[256,1408]{1,0:T(8,128)(2,1)} %copy-done.15, bf16[256,1408]{1,0:T(8,128)(2,1)} %copy-done.26, bf16[256,1408]{1,0:T(8,128)(2,1)} %copy-done.27), custom_call_target="tpu_custom_call" | custom-call | flops 738197504 | tf_op jit(solution)/shard_map/pallas_call | solution.py:356
  392.1 2.0 multiply_reduce_fusion.1
  394.1 3.8 collective-permute-done.41
  398.0 3.2 convert_add_fusion.3
  402.1 6.2 %collective-permute-done.39 = bf16[256,1024]{1,0:T(8,128)(2,1)S(1)} collective-permute-done((bf16[256,1024]{1,0:T(8,128)(2,1)}, bf16[256,1024]{1,0:T(8,128)(2,1)S(1)}, u32[]{:S(2)}, u32[]{:S(2)}) %collective-permute-start.39) | collective-permute-done | bytes 524320 | tf_op jit(solution)/shard_map/ppermute | solution.py:32
  408.3 2.8 convolution_convert_fusion.1
  414.0 2.0 add_convert_fusion.5.refs_1_
  416.1 2.5 collective-permute-start.44
  420.2 7.7 %collective-permute-done.46 = f32[32,2048]{1,0:T(8,128)} collective-permute-done((f32[32,2048]{1,0:T(8,128)S(1)}, f32[32,2048]{1,0:T(8,128)}, u32[]{:S(2)}, u32[]{:S(2)}) %collective-permute-start.46) | collective-permute-done | bytes 262176 | tf_op jit(solution)/shard_map/ppermute | solution.py:32
  428.9 4.5 convert_add_fusion.2
  433.5 3.8 collective-permute-done.43
  438.2 1.8 convolution_convert_fusion
  441.1 2.0 collective-permute-start.48
  444.9 1.8 convert_add_fusion.1
  447.0 7.7 %collective-permute-done.49.refs_4_ = bf16[256,1024]{1,0:T(8,128)(2,1)S(1)} collective-permute-done((bf16[256,1024]{1,0:T(8,128)(2,1)S(1)}, bf16[256,1024]{1,0:T(8,128)(2,1)S(1)}, u32[]{:S(2)}, u32[]{:S(2)}) %collective-permute-start.49) | collective-permute-done | bytes 524320 | tf_op jit(solution)/shard_map/ppermute | solution.py:36
  455.6 3.3 collective-permute-start.55
  459.2 1.8 collective-permute-start.53
  461.0 1.9 collective-permute-start.56
  462.9 21.0 %collective-permute-done.56 = f32[256,1]{1,0:T(8,128)S(1)} collective-permute-done((f32[256,1]{1,0:T(8,128)S(1)}, f32[256,1]{1,0:T(8,128)S(1)}, u32[]{:S(2)}, u32[]{:S(2)}) %collective-permute-start.56) | collective-permute-done | bytes 1056 | tf_op jit(solution)/shard_map/ppermute | solution.py:36
  484.8 2.5 collective-permute-start.58
  488.8 9.4 %collective-permute-done.58.refs_6_ = bf16[256,1024]{1,0:T(8,128)(2,1)S(1)} collective-permute-done((bf16[256,1024]{1,0:T(8,128)(2,1)S(1)}, bf16[256,1024]{1,0:T(8,128)(2,1)S(1)}, u32[]{:S(2)}, u32[]{:S(2)}) %collective-permute-start.58) | collective-permute-done | bytes 524320 | tf_op jit(solution)/shard_map/ppermute | solution.py:36
  499.9 2.3 collective-permute-start.60
  502.2 6.2 %shard_map.153 = bf16[256,4096]{1,0:T(8,128)(2,1)} custom-call(s32[2]{0:T(128)} %pad_add_fusion.at, bf16[256,4096]{1,0:T(8,128)(2,1)} %gs.1, bf16[256,4096]{1,0:T(8,128)(2,1)} %get-tuple-element.492.lower, bf16[1,4096]{1,0:T(2,128)(2,1)} %reshape.15.gain, f32[256,128]{1,0:T(8,128)} %get-tuple-element.493.inverse, f32[256,1]{1,0:T(8,128)} %add.114.curvature, ...), custom_call_target="tpu_custom_call" | custom-call | tf_op jit(solution)/shard_map/pallas_call | solution.py:393
  509.6 1.8 collective-permute-done.60.refs_6_
  512.2 4.6 shard_map.152
  (281 shorter events, 67.8 us)
Async XLA Ops:
  2.1 3.7 collective-permute-start
  5.7 4.3 collective-permute-start.1
  13.1 182.6 %copy-start.1 = (bf16[512,1408]{1,0:T(8,128)(2,1)}, bf16[512,1408]{1,0:T(8,128)(2,1)S(1)}, u32[]{:S(2)}) copy-start(bf16[512,1408]{1,0:T(8,128)(2,1)S(1)} %get-tuple-element.323.refs_0_.refs_2_.refs_4_) | copy-start | bytes 4325380
  13.1 35.4 %collective-permute-start.5 = (bf16[512,1408]{1,0:T(8,128)(2,1)S(1)}, bf16[512,1408]{1,0:T(8,128)(2,1)S(1)}, u32[]{:S(2)}, u32[]{:S(2)}) collective-permute-start(bf16[512,1408]{1,0:T(8,128)(2,1)S(1)} %get-tuple-element.323.refs_0_.refs_2_.refs_4_), channel_id=1, source_target_pairs={{0,4},{2,6},{4,0},{6,2},{8,12},{10,14},{12,8},{14,10},{16,20},{18,... | collective-permute-start | bytes 4325384 | tf_op jit(solution)/shard_map/ppermute | solution.py:32
  16.1 65.5 %collective-permute-start.3 = (bf16[512,1408]{1,0:T(8,128)(2,1)}, bf16[512,1408]{1,0:T(8,128)(2,1)}, u32[]{:S(2)}, u32[]{:S(2)}) collective-permute-start(bf16[512,1408]{1,0:T(8,128)(2,1)} %get-tuple-element.350.refs_2_.refs_4_.refs_0_), channel_id=1, source_target_pairs={{0,16},{2,18},{4,20},{6,22},{8,24},{10,26},{12,28},{14,30},{16,0},... | collective-permute-start | bytes 4325384 | tf_op jit(solution)/shard_map/ppermute | solution.py:32
  18.7 62.9 %collective-permute-start.4 = (bf16[512,1408]{1,0:T(8,128)(2,1)}, bf16[512,1408]{1,0:T(8,128)(2,1)}, u32[]{:S(2)}, u32[]{:S(2)}) collective-permute-start(bf16[512,1408]{1,0:T(8,128)(2,1)} %get-tuple-element.350.refs_2_.refs_4_.refs_0_), channel_id=1, source_target_pairs={{0,4},{2,6},{4,0},{6,2},{8,12},{10,14},{12,8},{14,10},{16,20},{18,... | collective-permute-start | bytes 4325384 | tf_op jit(solution)/shard_map/ppermute | solution.py:32
  19.2 63.1 %collective-permute-start.2 = (bf16[512,1408]{1,0:T(8,128)(2,1)}, bf16[512,1408]{1,0:T(8,128)(2,1)}, u32[]{:S(2)}, u32[]{:S(2)}) collective-permute-start(bf16[512,1408]{1,0:T(8,128)(2,1)} %get-tuple-element.271), channel_id=1, source_target_pairs={{0,8},{2,10},{4,12},{6,14},{8,0},{10,2},{12,4},{14,6},{16,24},{18,... | collective-permute-start | bytes 4325384 | tf_op jit(solution)/shard_map/ppermute | solution.py:32
  48.5 42.3 %copy-start.2 = (bf16[512,1408]{1,0:T(8,128)(2,1)}, bf16[512,1408]{1,0:T(8,128)(2,1)S(1)}, u32[]{:S(2)}) copy-start(bf16[512,1408]{1,0:T(8,128)(2,1)S(1)} %collective-permute-done.5.refs_1_.refs_3_.refs_5_) | copy-start | bytes 4325380
  82.3 56.9 %collective-permute-start.6 = (bf16[512,1408]{1,0:T(8,128)(2,1)}, bf16[512,1408]{1,0:T(8,128)(2,1)}, u32[]{:S(2)}, u32[]{:S(2)}) collective-permute-start(bf16[512,1408]{1,0:T(8,128)(2,1)} %get-tuple-element.271), channel_id=1, source_target_pairs={{0,24},{2,26},{4,28},{6,30},{8,16},{10,18},{12,20},{14,22},{16,8},... | collective-permute-start | bytes 4325384 | tf_op jit(solution)/shard_map/ppermute | solution.py:32
  84.7 54.5 %collective-permute-start.7 = (bf16[512,1408]{1,0:T(8,128)(2,1)}, bf16[512,1408]{1,0:T(8,128)(2,1)}, u32[]{:S(2)}, u32[]{:S(2)}) collective-permute-start(bf16[512,1408]{1,0:T(8,128)(2,1)} %collective-permute-done.2.refs_6_.refs_8_.refs_0_), channel_id=1, source_target_pairs={{0,4},{2,6},{4,0},{6,2},{8,12},{10,14},{12,8},{14,10},{16,20},{18,... | collective-permute-start | bytes 4325384 | tf_op jit(solution)/shard_map/ppermute | solution.py:32
  85.3 63.6 %collective-permute-start.8 = (bf16[512,1408]{1,0:T(8,128)(2,1)}, bf16[512,1408]{1,0:T(8,128)(2,1)}, u32[]{:S(2)}, u32[]{:S(2)}) collective-permute-start(bf16[512,1408]{1,0:T(8,128)(2,1)} %collective-permute-done.3.refs_10_.refs_12_.refs_0_), channel_id=1, source_target_pairs={{0,4},{2,6},{4,0},{6,2},{8,12},{10,14},{12,8},{14,10},{16,20},{18,... | collective-permute-start | bytes 4325384 | tf_op jit(solution)/shard_map/ppermute | solution.py:32
  86.7 52.4 %collective-permute-start.9 = (bf16[256,2048]{1,0:T(8,128)(2,1)}, bf16[256,2048]{1,0:T(8,128)(2,1)}, u32[]{:S(2)}, u32[]{:S(2)}) collective-permute-start(bf16[256,2048]{1,0:T(8,128)(2,1)} %get-tuple-element.273), channel_id=1, source_target_pairs={{0,8},{2,10},{4,12},{6,14},{8,0},{10,2},{12,4},{14,6},{16,24},{18,... | collective-permute-start | bytes 3145736 | tf_op jit(solution)/shard_map/ppermute | solution.py:32
  148.9 39.6 %collective-permute-start.11 = (bf16[512,1408]{1,0:T(8,128)(2,1)}, bf16[512,1408]{1,0:T(8,128)(2,1)S(1)}, u32[]{:S(2)}, u32[]{:S(2)}) collective-permute-start(bf16[512,1408]{1,0:T(8,128)(2,1)} %collective-permute-done.6.refs_14_.refs_16_.refs_0_), channel_id=1, source_target_pairs={{0,4},{2,6},{4,0},{6,2},{8,12},{10,14},{12,8},{14,10},{16,20},{18,... | collective-permute-start | bytes 4325384 | tf_op jit(solution)/shard_map/ppermute | solution.py:32
  149.5 39.1 %collective-permute-start.12 = (bf16[256,2048]{1,0:T(8,128)(2,1)}, bf16[256,2048]{1,0:T(8,128)(2,1)}, u32[]{:S(2)}, u32[]{:S(2)}) collective-permute-start(bf16[256,2048]{1,0:T(8,128)(2,1)} %get-tuple-element.287), channel_id=1, source_target_pairs={{0,8},{2,10},{4,12},{6,14},{8,0},{10,2},{12,4},{14,6},{16,24},{18,... | collective-permute-start | bytes 3145736 | tf_op jit(solution)/shard_map/ppermute | solution.py:32
  149.5 39.1 %collective-permute-start.13 = (bf16[256,2048]{1,0:T(8,128)(2,1)}, bf16[256,2048]{1,0:T(8,128)(2,1)}, u32[]{:S(2)}, u32[]{:S(2)}) collective-permute-start(bf16[256,2048]{1,0:T(8,128)(2,1)} %collective-permute-done.9.part), channel_id=1, source_target_pairs={{0,1},{1,0},{2,3},{3,2},{4,5},{5,4},{6,7},{7,6},{8,9},{9,8},{10,11... | collective-permute-start | bytes 3145736 | tf_op jit(solution)/shard_map/ppermute | solution.py:36
  151.0 2.3 collective-permute-start.14
  151.9 35.4 %collective-permute-start.10 = (bf16[256,1408]{1,0:T(8,128)(2,1)}, bf16[256,1408]{1,0:T(8,128)(2,1)}, u32[]{:S(2)}, u32[]{:S(2)}) collective-permute-start(bf16[256,1408]{1,0:T(8,128)(2,1)} %slice.96), channel_id=1, source_target_pairs={{0,16},{2,18},{4,20},{6,22},{8,24},{10,26},{12,28},{14,30},{16,0},... | collective-permute-start | bytes 2162696 | tf_op jit(solution)/shard_map/ppermute | solution.py:32
  194.0 7.5 %collective-permute-start.19 = (bf16[512,4096]{1,0:T(8,128)(2,1)}, bf16[512,4096]{1,0:T(8,128)(2,1)}, u32[]{:S(2)}, u32[]{:S(2)}) collective-permute-start(bf16[512,4096]{1,0:T(8,128)(2,1)} %shard_map.137.refs_0_), channel_id=1, source_target_pairs={{0,2},{2,0},{4,6},{6,4},{8,10},{10,8},{12,14},{14,12},{16,18},{18,... | collective-permute-start | bytes 12582920 | tf_op jit(solution)/shard_map/ppermute | solution.py:32
  194.0 36.4 %collective-permute-start.18 = (bf16[256,2048]{1,0:T(8,128)(2,1)}, bf16[256,2048]{1,0:T(8,128)(2,1)S(1)}, u32[]{:S(2)}, u32[]{:S(2)}) collective-permute-start(bf16[256,2048]{1,0:T(8,128)(2,1)} %collective-permute-done.12.part), channel_id=1, source_target_pairs={{0,1},{1,0},{2,3},{3,2},{4,5},{5,4},{6,7},{7,6},{8,9},{9,8},{10,11... | collective-permute-start | bytes 3145736 | tf_op jit(solution)/shard_map/ppermute | solution.py:36
  195.6 33.4 %collective-permute-start.15 = (bf16[256,1408]{1,0:T(8,128)(2,1)S(1)}, bf16[256,1408]{1,0:T(8,128)(2,1)S(1)}, u32[]{:S(2)}, u32[]{:S(2)}) collective-permute-start(bf16[256,1408]{1,0:T(8,128)(2,1)S(1)} %slice.99), channel_id=1, source_target_pairs={{0,8},{2,10},{4,12},{6,14},{8,0},{10,2},{12,4},{14,6},{16,24},{18,... | collective-permute-start | bytes 2162696 | tf_op jit(solution)/shard_map/ppermute | solution.py:32
  195.7 34.7 %collective-permute-start.16 = (bf16[256,1408]{1,0:T(8,128)(2,1)S(1)}, bf16[256,1408]{1,0:T(8,128)(2,1)S(1)}, u32[]{:S(2)}, u32[]{:S(2)}) collective-permute-start(bf16[256,1408]{1,0:T(8,128)(2,1)S(1)} %slice.100), channel_id=1, source_target_pairs={{0,16},{2,18},{4,20},{6,22},{8,24},{10,26},{12,28},{14,30},{16,0},... | collective-permute-start | bytes 2162696 | tf_op jit(solution)/shard_map/ppermute | solution.py:32
  197.0 33.5 %collective-permute-start.17 = (bf16[256,1408]{1,0:T(8,128)(2,1)}, bf16[256,1408]{1,0:T(8,128)(2,1)S(1)}, u32[]{:S(2)}, u32[]{:S(2)}) collective-permute-start(bf16[256,1408]{1,0:T(8,128)(2,1)} %collective-permute-done.10.refs_0_.refs_4_), channel_id=1, source_target_pairs={{0,4},{2,6},{4,0},{6,2},{8,12},{10,14},{12,8},{14,10},{16,20},{18,... | collective-permute-start | bytes 2162696 | tf_op jit(solution)/shard_map/ppermute | solution.py:32
  236.0 14.4 %collective-permute-start.24 = (bf16[512,4096]{1,0:T(8,128)(2,1)}, bf16[512,4096]{1,0:T(8,128)(2,1)S(1)}, u32[]{:S(2)}, u32[]{:S(2)}) collective-permute-start(bf16[512,4096]{1,0:T(8,128)(2,1)} %shard_map.139.refs_0_), channel_id=1, source_target_pairs={{0,2},{2,0},{4,6},{6,4},{8,10},{10,8},{12,14},{14,12},{16,18},{18,... | collective-permute-start | bytes 12582920 | tf_op jit(solution)/shard_map/ppermute | solution.py:32
  237.3 25.6 %collective-permute-start.20 = (bf16[256,1408]{1,0:T(8,128)(2,1)}, bf16[256,1408]{1,0:T(8,128)(2,1)S(1)}, u32[]{:S(2)}, u32[]{:S(2)}) collective-permute-start(bf16[256,1408]{1,0:T(8,128)(2,1)} %get-tuple-element.517), channel_id=1, source_target_pairs={{0,8},{2,10},{4,12},{6,14},{8,0},{10,2},{12,4},{14,6},{16,24},{18,... | collective-permute-start | bytes 2162696 | tf_op jit(solution)/shard_map/ppermute | solution.py:32
  237.5 34.7 %collective-permute-start.21 = (bf16[256,1408]{1,0:T(8,128)(2,1)}, bf16[256,1408]{1,0:T(8,128)(2,1)S(1)}, u32[]{:S(2)}, u32[]{:S(2)}) collective-permute-start(bf16[256,1408]{1,0:T(8,128)(2,1)} %get-tuple-element.516), channel_id=1, source_target_pairs={{0,24},{2,26},{4,28},{6,30},{8,16},{10,18},{12,20},{14,22},{16,8},... | collective-permute-start | bytes 2162696 | tf_op jit(solution)/shard_map/ppermute | solution.py:32
  239.7 32.6 %collective-permute-start.22 = (bf16[256,1408]{1,0:T(8,128)(2,1)S(1)}, bf16[256,1408]{1,0:T(8,128)(2,1)S(1)}, u32[]{:S(2)}, u32[]{:S(2)}) collective-permute-start(bf16[256,1408]{1,0:T(8,128)(2,1)S(1)} %collective-permute-done.15.refs_2_.refs_0_), channel_id=1, source_target_pairs={{0,4},{2,6},{4,0},{6,2},{8,12},{10,14},{12,8},{14,10},{16,20},{18,... | collective-permute-start | bytes 2162696 | tf_op jit(solution)/shard_map/ppermute | solution.py:32
  241.2 32.3 %collective-permute-start.23 = (bf16[256,1408]{1,0:T(8,128)(2,1)S(1)}, bf16[256,1408]{1,0:T(8,128)(2,1)}, u32[]{:S(2)}, u32[]{:S(2)}) collective-permute-start(bf16[256,1408]{1,0:T(8,128)(2,1)S(1)} %collective-permute-done.16.refs_2_.refs_6_), channel_id=1, source_target_pairs={{0,4},{2,6},{4,0},{6,2},{8,12},{10,14},{12,8},{14,10},{16,20},{18,... | collective-permute-start | bytes 2162696 | tf_op jit(solution)/shard_map/ppermute | solution.py:32
  273.5 3.5 collective-permute-start.28
  273.5 39.8 %collective-permute-start.25 = (bf16[256,1408]{1,0:T(8,128)(2,1)}, bf16[256,1408]{1,0:T(8,128)(2,1)S(1)}, u32[]{:S(2)}, u32[]{:S(2)}) collective-permute-start(bf16[256,1408]{1,0:T(8,128)(2,1)} %get-tuple-element.517), channel_id=1, source_target_pairs={{0,24},{2,26},{4,28},{6,30},{8,16},{10,18},{12,20},{14,22},{16,8},... | collective-permute-start | bytes 2162696 | tf_op jit(solution)/shard_map/ppermute | solution.py:32
  275.0 38.3 %collective-permute-start.26 = (bf16[256,1408]{1,0:T(8,128)(2,1)S(1)}, bf16[256,1408]{1,0:T(8,128)(2,1)S(1)}, u32[]{:S(2)}, u32[]{:S(2)}) collective-permute-start(bf16[256,1408]{1,0:T(8,128)(2,1)S(1)} %collective-permute-done.20.refs_2_), channel_id=1, source_target_pairs={{0,4},{2,6},{4,0},{6,2},{8,12},{10,14},{12,8},{14,10},{16,20},{18,... | collective-permute-start | bytes 2162696 | tf_op jit(solution)/shard_map/ppermute | solution.py:32
  276.5 36.8 %collective-permute-start.27 = (bf16[256,1408]{1,0:T(8,128)(2,1)S(1)}, bf16[256,1408]{1,0:T(8,128)(2,1)S(1)}, u32[]{:S(2)}, u32[]{:S(2)}) collective-permute-start(bf16[256,1408]{1,0:T(8,128)(2,1)S(1)} %collective-permute-done.21.refs_4_.refs_0_), channel_id=1, source_target_pairs={{0,4},{2,6},{4,0},{6,2},{8,12},{10,14},{12,8},{14,10},{16,20},{18,... | collective-permute-start | bytes 2162696 | tf_op jit(solution)/shard_map/ppermute | solution.py:32
  279.2 34.2 %collective-permute-start.29 = (bf16[256,1024]{1,0:T(8,128)(2,1)S(1)}, bf16[256,1024]{1,0:T(8,128)(2,1)S(1)}, u32[]{:S(2)}, u32[]{:S(2)}) collective-permute-start(bf16[256,1024]{1,0:T(8,128)(2,1)S(1)} %slice.165), channel_id=1, source_target_pairs={{0,8},{2,10},{4,12},{6,14},{8,0},{10,2},{12,4},{14,6},{16,24},{18,... | collective-permute-start | bytes 1572872 | tf_op jit(solution)/shard_map/ppermute | solution.py:32
  313.4 2.7 collective-permute-start.31
  313.5 25.2 %collective-permute-start.30 = (bf16[256,1408]{1,0:T(8,128)(2,1)S(1)}, bf16[256,1408]{1,0:T(8,128)(2,1)S(1)}, u32[]{:S(2)}, u32[]{:S(2)}) collective-permute-start(bf16[256,1408]{1,0:T(8,128)(2,1)S(1)} %collective-permute-done.25.refs_2_), channel_id=1, source_target_pairs={{0,4},{2,6},{4,0},{6,2},{8,12},{10,14},{12,8},{14,10},{16,20},{18,... | collective-permute-start | bytes 2162696 | tf_op jit(solution)/shard_map/ppermute | solution.py:32
  316.6 22.1 %collective-permute-start.32 = (bf16[256,1024]{1,0:T(8,128)(2,1)S(1)}, bf16[256,1024]{1,0:T(8,128)(2,1)S(1)}, u32[]{:S(2)}, u32[]{:S(2)}) collective-permute-start(bf16[256,1024]{1,0:T(8,128)(2,1)S(1)} %slice.164), channel_id=1, source_target_pairs={{0,8},{2,10},{4,12},{6,14},{8,0},{10,2},{12,4},{14,6},{16,24},{18,... | collective-permute-start | bytes 1572872 | tf_op jit(solution)/shard_map/ppermute | solution.py:32
  338.7 2.7 collective-permute-start.33
  341.9 14.0 %collective-permute-start.34 = (bf16[256,1024]{1,0:T(8,128)(2,1)S(1)}, bf16[256,1024]{1,0:T(8,128)(2,1)S(1)}, u32[]{:S(2)}, u32[]{:S(2)}) collective-permute-start(bf16[256,1024]{1,0:T(8,128)(2,1)S(1)} %slice.163), channel_id=1, source_target_pairs={{0,8},{2,10},{4,12},{6,14},{8,0},{10,2},{12,4},{14,6},{16,24},{18,... | collective-permute-start | bytes 1572872 | tf_op jit(solution)/shard_map/ppermute | solution.py:32
  342.6 12.4 %collective-permute-start.35 = (f32[32,2048]{1,0:T(8,128)S(1)}, f32[32,2048]{1,0:T(8,128)S(1)}, u32[]{:S(2)}, u32[]{:S(2)}) collective-permute-start(f32[32,2048]{1,0:T(8,128)S(1)} %copy-done.59), channel_id=1, source_target_pairs={{0,4},{2,6},{4,0},{6,2},{8,12},{10,14},{12,8},{14,10},{16,20},{18,... | collective-permute-start | bytes 786440 | tf_op jit(solution)/shard_map/ppermute | solution.py:32
  360.2 2.7 collective-permute-start.36
  360.4 16.2 %collective-permute-start.37 = (bf16[256,1024]{1,0:T(8,128)(2,1)S(1)}, bf16[256,1024]{1,0:T(8,128)(2,1)S(1)}, u32[]{:S(2)}, u32[]{:S(2)}) collective-permute-start(bf16[256,1024]{1,0:T(8,128)(2,1)S(1)} %add_convert_fusion.7.refs_0_), channel_id=1, source_target_pairs={{1,0},{3,2},{5,4},{7,6},{9,8},{11,10},{13,12},{15,14},{16,17},{18,... | collective-permute-start | bytes 1572872 | tf_op jit(solution)/shard_map/ppermute | solution.py:695
  379.5 18.5 %collective-permute-start.38 = (bf16[512,1024]{1,0:T(8,128)(2,1)}, bf16[512,1024]{1,0:T(8,128)(2,1)}, u32[]{:S(2)}, u32[]{:S(2)}) collective-permute-start(bf16[512,1024]{1,0:T(8,128)(2,1)} %convolution_convert_fusion.2), channel_id=1, source_target_pairs={{0,2},{2,0},{4,6},{6,4},{8,10},{10,8},{12,14},{14,12},{16,18},{18,... | collective-permute-start | bytes 3145736 | tf_op jit(solution)/shard_map/ppermute | solution.py:32
  388.2 23.0 %collective-permute-start.50 = (bf16[512,1024]{1,0:T(8,128)(2,1)}, bf16[512,1024]{1,0:T(8,128)(2,1)S(1)}, u32[]{:S(2)}, u32[]{:S(2)}) collective-permute-start(bf16[512,1024]{1,0:T(8,128)(2,1)} %get-tuple-element.443), channel_id=1, source_target_pairs={{0,2},{2,0},{4,6},{6,4},{8,10},{10,8},{12,14},{14,12},{16,18},{18,... | collective-permute-start | bytes 3145736 | tf_op jit(solution)/shard_map/ppermute | solution.py:32
  388.8 9.2 %collective-permute-start.41 = (f32[32,2048]{1,0:T(8,128)S(1)}, f32[32,2048]{1,0:T(8,128)S(1)}, u32[]{:S(2)}, u32[]{:S(2)}) collective-permute-start(f32[32,2048]{1,0:T(8,128)S(1)} %add.98), channel_id=1, source_target_pairs={{0,8},{2,10},{4,12},{6,14},{8,0},{10,2},{12,4},{14,6},{16,24},{18,... | collective-permute-start | bytes 786440 | tf_op jit(solution)/shard_map/ppermute | solution.py:32
  390.3 18.1 %collective-permute-start.39 = (bf16[256,1024]{1,0:T(8,128)(2,1)}, bf16[256,1024]{1,0:T(8,128)(2,1)S(1)}, u32[]{:S(2)}, u32[]{:S(2)}) collective-permute-start(bf16[256,1024]{1,0:T(8,128)(2,1)} %slice.162), channel_id=1, source_target_pairs={{0,8},{2,10},{4,12},{6,14},{8,0},{10,2},{12,4},{14,6},{16,24},{18,... | collective-permute-start | bytes 1572872 | tf_op jit(solution)/shard_map/ppermute | solution.py:32
  390.8 17.5 %collective-permute-start.40 = (bf16[256,1024]{1,0:T(8,128)(2,1)S(1)}, bf16[256,1024]{1,0:T(8,128)(2,1)S(1)}, u32[]{:S(2)}, u32[]{:S(2)}) collective-permute-start(bf16[256,1024]{1,0:T(8,128)(2,1)S(1)} %add_convert_fusion.6.refs_1_), channel_id=1, source_target_pairs={{1,0},{3,2},{5,4},{7,6},{9,8},{11,10},{13,12},{15,14},{16,17},{18,... | collective-permute-start | bytes 1572872 | tf_op jit(solution)/shard_map/ppermute | solution.py:695
  411.2 17.7 %collective-permute-start.42 = (bf16[512,1024]{1,0:T(8,128)(2,1)}, bf16[512,1024]{1,0:T(8,128)(2,1)}, u32[]{:S(2)}, u32[]{:S(2)}) collective-permute-start(bf16[512,1024]{1,0:T(8,128)(2,1)} %convolution_convert_fusion.1), channel_id=1, source_target_pairs={{0,2},{2,0},{4,6},{6,4},{8,10},{10,8},{12,14},{14,12},{16,18},{18,... | collective-permute-start | bytes 3145736 | tf_op jit(solution)/shard_map/ppermute | solution.py:32
  412.5 15.4 %collective-permute-start.46 = (f32[32,2048]{1,0:T(8,128)S(1)}, f32[32,2048]{1,0:T(8,128)}, u32[]{:S(2)}, u32[]{:S(2)}) collective-permute-start(f32[32,2048]{1,0:T(8,128)S(1)} %add.103), channel_id=1, source_target_pairs={{0,16},{2,18},{4,20},{6,22},{8,24},{10,26},{12,28},{14,30},{16,0},... | collective-permute-start | bytes 786440 | tf_op jit(solution)/shard_map/ppermute | solution.py:32
  413.7 5.5 %collective-permute-start.45 = (f32[512,1]{1,0:T(8,128)}, f32[512,1]{1,0:T(8,128)}, u32[]{:S(2)}, u32[]{:S(2)}) collective-permute-start(f32[512,1]{1,0:T(8,128)} %copy.15), channel_id=1, source_target_pairs={{0,2},{2,0},{4,6},{6,4},{8,10},{10,8},{12,14},{14,12},{16,18},{18,... | collective-permute-start | bytes 6152 | tf_op jit(solution)/shard_map/ppermute | solution.py:32
  416.1 17.4 %collective-permute-start.44 = (bf16[256,1024]{1,0:T(8,128)(2,1)}, bf16[256,1024]{1,0:T(8,128)(2,1)S(1)}, u32[]{:S(2)}, u32[]{:S(2)}) collective-permute-start(bf16[256,1024]{1,0:T(8,128)(2,1)} %add_convert_fusion.5.refs_1_), channel_id=1, source_target_pairs={{0,1},{1,0},{2,3},{3,2},{4,5},{5,4},{6,7},{7,6},{8,9},{9,8},{10,11... | collective-permute-start | bytes 1572872 | tf_op jit(solution)/shard_map/ppermute | solution.py:36
  418.6 18.7 %collective-permute-start.43 = (bf16[256,1024]{1,0:T(8,128)(2,1)}, bf16[256,1024]{1,0:T(8,128)(2,1)S(1)}, u32[]{:S(2)}, u32[]{:S(2)}) collective-permute-start(bf16[256,1024]{1,0:T(8,128)(2,1)} %slice.161), channel_id=1, source_target_pairs={{0,8},{2,10},{4,12},{6,14},{8,0},{10,2},{12,4},{14,6},{16,24},{18,... | collective-permute-start | bytes 1572872 | tf_op jit(solution)/shard_map/ppermute | solution.py:32
  437.3 7.4 %collective-permute-start.52 = (f32[32,2048]{1,0:T(8,128)S(1)}, f32[32,2048]{1,0:T(8,128)S(1)}, u32[]{:S(2)}, u32[]{:S(2)}) collective-permute-start(f32[32,2048]{1,0:T(8,128)S(1)} %add.107), channel_id=1, source_target_pairs={{0,4},{2,6},{4,0},{6,2},{8,12},{10,14},{12,8},{14,10},{16,20},{18,... | collective-permute-start | bytes 786440 | tf_op jit(solution)/shard_map/ppermute | solution.py:32
  438.1 5.1 collective-permute-start.51
  440.0 4.9 collective-permute-start.47
  440.3 14.4 %collective-permute-start.49 = (bf16[256,1024]{1,0:T(8,128)(2,1)S(1)}, bf16[256,1024]{1,0:T(8,128)(2,1)S(1)}, u32[]{:S(2)}, u32[]{:S(2)}) collective-permute-start(bf16[256,1024]{1,0:T(8,128)(2,1)S(1)} %add_convert_fusion.4.refs_0_), channel_id=1, source_target_pairs={{0,1},{1,0},{2,3},{3,2},{4,5},{5,4},{6,7},{7,6},{8,9},{9,8},{10,11... | collective-permute-start | bytes 1572872 | tf_op jit(solution)/shard_map/ppermute | solution.py:36
  441.1 14.3 %collective-permute-start.48 = (bf16[256,1024]{1,0:T(8,128)(2,1)S(1)}, bf16[256,1024]{1,0:T(8,128)(2,1)S(1)}, u32[]{:S(2)}, u32[]{:S(2)}) collective-permute-start(bf16[256,1024]{1,0:T(8,128)(2,1)S(1)} %slice.160), channel_id=1, source_target_pairs={{0,8},{2,10},{4,12},{6,14},{8,0},{10,2},{12,4},{14,6},{16,24},{18,... | collective-permute-start | bytes 1572872 | tf_op jit(solution)/shard_map/ppermute | solution.py:32
  444.8 39.8 %collective-permute-start.57 = (f32[64,2048]{1,0:T(8,128)S(1)}, f32[64,2048]{1,0:T(8,128)S(1)}, u32[]{:S(2)}, u32[]{:S(2)}) collective-permute-start(f32[64,2048]{1,0:T(8,128)S(1)} %pad_maximum_fusion), channel_id=1, source_target_pairs={{0,2},{2,0},{4,6},{6,4},{8,10},{10,8},{12,14},{14,12},{16,18},{18,... | collective-permute-start | bytes 1572872 | tf_op jit(solution)/shard_map/ppermute | solution.py:32
  455.6 44.1 %slice-start = ((f32[512,1024]{1,0:T(8,128)}), f32[256,1024]{1,0:T(8,128)S(1)}, s32[]{:S(2)}) async-start(f32[512,1024]{1,0:T(8,128)} %copy-done.6), calls=%async_computation | async-start | bytes 2097152 | tf_op jit(solution)/shard_map/slice | solution.py:640
  455.6 29.0 %collective-permute-start.55 = (bf16[256,1024]{1,0:T(8,128)(2,1)S(1)}, bf16[256,1024]{1,0:T(8,128)(2,1)S(1)}, u32[]{:S(2)}, u32[]{:S(2)}) collective-permute-start(bf16[256,1024]{1,0:T(8,128)(2,1)S(1)} %add_convert_fusion.2.refs_3_), channel_id=1, source_target_pairs={{0,1},{2,3},{4,5},{6,7},{8,9},{10,11},{12,13},{14,15},{17,16},{19,... | collective-permute-start | bytes 1572872 | tf_op jit(solution)/shard_map/ppermute | solution.py:695
  459.1 25.5 %collective-permute-start.54 = (bf16[256,1024]{1,0:T(8,128)(2,1)S(1)}, bf16[256,1024]{1,0:T(8,128)(2,1)S(1)}, u32[]{:S(2)}, u32[]{:S(2)}) collective-permute-start(bf16[256,1024]{1,0:T(8,128)(2,1)S(1)} %add_convert_fusion.3.refs_3_), channel_id=1, source_target_pairs={{0,1},{1,0},{2,3},{3,2},{4,5},{5,4},{6,7},{7,6},{8,9},{9,8},{10,11... | collective-permute-start | bytes 1572872 | tf_op jit(solution)/shard_map/ppermute | solution.py:36
  459.2 25.4 %collective-permute-start.53 = (bf16[256,1024]{1,0:T(8,128)(2,1)S(1)}, bf16[256,1024]{1,0:T(8,128)(2,1)S(1)}, u32[]{:S(2)}, u32[]{:S(2)}) collective-permute-start(bf16[256,1024]{1,0:T(8,128)(2,1)S(1)} %slice.159), channel_id=1, source_target_pairs={{0,8},{2,10},{4,12},{6,14},{8,0},{10,2},{12,4},{14,6},{16,24},{18,... | collective-permute-start | bytes 1572872 | tf_op jit(solution)/shard_map/ppermute | solution.py:32
  461.0 22.9 %collective-permute-start.56 = (f32[256,1]{1,0:T(8,128)S(1)}, f32[256,1]{1,0:T(8,128)S(1)}, u32[]{:S(2)}, u32[]{:S(2)}) collective-permute-start(f32[256,1]{1,0:T(8,128)S(1)} %slice_add_fusion), channel_id=1, source_target_pairs={{0,1},{1,0},{2,3},{3,2},{4,5},{5,4},{6,7},{7,6},{8,9},{9,8},{10,11... | collective-permute-start | bytes 3080 | tf_op jit(solution)/shard_map/ppermute | solution.py:36
  484.8 13.4 %collective-permute-start.58 = (bf16[256,1024]{1,0:T(8,128)(2,1)S(1)}, bf16[256,1024]{1,0:T(8,128)(2,1)S(1)}, u32[]{:S(2)}, u32[]{:S(2)}) collective-permute-start(bf16[256,1024]{1,0:T(8,128)(2,1)S(1)} %add_convert_fusion.1.refs_2_), channel_id=1, source_target_pairs={{0,1},{1,0},{2,3},{3,2},{4,5},{5,4},{6,7},{7,6},{8,9},{9,8},{10,11... | collective-permute-start | bytes 1572872 | tf_op jit(solution)/shard_map/ppermute | solution.py:36
  487.4 12.3 %collective-permute-start.59 = (bf16[256,1024]{1,0:T(8,128)(2,1)S(1)}, bf16[256,1024]{1,0:T(8,128)(2,1)S(1)}, u32[]{:S(2)}, u32[]{:S(2)}) collective-permute-start(bf16[256,1024]{1,0:T(8,128)(2,1)S(1)} %copy-done.45), channel_id=1, source_target_pairs={{0,8},{2,10},{4,12},{6,14},{8,0},{10,2},{12,4},{14,6},{16,24},{18,... | collective-permute-start | bytes 1572872 | tf_op jit(solution)/shard_map/ppermute | solution.py:32
  499.9 11.5 %collective-permute-start.60 = (bf16[256,1024]{1,0:T(8,128)(2,1)S(1)}, bf16[256,1024]{1,0:T(8,128)(2,1)S(1)}, u32[]{:S(2)}, u32[]{:S(2)}) collective-permute-start(bf16[256,1024]{1,0:T(8,128)(2,1)S(1)} %add_convert_fusion.refs_2_), channel_id=1, source_target_pairs={{0,1},{2,3},{4,5},{6,7},{8,9},{10,11},{12,13},{14,15},{17,16},{19,... | collective-permute-start | bytes 1572872 | tf_op jit(solution)/shard_map/ppermute | solution.py:695
  (69 other events, 680.7 us)

commit v3 on v2

v3 whole, which is shorter than its diff:
```python
import functools
import math

import jax
import jax.numpy as jnp
from jax import lax
from jax.experimental import pallas as pl
from jax.experimental.pallas import tpu as pltpu
from jax.sharding import PartitionSpec as P

coupling = 0.5
SMEM = pl.BlockSpec(memory_space=pltpu.SMEM)
FREE = pl.CostEstimate(flops=0, bytes_accessed=0, transcendentals=0)
MIB = 1024 * 1024


def silu_slope(argument):
    sigmoid_value = jax.nn.sigmoid(argument)
    return sigmoid_value * (1.0 + argument * (1.0 - sigmoid_value))


def after(value, *earlier):
    return lax.optimization_barrier((value, *earlier))[0]


def together(*values):
    return lax.optimization_barrier(values)


def hop(value, bits):
    size = lax.axis_size("dp")
    return lax.ppermute(value, "dp", [(i, i ^ bits) for i in range(size)])


def swap_mp(value):
    return lax.ppermute(value, "mp", [(0, 1), (1, 0)])


def place_of(block, me):
    relative = block ^ (me & ~1)
    return (relative & ~3) | ((relative & 1) << 1) | ((relative >> 1) & 1)


def block_at(place, me):
    return ((place & ~3) | ((place & 1) << 1) | ((place >> 1) & 1)) ^ (me & ~1)


def dot(left, right):
    return jnp.dot(left, right, preferred_element_type=jnp.float32)


def dot_t(left, right):
    return lax.dot_general(
        left, right, (((1,), (1,)), ((), ())), preferred_element_type=jnp.float32
    )


def call(body, cost=FREE, room=24, **settings):
    params = pltpu.CompilerParams(vmem_limit_bytes=room * MIB)
    return pl.pallas_call(body, compiler_params=params, cost_estimate=cost, **settings)


def head_body(blocks, groups, at, uf, us, gf, gs, gain, down_t, up, *outs):
    (squashed_o, apg_o, inverse_o, lower_o, lower_share, input_share) = outs[:6]
    normed_own, carried_own, first_send, second_send = outs[6:]
    me, rank = at[0], at[1]
    width = uf.shape[1]
    column = width // blocks
    share = width // groups
    pre = dot_t(uf[...], down_t[...])
    squashed = (pre * jax.nn.sigmoid(pre)).astype(jnp.bfloat16)
    squashed_o[...] = squashed
    lower = (us[...].astype(jnp.float32) - dot(squashed, up[...])).astype(jnp.bfloat16)
    lower_o[...] = lower
    value = lower.astype(jnp.float32)
    inverse = lax.rsqrt(jnp.mean(value * value, axis=1, keepdims=True) + 1e-05)
    inverse_o[...] = jnp.broadcast_to(inverse, inverse_o.shape)
    normed = (value * inverse * gain[...].astype(jnp.float32)).astype(jnp.bfloat16)
    apg = (dot_t(gs[...], up[...]) * silu_slope(pre)).astype(jnp.bfloat16)
    apg_o[...] = apg
    carried = (gf[...].astype(jnp.float32) + dot(apg, down_t[...])).astype(jnp.bfloat16)
    for group in range(groups):

        @pl.when(rank == group)
        def _():
            part = slice(group * share, (group + 1) * share)
            lower_share[...] = lower[:, part]
            input_share[...] = (coupling * carried[:, part].astype(jnp.float32)).astype(
                jnp.bfloat16
            )

    for block in range(blocks):
        part = slice(block * column, (block + 1) * column)
        own = pl.multiple_of(place_of(block, me) * column, column)
        normed_own[:, pl.ds(own, column)] = normed[:, part]
        carried_own[:, pl.ds(own, column)] = carried[:, part]
        place = place_of(block, me ^ 4) * column - rank * share

        @pl.when((place >= 0) & (place < share))
        def _():
            first_send[:, pl.ds(pl.multiple_of(place, column), column)] = normed[:, part]

        @pl.when((place >= 0) & (place < share // 2))
        def _():
            to = pl.multiple_of(share + place, column)
            first_send[:, pl.ds(to, column)] = carried[:, part]

        @pl.when((place >= share // 2) & (place < share))
        def _():
            to = pl.multiple_of(place - share // 2, column)
            second_send[:, pl.ds(to, column)] = carried[:, part]


def head(at, blocks, groups, uf, us, gf, gs, gain, down_t, up):
    tokens, width = uf.shape
    rank = up.shape[0]
    share = width // groups
    step = 64 if tokens % 64 == 0 else tokens
    row = lambda columns: pl.BlockSpec((step, columns), lambda i: (i, 0))
    whole = lambda a: pl.BlockSpec(a.shape, lambda i: (0, 0))
    outs = [rank, rank, 128, width, share, share, width, width, share + share // 2, share // 2]
    types = [jnp.bfloat16, jnp.bfloat16, jnp.float32] + [jnp.bfloat16] * 7
    return call(
        functools.partial(head_body, blocks, groups),
        grid=(tokens // step,),
        in_specs=[SMEM] + [row(width)] * 4 + [whole(gain), whole(down_t), whole(up)],
        out_specs=[row(c) for c in outs],
        out_shape=[jax.ShapeDtypeStruct((tokens, c), t) for c, t in zip(outs, types)],
    )(at, uf, us, gf, gs, gain, down_t, up)


def both_body(at, own, part, other, out):
    tokens, share = part.shape
    out[:tokens] = own[...]
    for group in range(2):
        place = group * share

        @pl.when(at[1] == group)
        def _():
            out[tokens:, place : place + share] = part[...]
            out[tokens:, share - place : 2 * share - place] = other[...]


def both_tokens(at, own, part, other):
    tokens, width = own.shape
    return call(
        both_body,
        in_specs=[SMEM] + [pl.BlockSpec(memory_space=pltpu.VMEM)] * 3,
        out_specs=pl.BlockSpec(memory_space=pltpu.VMEM),
        out_shape=jax.ShapeDtypeStruct((2 * tokens, width), own.dtype),
    )(at, own, part, other)


def stack(*units):
    columns, dtype = units[0][0].shape[1], units[0][0].dtype
    arrays = []
    for array, _, _ in units:
        if not any(array is a for a in arrays):
            arrays.append(array)
    which = [next(k for k, a in enumerate(arrays) if a is u[0]) for u in units]
    total = sum(u[2] for u in units)

    def body(*refs):
        out, held, got, put = refs[-4:]
        reads, writes, at = [], [], 0
        for i, (_, first, rows) in enumerate(units):
            here = held.at[pl.ds(at, rows)]
            reads.append(
                pltpu.make_async_copy(refs[which[i]].at[pl.ds(first, rows)], here, got.at[i])
            )
            writes.append(pltpu.make_async_copy(here, out.at[pl.ds(at, rows)], put.at[i]))
            at += rows
        for read in reads:
            read.start()
        for read, write in zip(reads, writes):
            read.wait()
            write.start()
        for write in writes:
            write.wait()

    anywhere = pl.BlockSpec(memory_space=pl.ANY)
    return call(
        body,
        in_specs=[anywhere] * len(arrays),
        out_specs=anywhere,
        out_shape=jax.ShapeDtypeStruct((total, columns), dtype),
        scratch_shapes=[
            pltpu.VMEM((total, columns), dtype),
            pltpu.SemaphoreType.DMA((len(units),)),
            pltpu.SemaphoreType.DMA((len(units),)),
        ],
    )(*arrays)


ANY = pl.BlockSpec(memory_space=pl.ANY)


def fetch(units, refs, held, sems):
    copies, at = [], 0
    for i, (_, first, rows) in enumerate(units):
        copies.append(
            pltpu.make_async_copy(
                refs[i].at[pl.ds(first, rows)], held.at[pl.ds(at, rows)], sems.at[i]
            )
        )
        at += rows
    for copy in copies:
        copy.start()
    for copy in copies:
        copy.wait()


def held_scratch(units):
    array = units[0][0]
    return [
        pltpu.VMEM((sum(u[2] for u in units), array.shape[1]), array.dtype),
        pltpu.SemaphoreType.DMA((len(units),)),
    ]


def token_specs(count, width, step, at):
    half = count // step
    return [
        pl.BlockSpec((step, width), lambda i: (jnp.minimum(i, half - 1), at)),
        pl.BlockSpec((step, width), lambda i: (jnp.maximum(i - half, 0), at)),
    ]


def hidden_body(units, *refs):
    count = len(units)
    at, tokens, refs = refs[0], refs[1:7], refs[7:]
    hidden, slope, activated, held, sems = refs[count:]
    step = pl.program_id(0)

    @pl.when(step == 0)
    def _():
        fetch(units, refs, held, sems)

    def use(total):
        hidden[...] = total
        sigmoid_value = jax.nn.sigmoid(total)
        slope[...] = sigmoid_value * (1.0 + total * (1.0 - sigmoid_value))
        activated[...] = (total * sigmoid_value).astype(jnp.bfloat16)

    share = tokens[1].shape[1]
    for core in range(2):
        own, part, other = tokens[3 * core : 3 * core + 3]

        @pl.when(step == 2 * core)
        def _():
            use(dot(own[...], held[...]))

        for rank in range(2):

            @pl.when((step == 2 * core + 1) & (at[1] == rank))
            def _():
                first, second = (part, other) if rank == 0 else (other, part)
                use(dot(first[...], held[:share]) + dot(second[...], held[share:]))


def hidden_kernel(at, tokens, units):
    count = tokens[0].shape[0]
    columns = units[0][0].shape[1]
    out = pl.BlockSpec((count, columns), lambda i: (i, 0))
    return call(
        functools.partial(hidden_body, units),
        cost=work(8 * count * columns * tokens[0].shape[1]),
        room=56,
        grid=(4,),
        in_specs=[SMEM]
        + [pl.BlockSpec(t.shape, lambda i: (0, 0)) for t in tokens]
        + [ANY] * len(units),
        out_specs=[out] * 3,
        out_shape=[
            jax.ShapeDtypeStruct((4 * count, columns), t)
            for t in (jnp.float32, jnp.float32, jnp.bfloat16)
        ],
        scratch_shapes=held_scratch(units),
    )(at, *tokens, *[u[0] for u in units])


def act_body(units, places, depth, extras, slope_given, *refs):
    count = len(units)
    tokens, refs = refs[: 2 * places], refs[2 * places :]
    outs, (held, sems) = refs[count + extras : -2], refs[-2:]
    step = pl.program_id(0)

    @pl.when(step == 0)
    def _():
        fetch(units, refs, held, sems)

    cases = [(step == 0, 0), (step == 1, 0), (step >= 2, 1)]
    if not slope_given:
        cases = [(step < 2, 0), (step >= 2, 1)]
    for case, (chosen, which) in enumerate(cases):
        out = outs[case if slope_given else 0]

        @pl.when(chosen)
        def _():
            left = jnp.concatenate([t[...] for t in tokens[which::2]], axis=1)
            total = dot(left, held[...])
            if extras > slope_given:
                total = total + refs[count][...]
            if slope_given:
                total = total * refs[count + extras - 1][...]
            out[...] = total.astype(out.dtype)


def act_kernel(tokens, spans, partial, slope=None):
    count, width = tokens[0].shape
    units = [u for _, us in spans for u in us]
    depth = 2 * units[0][2]
    places = [
        first // depth + i for first, us in spans for i in range(sum(u[2] for u in us) // depth)
    ]
    columns = units[0][0].shape[1]
    step = count // 2
    out = pl.BlockSpec((step, columns), lambda i: (i, 0))
    extra = [a for a in (partial, slope) if a is not None]
    if slope is None:
        out_specs, out_shape = out, jax.ShapeDtypeStruct((2 * count, columns), jnp.float32)
    else:
        own = pl.BlockSpec((step, columns), lambda i: (0, 0))
        out_specs = [own, own, token_specs(count, columns, step, 0)[1]]
        out_shape = [
            jax.ShapeDtypeStruct((r, columns), jnp.bfloat16) for r in (step, step, count)
        ]
    return call(
        functools.partial(
            act_body, units, len(places), depth, len(extra), int(slope is not None)
        ),
        cost=work(4 * count * columns * depth * len(places)),
        room=36,
        grid=(4,),
        in_specs=sum([token_specs(count, depth, step, p) for p in places], [])
        + [ANY] * len(units)
        + [out] * len(extra),
        out_specs=out_specs,
        out_shape=out_shape,
        scratch_shapes=held_scratch(units),
    )(*[t for _ in places for t in tokens], *[u[0] for u in units], *extra)


def work(flops):
    return pl.CostEstimate(flops=flops // 4, bytes_accessed=0, transcendentals=0)


def parity_body(rows, quarter, eighth, at, weight, got, *refs):
    outs, (held, reads_done, writes_done) = refs[:2], refs[2:]
    core = at[0] & 1
    parity = (at[0] >> 2) & 1
    reads, writes = [], []
    for i in range(2):
        group = parity if i == 0 else 1 - parity
        for j, (source, base) in enumerate(((weight, core * quarter), (got, 0))):
            first = pl.multiple_of((core if j == 0 else 1 - core) * rows, rows)
            from_column = pl.multiple_of(base + group * eighth, 128)
            reads.append(
                pltpu.make_async_copy(
                    source.at[:, pl.ds(from_column, eighth)],
                    held.at[i, pl.ds(first, rows)],
                    reads_done.at[2 * i + j],
                )
            )
        writes.append(pltpu.make_async_copy(held.at[i], outs[i], writes_done.at[i]))
    for read in reads:
        read.start()
    for i in range(2):
        reads[2 * i].wait()
        reads[2 * i + 1].wait()
        writes[i].start()
    for write in writes:
        write.wait()


def parity_kernel(at, weight, got):
    rows, quarter = got.shape
    eighth = quarter // 2
    out = jax.ShapeDtypeStruct((2 * rows, eighth), weight.dtype)
    return call(
        functools.partial(parity_body, rows, quarter, eighth),
        in_specs=[SMEM, ANY, ANY],
        out_specs=[ANY, ANY],
        out_shape=[out, out],
        scratch_shapes=[
            pltpu.VMEM((2, 2 * rows, eighth), weight.dtype),
            pltpu.SemaphoreType.DMA((4,)),
            pltpu.SemaphoreType.DMA((2,)),
        ],
    )(at, weight, got)


def core_add_body(mine, got, own, partner):
    tokens = own.shape[0]
    total = mine[...] + got[...].astype(jnp.float32)
    own[...] = total[:tokens]
    partner[...] = total[tokens:].astype(jnp.bfloat16)


def core_add(mine, got):
    count, columns = mine.shape
    vmem = pl.BlockSpec(memory_space=pltpu.VMEM)
    return call(
        core_add_body,
        in_specs=[vmem, vmem],
        out_specs=[vmem, vmem],
        out_shape=[
            jax.ShapeDtypeStruct((count // 2, columns), jnp.float32),
            jax.ShapeDtypeStruct((count // 2, columns), jnp.bfloat16),
        ],
    )(mine, got)


def whole_add_body(mine, got, got_pair, own, partner):
    tokens = own.shape[0]
    total = mine[...] + got[...].astype(jnp.float32)
    own[...] = (total[:tokens] + got_pair[...].astype(jnp.float32)).astype(own.dtype)
    partner[...] = total[tokens:].astype(jnp.bfloat16)


def whole_add(mine, got, got_pair):
    count, columns = mine.shape
    vmem = pl.BlockSpec(memory_space=pltpu.VMEM)
    return call(
        whole_add_body,
        in_specs=[vmem] * 3,
        out_specs=[vmem, vmem],
        out_shape=[jax.ShapeDtypeStruct((count // 2, columns), jnp.bfloat16)] * 2,
    )(mine, got, got_pair)


def pair_add_body(swapped, own, got, out):
    half = own.shape[1] // 2
    if swapped:
        out[:, :half] = (own[:, :half] + got[:, half:].astype(jnp.float32)).astype(out.dtype)
        out[:, half:] = (own[:, half:] + got[:, :half].astype(jnp.float32)).astype(out.dtype)
    else:
        out[...] = (own[...] + got[...].astype(jnp.float32)).astype(out.dtype)


def pair_add(own, got, swapped=False):
    vmem = pl.BlockSpec(memory_space=pltpu.VMEM)
    return call(
        functools.partial(pair_add_body, swapped),
        in_specs=[vmem, vmem],
        out_specs=vmem,
        out_shape=jax.ShapeDtypeStruct(own.shape, jnp.bfloat16),
    )(own, got)


def out_body(units, left, *refs):
    own, other, held, sems = refs[len(units) :]
    step = pl.program_id(0)

    @pl.when(step == 0)
    def _():
        fetch(units, refs, held, sems)
        own[...] = dot_t(left[...], held[...])

    @pl.when(step == 1)
    def _():
        other[...] = dot_t(left[...], held[...]).astype(jnp.bfloat16)


def out_kernel(left, units):
    count, depth = left.shape
    columns = sum(u[2] for u in units)
    out = pl.BlockSpec((count // 2, columns), lambda i: (0, 0))
    return call(
        functools.partial(out_body, units),
        cost=work(2 * count * columns * depth),
        grid=(2,),
        in_specs=[pl.BlockSpec((count // 2, depth), lambda i: (i, 0))] + [ANY] * len(units),
        out_specs=[out, out],
        out_shape=[
            jax.ShapeDtypeStruct((count // 2, columns), jnp.float32),
            jax.ShapeDtypeStruct((count // 2, columns), jnp.bfloat16),
        ],
        scratch_shapes=held_scratch(units),
    )(left, *[u[0] for u in units])


def final_body(blocks, layers, at, gs, lower, gain, inverse, curvature, *refs):
    mine, got, out = refs[:layers], refs[layers:-1], refs[-1]
    me = at[0]
    width = out.shape[1]
    column = width // blocks
    scale = inverse[...][:, :1]
    drop = scale * scale * curvature[...] / width
    for place in range(blocks):
        layer, inner = divmod(place * column, mine[0].shape[1])
        part = slice(inner, inner + column)
        grad = mine[layer][:, part].astype(jnp.float32) + got[layer][:, part].astype(jnp.float32)
        spot = pl.ds(pl.multiple_of(block_at(place, me) * column, column), column)
        out[:, spot] = (
            gs[:, spot].astype(jnp.float32)
            + scale * gain[:, spot].astype(jnp.float32) * grad
            - lower[:, spot].astype(jnp.float32) * drop
        ).astype(jnp.bfloat16)


def final_kernel(at, blocks, gs, lower, gain, inverse, curvature, mine, got):
    tokens, width = gs.shape
    step = 64 if tokens % 64 == 0 else tokens
    row = lambda a: pl.BlockSpec((step, a.shape[1]), lambda i: (i, 0))
    return call(
        functools.partial(final_body, blocks, len(mine)),
        grid=(tokens // step,),
        in_specs=[SMEM, row(gs), row(lower), pl.BlockSpec(gain.shape, lambda i: (0, 0))]
        + [row(a) for a in [inverse, curvature, *mine, *got]],
        out_specs=row(gs),
        out_shape=jax.ShapeDtypeStruct(gs.shape, jnp.bfloat16),
    )(at, gs, lower, gain, inverse, curvature, *mine, *got)


def restore_body(blocks, layers, at, *refs):
    out = refs[layers]
    column = out.shape[1] // blocks
    for place in range(blocks):
        layer, inner = divmod(place * column, refs[0].shape[1])
        spot = pl.multiple_of(block_at(place, at[0]) * column, column)
        out[:, pl.ds(spot, column)] = refs[layer][:, inner : inner + column]


def restore(at, blocks, arrays):
    vmem = pl.BlockSpec(memory_space=pltpu.VMEM)
    tokens, chunk = arrays[0].shape
    return call(
        functools.partial(restore_body, blocks, len(arrays)),
        in_specs=[SMEM] + [vmem] * len(arrays),
        out_specs=vmem,
        out_shape=jax.ShapeDtypeStruct((tokens, chunk * len(arrays)), arrays[0].dtype),
    )(at, *arrays)


def first_body(blocks, at, upper, *refs):
    sums, got, out = refs[:4], refs[4:8], refs[8]
    me, rank = at[0], at[1]
    share = out.shape[1]
    chunk = share // 2
    column = 2 * share // blocks
    pair = (rank ^ (me >> 3)) & 1
    for which in range(2):

        @pl.when(pair == which)
        def _():
            for place in range(which * blocks // 2, (which + 1) * blocks // 2):
                layer, part = divmod(place * column, chunk)
                if which:
                    half, inner = divmod(part, chunk // 2)
                    layer, part = 2 + half, (layer - 2) * (chunk // 2) + inner
                block = block_at(place, me)
                to = pl.multiple_of(block * column - rank * share, column)
                columns = slice(part, part + column)
                frozen = sums[layer][:, columns].astype(jnp.float32) + got[layer][
                    :, columns
                ].astype(jnp.float32)
                out[:, pl.ds(to, column)] = (
                    (upper[:, pl.ds(to, column)].astype(jnp.float32) - frozen) / coupling
                ).astype(jnp.bfloat16)


def first_kernel(at, blocks, upper, sums, got):
    tokens, share = upper.shape
    step = 64 if tokens % 64 == 0 else tokens
    row = lambda columns: pl.BlockSpec((step, columns), lambda i: (i, 0))
    return call(
        functools.partial(first_body, blocks),
        grid=(tokens // step,),
        in_specs=[SMEM, row(share)] + [row(a.shape[1]) for a in [*sums, *got]],
        out_specs=row(share),
        out_shape=jax.ShapeDtypeStruct((tokens, share), jnp.bfloat16),
    )(at, upper, *sums, *got)


def on_device(
    upper_first,
    upper_second,
    grad_first,
    grad_second,
    norm_gain,
    up_weight,
    down_weight,
    adapter_down,
    adapter_up,
):
    size = lax.axis_size("dp")
    groups = lax.axis_size("mp")
    me = lax.axis_index("dp")
    mp_rank = lax.axis_index("mp")
    at = jnp.stack([me, mp_rank]).astype(jnp.int32)
    tokens, model_width = upper_first.shape
    layers = size // 4
    share_width = model_width // groups
    offset = mp_rank * share_width
    grad_scale = 1.0 / math.sqrt(tokens * size)
    parity = (me >> 2) & 1
    quarter = up_weight.shape[1] // 2
    gain = norm_gain.reshape(1, model_width)
    paired = groups == 2 and layers == 4

    rows = up_weight.shape[0]
    chunk = 4 * rows
    far = range(3, layers)
    eighth = quarter // 2
    core = me & 1

    def send_columns(weight):
        return lax.dynamic_slice_in_dim(weight, (1 - core) * quarter, quarter, 1)

    def by_parity(weight, got):
        if eighth % 128 == 0:
            return parity_kernel(at, weight, got)
        own = lax.dynamic_slice_in_dim(weight, core * quarter, quarter, 1)
        first = jnp.where(core == 0, own, got)
        pair = jnp.concatenate([first, jnp.where(core == 0, got, own)], axis=0)
        mine = lax.dynamic_slice_in_dim(pair, parity * eighth, eighth, 1)
        other = lax.dynamic_slice_in_dim(pair, (1 - parity) * eighth, eighth, 1)
        return [mine, other]

    def of_z(pair, s):
        return pair[s & 1]

    def units_of(piece, piece_y):
        return [(a, u * rows, rows) for u in range(2) for a in (piece, piece_y)]

    up_got = hop(send_columns(up_weight), 1)
    up = by_parity(up_weight, up_got)
    up, (down_weight, upper_first, upper_second, grad_first, grad_second, adapter_up) = together(
        up, (down_weight, upper_first, upper_second, grad_first, grad_second, adapter_up)
    )

    uz, uy, dz, dy = [[None] * layers for _ in range(4)]
    uz[0] = up[0]
    uz[2] = hop(up[0], 2 << 2)
    uz[1] = hop(up[1], 1 << 2)
    uy[0] = hop(up[0], 2)
    down = by_parity(down_weight, hop(send_columns(down_weight), 1))
    dz[0] = down[0]
    dy[0] = hop(down[0], 2)
    (
        squashed,
        adapter_pre_grad,
        inverse_rms,
        lower_full,
        lower_second,
        input_grad_first,
        normed_own,
        carried_own,
        first_send,
        second_send,
    ) = head(
        at,
        size,
        groups,
        upper_first,
        upper_second,
        grad_first,
        grad_second,
        gain,
        adapter_down.T,
        adapter_up,
    )
    up, down, uz, uy, dz, dy, normed_own, first_send, second_send, adapter_pre_grad, squashed = (
        together(
            up, down, uz, uy, dz, dy, normed_own, first_send, second_send, adapter_pre_grad,
            squashed,
        )
    )

    for s in far:
        uz[s] = hop(of_z(up, s), s << 2)
    first_part = hop(first_send, 4)
    uy[2] = hop(uz[2], 2)
    uy[1] = hop(uz[1], 2)
    sibling_own = hop(normed_own, 1)
    up_chunks = [stack(*units_of(uz[0], uy[0]))]
    upper_slice = lax.dynamic_slice_in_dim(upper_first, offset, share_width, 1)
    second_slice = lax.dynamic_slice_in_dim(grad_second, offset, share_width, 1)
    down_grad_part = (
        jnp.einsum("tr,td->rd", adapter_pre_grad, upper_slice, preferred_element_type=jnp.float32)
        * grad_scale
    )
    up_grad_part = (
        jnp.einsum("tr,td->rd", squashed, second_slice, preferred_element_type=jnp.float32)
        * grad_scale
    )
    rank = down_grad_part.shape[0]
    is_core, is_y = (me & 1) == 1, (me & 2) == 2
    keep = jnp.where(is_core, up_grad_part, down_grad_part)
    give = jnp.where(is_core, down_grad_part, up_grad_part).astype(jnp.bfloat16)
    normed_part = first_part[:, :share_width]
    uz, uy, normed_part, first_part, sibling_own, up_chunks, down, second_send, keep, give = (
        together(
            uz, uy, normed_part, first_part, sibling_own, up_chunks, down, second_send, keep, give
        )
    )

    low_rows, high_rows = slice(0, rows), slice(rows, 2 * rows)
    dzp = [[None, None] for _ in range(layers)]
    dyp = [[None, None] for _ in range(layers)]
    dzp[2][0] = hop(down[0][low_rows], 2 << 2)
    second_part = hop(second_send, 4)
    carried_part = jnp.concatenate([first_part[:, share_width:], second_part], axis=1)
    for s in far:
        uy[s] = hop(uz[s], 2)
    normed_other = swap_mp(normed_part) if groups == 2 else normed_part
    sibling_part = hop(normed_part, 1) if groups == 2 else normed_part
    up_chunks = up_chunks + [stack(*units_of(uz[s], uy[s])) for s in (1, 2)]
    downs = [[down[0][high_rows]], [down[1][low_rows]], [down[1][high_rows]]]
    (
        dzp, uz, uy, carried_part, normed_part, normed_other, sibling_own, sibling_part, downs,
        normed_own, carried_own, keep, give, up_chunks,
    ) = together(
        dzp, uz, uy, carried_part, normed_part, normed_other, sibling_own, sibling_part, downs,
        normed_own, carried_own, keep, give, up_chunks,
    )
    [mine_high], [other_low], [other_high] = downs

    for s in far:
        dzp[s][0] = hop(other_low if s & 1 else down[0][low_rows], s << 2)
    dzp[1][0] = hop(other_low, 1 << 2)
    dyp[2][0] = hop(dzp[2][0], 2)
    carried_other = swap_mp(carried_part) if groups == 2 else carried_part

    def pair_tokens(own, piece, other):
        if groups == 2:
            return both_tokens(at, own, piece, other)
        return jnp.concatenate([own, lax.all_gather(piece, "mp", axis=1, tiled=True)], axis=0)

    up_units = sum([units_of(uz[s], uy[s]) for s in range(layers)], [])
    if groups == 2:
        here = [normed_own, normed_part, normed_other]
        there = [sibling_own, sibling_part, hop(normed_other, 1)]
        rank_at = at
    else:
        whole = lax.all_gather(normed_part, "mp", axis=1, tiled=True)
        here = [normed_own, whole[:, : model_width // 2], whole[:, model_width // 2 :]]
        there = [hop(t, 1) for t in here]
        rank_at = at * jnp.array([1, 0], jnp.int32)
    hidden_pre, slope, activated = hidden_kernel(rank_at, here + there, up_units)
    (
        dzp, dyp, carried_part, carried_other, hidden_pre, slope, activated, mine_high, other_high,
        dz, dy, keep, give, uz, uy,
    ) = together(
        dzp, dyp, carried_part, carried_other, hidden_pre, slope, activated, mine_high, other_high,
        dz, dy, keep, give, uz, uy,
    )

    dzp[2][1] = hop(mine_high, 2 << 2)
    dzp[1][1] = hop(other_high, 1 << 2)
    for s in far:
        dyp[s][0] = hop(dzp[s][0], 2)
    dyp[1][0] = hop(dzp[1][0], 2)
    keep = keep + hop(give, 1).astype(jnp.float32)
    low, high = keep[: rank // 2], keep[rank // 2 :]
    share = jnp.where(is_y, high, low)
    give = jnp.where(is_y, low, high).astype(jnp.bfloat16)
    carried_both = pair_tokens(carried_own, carried_part, carried_other)
    zero = units_of(dz[0], dy[0])
    out_zero = out_kernel(activated, zero)
    up_chunks = up_chunks + [stack(*units_of(uz[s], uy[s])) for s in far]
    (
        dzp, dyp, carried_both, out_zero, share, give, mine_high, other_high, dz, dy, up_chunks,
    ) = together(
        dzp, dyp, carried_both, out_zero, share, give, mine_high, other_high, dz, dy, up_chunks
    )

    def unit(s, u):
        return [(dzp[s][u], 0, rows), (dyp[s][u], 0, rows)]

    zero = units_of(dz[0], dy[0])
    for s in far:
        dzp[s][1] = hop(other_high if s & 1 else mine_high, s << 2)
    dyp[2][1] = hop(dzp[2][1], 2)
    dyp[1][1] = hop(dzp[1][1], 2)
    carried_both = [carried_both, hop(carried_both, 1)]
    ends = range(2, layers)
    out_low = out_kernel(activated, sum([unit(s, 0) for s in ends], []))
    partial = act_kernel(
        carried_both,
        [(0, zero), (chunk, unit(1, 0))] + [(s * chunk, unit(s, 0)) for s in ends],
        None,
    )
    dzp, dyp, carried_both, out_zero, out_low, partial, slope, share, give = together(
        dzp, dyp, carried_both, out_zero, out_low, partial, slope, share, give
    )

    for s in far:
        dyp[s][1] = hop(dzp[s][1], 2)
    core_zero = core_add(out_zero[0], hop(out_zero[1], 1))
    got_one = hop(core_zero[1], 4)
    core_low = core_add(out_low[0], hop(out_low[1], 1))
    share = share + hop(give, 2).astype(jnp.float32)
    out_one = out_kernel(activated, unit(1, 0) + unit(1, 1))
    dyp, core_zero, got_one, core_low, out_one, share = together(
        dyp, core_zero, got_one, core_low, out_one, share
    )

    pre_own, pre_pair, pre_other = act_kernel(
        carried_both,
        [(s * chunk + chunk // 2, unit(s, 1)) for s in range(1, layers)],
        partial,
        slope,
    )

    def other_product(s):
        return dot_t(pre_other, up_chunks[s]).astype(jnp.bfloat16)

    def pair_product(s):
        return (
            dot_t(pre_pair, up_chunks[s]) + from_core[s][tokens:].astype(jnp.float32)
        ).astype(jnp.bfloat16)

    def own_product(s):
        return (
            dot_t(pre_own, up_chunks[s])
            + from_core[s][:tokens].astype(jnp.float32)
            + from_pair[s].astype(jnp.float32)
        ).astype(jnp.bfloat16)

    def share_mp(piece):
        if groups == 2:
            return swap_mp(piece)
        whole = lax.psum(piece.astype(jnp.float32), "mp")
        return whole - piece.astype(jnp.float32)

    to_core, from_core, to_pair, from_pair, grad_mine, grad_got = [
        [None] * layers for _ in range(6)
    ]
    to_core[0] = other_product(0)
    share = share + hop(share.astype(jnp.bfloat16), 4).astype(jnp.float32)
    got_low = hop(core_low[1], 4)
    one_got = hop(out_one[1], 1)
    (
        pre_own, pre_pair, pre_other, to_core, hidden_pre, share, activated, out_one, one_got,
        got_low, core_low,
    ) = together(
        pre_own, pre_pair, pre_other, to_core, hidden_pre, share, activated, out_one, one_got,
        got_low, core_low,
    )

    def to_holder(value, p):
        if not paired:
            return value
        moves = []
        for i in range(size):
            holder = ((i >> 3) ^ p) & 1
            moves.append((2 * i + 1 - holder, 2 * i + holder))
        return lax.ppermute(value, ("dp", "mp"), moves)

    from_core[0] = hop(to_core[0], 1)
    to_pair[0] = pair_product(0)
    to_core[1] = other_product(1)
    from_core, to_pair, to_core, pre_own, pre_pair, pre_other = together(
        from_core, to_pair, to_core, pre_own, pre_pair, pre_other
    )
    high, pair_one, core_high, got_zero, got_high = [None] * 5
    sum_one, sum_zero, sum_high, sent_zero, sent_one, sent_low, sent_high = [None] * 7
    stat = other = half = None
    for step in range(layers + 3):
        if step < layers:
            from_pair[step ^ 1] = hop(to_pair[step], 4)
        if 2 <= step < layers + 2:
            s = (step - 2) ^ 1
            grad_got[s] = share_mp(grad_mine[s])
        if 1 <= step <= layers:
            s = (step - 1) ^ 1
            grad_mine[s] = own_product(s)
        if step + 1 < layers:
            from_core[step + 1] = hop(to_core[step + 1], 1)
            to_pair[step + 1] = pair_product(step + 1)
        if step + 2 < layers:
            to_core[step + 2] = other_product(step + 2)
        if step == 0:
            sum_low = pair_add(core_low[0], got_low, swapped=True) if paired else None
            sum_one, pair_one = whole_add(out_one[0], one_got, got_one)
            stat = [
                jnp.sum(hidden_pre[first:last] * rows_of.astype(jnp.float32), axis=1)[:, None]
                for first, last, rows_of in (
                    (0, tokens, pre_own),
                    (tokens, 2 * tokens, pre_pair),
                    (2 * tokens, 4 * tokens, pre_other),
                )
            ]
        if step == 1:
            sent_one = to_holder(sum_one, 0)
            if paired:
                sent_low = to_holder(sum_low, 1)
            stat_got = hop(stat[2], 1)
            stat = [stat[0] + stat_got[:tokens], stat[1] + stat_got[tokens:]]
        if step == 2:
            high = out_kernel(activated, sum([unit(s, 1) for s in ends], []))
            stat = stat[0] + hop(stat[1], 4)
        if step == 3:
            core_high = core_add(high[0], hop(high[1], 1))
            stat = stat + swap_mp(stat) if groups == 2 else lax.psum(stat, "mp")
            bit = 8
            while bit < size:
                share = share + hop(share.astype(jnp.bfloat16), bit).astype(jnp.float32)
                bit *= 2
        if step == layers:
            got_zero = hop(pair_one, 4)
            other = hop(share, 2)
            half = jnp.concatenate(
                [jnp.where(is_y, other, share), jnp.where(is_y, share, other)], axis=0
            )
        if step == layers + 1:
            got_high = hop(core_high[1], 4)
            sum_zero = pair_add(core_zero[0], got_zero)
            other = hop(half, 1)
        if step == layers + 2:
            sent_zero = to_holder(sum_zero, 0)
            if paired:
                sum_high = pair_add(core_high[0], got_high, swapped=True)
                sent_high = to_holder(sum_high, 1)
            break
        state = (
            to_core, from_core, to_pair, from_pair, grad_mine, grad_got, high, pair_one, sum_low, core_high,
            got_zero, got_high, sum_one, sum_zero, sent_one, sent_low, stat, share, other, half,
            pre_own, pre_pair, pre_other, hidden_pre, activated, core_zero,
        )
        (
            to_core, from_core, to_pair, from_pair, grad_mine, grad_got, high, pair_one, sum_low, core_high,
            got_zero, got_high, sum_one, sum_zero, sent_one, sent_low, stat, share, other, half,
            pre_own, pre_pair, pre_other, hidden_pre, activated, core_zero,
        ) = together(*state)
    adapter_down_grad = jnp.where(is_core, other, half).T
    adapter_up_grad = jnp.where(is_core, half, other)

    input_grad_second = final_kernel(
        at, size, grad_second, lower_full, gain, inverse_rms, stat, grad_mine, grad_got
    )

    if paired:
        lower_first = first_kernel(
            at,
            size,
            upper_slice,
            [sum_zero, sum_one, sum_low, sum_high],
            [sent_zero, sent_one, sent_low, sent_high],
        )
    else:
        width = chunk // 2
        pieces = [sum_zero, sum_one]
        for s in ends:
            for own, got in ((core_low, got_low), (core_high, got_high)):
                mine = own[0][:, (s - 2) * width : (s - 1) * width]
                theirs = got[:, ((s ^ 1) - 2) * width : ((s ^ 1) - 1) * width]
                pieces.append((mine + theirs.astype(jnp.float32)).astype(jnp.bfloat16))
        chunks = pieces[:2] + [
            jnp.concatenate(pieces[i : i + 2], axis=1) for i in range(2, len(pieces), 2)
        ]
        out_whole = restore(at, size, chunks)
        frozen_share = lax.psum_scatter(
            out_whole.astype(jnp.float32), "mp", scatter_dimension=1, tiled=True
        )
        lower_first = ((upper_slice.astype(jnp.float32) - frozen_share) / coupling).astype(
            jnp.bfloat16
        )
    return (
        lower_first,
        lower_second,
        input_grad_first,
        input_grad_second,
        adapter_down_grad,
        adapter_up_grad,
    )


def solution(mesh):
    return jax.shard_map(
        on_device,
        mesh=mesh,
        in_specs=(
            P("dp", None),
            P("dp", None),
            P("dp", None),
            P("dp", None),
            P(),
            P("dp", "mp"),
            P("dp", "mp"),
            P(),
            P(),
        ),
        out_specs=(
            P("dp", "mp"),
            P("dp", "mp"),
            P("dp", "mp"),
            P("dp", None),
            P("mp", None),
            P(None, "mp"),
        ),
        check_vma=False,
    )
```

time: 522 us -> 473 us (0.906)
  Pallas kernels: 151 us -> 104 us
  local copies, waits for them, and re-layouts: 16.5 us -> 42.7 us
  waiting for transfers between devices: 240 us -> 225 us
  other arithmetic: 21.9 us -> 7.93 us
    unnamed x130 -> x202, local copies, waits for them, and re-layouts: 4.89 us -> 30.7 us
    ppermute x7, waiting for transfers between devices: 38.1 us -> 19.3 us  [swap_mp(): return lax.ppermute(value, 'mp', [(0, 1), (1, 0)])]
    pallas_call x5 -> x12, Pallas kernels: 71.5 us -> 55.6 us  [the longest x1 24.6 us: hidden_kernel(): call(functools.partial(hidden_body, units), cost=work(8 * count * columns...]
    pallas_call x4, Pallas kernels: 35.1 us -> 21.1 us  [out_kernel(): call(functools.partial(out_body, units), cost=work(2 * count * columns *...]
    ppermute x50 -> x52, waiting for transfers between devices: 189 us -> 199 us  [hop(): return lax.ppermute(value, 'dp', [(i, i ^ bits) for i in range(size)])]
    pallas_call x2 -> x1, Pallas kernels: 9.99 us -> 0.82 us  [both_tokens(): call(both_body, in_specs=[SMEM] + [pl.BlockSpec(memory_space=pltpu.VMEM)]...]
    ppermute x4, waiting for transfers between devices: 12.8 us -> 6.14 us  [to_holder(): return lax.ppermute(value, ('dp', 'mp'), moves)]
    dot_general x8 -> x12, matrix products: 22 us -> 25.6 us  [dot_t(): lax.dot_general(left, right, (((1,), (1,)), ((), ())), preferred_element_...]
  transfers between devices with their start and end apart: 61 -> 63, of which waited for: 29 -> 27; matrix products, arithmetic and copies ran while one was open for 9% -> 9% of each run, Pallas kernels for 26% -> 21%
where the time goes in v3:
time: 473 us; the launch traced here: 468 us
  waiting for transfers between devices  225 us (48%)
  Pallas kernels  104 us (22%)
  starting transfers between devices  58.7 us (12%)
  local copies, waits for them, and re-layouts  42.7 us (9%)
  matrix products  27.4 us (6%)
  other arithmetic  7.93 us (2%)
    ppermute x52, waiting for transfers between devices, hop(): return lax.ppermute(value, 'dp', [(i, i ^ bits) for i in range(size)])  199 us
    ppermute x52, starting transfers between devices, hop(): return lax.ppermute(value, 'dp', [(i, i ^ bits) for i in range(size)])  39.2 us
    unnamed x202, local copies, waits for them, and re-layouts  30.7 us
    dot_general x12, matrix products, dot_t(): lax.dot_general(left, right, (((1,), (1,)), ((), ())), preferred_element_...  25.6 us
    pallas_call x1, Pallas kernels, hidden_kernel(): call(functools.partial(hidden_body, units), cost=work(8 * count * columns...  24.6 us
    pallas_call x2, Pallas kernels, act_kernel(): call(functools.partial(act_body, units, len(places), depth, len(extra), i...  24.6 us
    pallas_call x4, Pallas kernels, out_kernel(): call(functools.partial(out_body, units), cost=work(2 * count * columns *...  21.1 us
    ppermute x7, waiting for transfers between devices, swap_mp(): return lax.ppermute(value, 'mp', [(0, 1), (1, 0)])  19.3 us
  transfers between devices with their start and end apart: 63, of which 27 were waited for; matrix products, arithmetic and copies ran while one was open for 9% of the time, Pallas kernels for 21%

profile of v3, /device:TPU:0, one launch (start us, length us, event | category | flops | bytes accessed | tf_op | source)
XLA Modules:
  0.0 467.9 jit_solution(13756371687660139562)
XLA Ops:
  0.7 2.7 constant_dynamic-slice_fusion.2
  3.9 3.1 collective-permute-done.got
  7.0 3.2 shard_map.136
  10.8 3.7 collective-permute-start.3
  14.6 1.5 collective-permute-start.4
  16.1 1.6 collective-permute-start.2
  22.8 9.8 %shard_map.138 = (bf16[256,64]{1,0:T(8,128)(2,1)S(1)}, bf16[256,64]{1,0:T(8,128)(2,1)S(1)}, f32[256,128]{1,0:T(8,128)S(1)}, bf16[256,4096]{1,0:T(8,128)(2,1)S(1)...) custom-call(s32[2]{0:T(128)S(1)} %pad_add_fusion.at.refs_0_, ...), custom_call_target="tpu_custom_call" | custom-call | tf_op jit(solution)/shard_map/pallas_call | solution.py:123
  37.9 39.8 %collective-permute-done.3.refs_0_.refs_15_.refs_17_ = bf16[512,1408]{1,0:T(8,128)(2,1)} collective-permute-done((bf16[512,1408]{1,0:T(8,128)(2,1)S(1)}, bf16[512,1408]{1,0:T(8,128)(2,1)}, u32[]{:S(2)}, u32[]{:S(2)}) %collective-permute-start.3) | collective-permute-done | bytes 1441824 | tf_op jit(solution)/shard_map/ppermute | solution.py:32
  81.7 1.9 collective-permute-start.6
  88.6 2.4 shard_map.139
  93.5 24.1 %collective-permute-done.9 = bf16[256,3072]{1,0:T(8,128)(2,1)} collective-permute-done((bf16[256,3072]{1,0:T(8,128)(2,1)}, bf16[256,3072]{1,0:T(8,128)(2,1)}, u32[]{:S(2)}, u32[]{:S(2)}) %collective-permute-start.9) | collective-permute-done | bytes 1572896 | tf_op jit(solution)/shard_map/ppermute | solution.py:32
  118.9 30.9 %collective-permute-done.6.refs_19_.refs_21_.refs_0_ = bf16[512,1408]{1,0:T(8,128)(2,1)} collective-permute-done((bf16[512,1408]{1,0:T(8,128)(2,1)}, bf16[512,1408]{1,0:T(8,128)(2,1)}, u32[]{:S(2)}, u32[]{:S(2)}) %collective-permute-start.6) | collective-permute-done | bytes 1441824 | tf_op jit(solution)/shard_map/ppermute | solution.py:32
  149.8 1.5 collective-permute-start.12
  151.3 1.5 collective-permute-start.14
  154.9 2.3 collective-permute-start.11
  157.2 2.3 shard_map.141
  159.6 1.6 copy-done.24
  161.2 2.4 shard_map.140
  165.1 10.5 %collective-permute-done.13 = bf16[256,1024]{1,0:T(8,128)(2,1)S(1)} collective-permute-done((bf16[256,1024]{1,0:T(8,128)(2,1)S(1)}, bf16[256,1024]{1,0:T(8,128)(2,1)S(1)}, u32[]{:S(2)}, u32[]{:S(2)}) %collective-permute-start.13) | collective-permute-done | bytes 524320 | tf_op jit(solution)/shard_map/ppermute | solution.py:32
  175.6 14.2 %collective-permute-done.11.refs_0_.refs_16_ = bf16[256,1408]{1,0:T(8,128)(2,1)S(1)} collective-permute-done((bf16[256,1408]{1,0:T(8,128)(2,1)S(1)}, bf16[256,1408]{1,0:T(8,128)(2,1)S(1)}, u32[]{:S(2)}, u32[]{:S(2)}) %collective-permute-start.11) | collective-permute-done | bytes 720928 | tf_op jit(solution)/shard_map/ppermute | solution.py:32
  192.4 1.8 collective-permute-start.17
  196.6 24.6 %shard_map.142 = (f32[1024,1408]{1,0:T(8,128)}, f32[1024,1408]{1,0:T(8,128)}, bf16[1024,1408]{1,0:T(8,128)(2,1)}) custom-call(s32[2]{0:T(128)} %copy-done.76, bf16[256,4096]{1,0:T(8,128)(2,1)} %get-tuple-element.340.refs_1_, bf16[256,2048]{1,0:T(8,128)(2,1)} %copy-done.83, bf16[256,2048]{1,0:T(8,128)(2,1)} %copy-done.86, ...), custom_call_target="tpu_custom_call" | custom-call | flops 2952790016 | tf_op jit(solution)/shard_map/pallas_call | solution.py:265
  221.3 5.3 %collective-permute-done.17.refs_2_.refs_18_ = bf16[256,1408]{1,0:T(8,128)(2,1)} collective-permute-done((bf16[256,1408]{1,0:T(8,128)(2,1)}, bf16[256,1408]{1,0:T(8,128)(2,1)}, u32[]{:S(2)}, u32[]{:S(2)}) %collective-permute-start.17) | collective-permute-done | bytes 720928 | tf_op jit(solution)/shard_map/ppermute | solution.py:32
  228.4 1.6 collective-permute-start.21
  234.5 2.5 shard_map.145
  237.0 1.6 copy-done.33
  241.3 4.9 %shard_map.144 = (f32[512,1024]{1,0:T(8,128)S(1)}, bf16[512,1024]{1,0:T(8,128)(2,1)S(1)}) custom-call(bf16[1024,1408]{1,0:T(8,128)(2,1)S(1)} %copy-done, bf16[512,1408]{1,0:T(8,128)(2,1)S(1)} %copy-done.2, bf16[512,1408]{1,0:T(8,128)(2,1)S(1)} %copy-done.4, bf16[512,1408]{1,0:T(8,128)(2,1)S(1)} %copy-done.2, bf16[512,1408]{1,0:T(8,128)(2,1)S(1)} %copy-done.4), custom_call_target="tpu_custom_call" | custom-call | flops 738197504 | tf_op jit(solution)/shard_map/pallas_call | solution.py:469
  248.1 13.8 %collective-permute-done.21.refs_2_.refs_6_ = bf16[256,1408]{1,0:T(8,128)(2,1)S(1)} collective-permute-done((bf16[256,1408]{1,0:T(8,128)(2,1)}, bf16[256,1408]{1,0:T(8,128)(2,1)S(1)}, u32[]{:S(2)}, u32[]{:S(2)}) %collective-permute-start.21) | collective-permute-done | bytes 720928 | tf_op jit(solution)/shard_map/ppermute | solution.py:32
  261.8 3.0 collective-permute-done.22.refs_8_.refs_0_
  265.0 1.9 collective-permute-start.26
  268.9 5.4 %shard_map.146 = (f32[512,1024]{1,0:T(8,128)S(1)}, bf16[512,1024]{1,0:T(8,128)(2,1)S(1)}) custom-call(bf16[1024,1408]{1,0:T(8,128)(2,1)S(1)} %copy-done, bf16[256,1408]{1,0:T(8,128)(2,1)S(1)} %copy-done.21, bf16[256,1408]{1,0:T(8,128)(2,1)S(1)} %copy-done.23, bf16[256,1408]{1,0:T(8,128)(2,1)} %collective-permute-done.17.refs_2_.refs_18_, ...), custom_call_target="tpu_custom_call" | custom-call | flops 738197504 | tf_op jit(solution)/shard_map/pallas_call | solution.py:469
  275.6 14.1 %shard_map.147.refs_12_ = f32[1024,1408]{1,0:T(8,128)} custom-call(bf16[512,4096]{1,0:T(8,128)(2,1)S(1)} %shard_map.143.refs_0_.refs_2_.refs_4_.refs_6_.refs_8_, bf16[512,4096]{1,0:T(8,128)(2,1)S(1)} %collective-permute-done.29.refs_1_.refs_3_.refs_5_.refs_7_.refs_9_, bf16[512,4096]{1,0:T(8,128)(2,1)S(1)} %shard_map.143.refs_0_.refs_2_.refs_4_.refs_6_.refs_8_, ...), custom_call_target="tpu_custom_call" | custom-call | flops 1845493760 | tf_op jit(solution)/shard_map/pallas_call | solution.py:328
  289.8 10.7 %collective-permute-done.28.refs_9_.refs_1_ = bf16[256,1408]{1,0:T(8,128)(2,1)S(1)} collective-permute-done((bf16[256,1408]{1,0:T(8,128)(2,1)S(1)}, bf16[256,1408]{1,0:T(8,128)(2,1)S(1)}, u32[]{:S(2)}, u32[]{:S(2)}) %collective-permute-start.28) | collective-permute-done | bytes 720928 | tf_op jit(solution)/shard_map/ppermute | solution.py:32
  304.7 6.0 %shard_map.150 = (f32[512,1024]{1,0:T(8,128)S(1)}, bf16[512,1024]{1,0:T(8,128)(2,1)}) custom-call(bf16[1024,1408]{1,0:T(8,128)(2,1)S(1)} %copy-done, bf16[256,1408]{1,0:T(8,128)(2,1)} %collective-permute-done.16.refs_14_.refs_0_, bf16[256,1408]{1,0:T(8,128)(2,1)S(1)} %collective-permute-done.23.refs_15_.refs_1_, ...), custom_call_target="tpu_custom_call" | custom-call | flops 738197504 | tf_op jit(solution)/shard_map/pallas_call | solution.py:469
  310.7 11.2 %collective-permute-done.34 = bf16[32,2048]{1,0:T(8,128)(2,1)S(1)} collective-permute-done((bf16[32,2048]{1,0:T(8,128)(2,1)S(1)}, bf16[32,2048]{1,0:T(8,128)(2,1)S(1)}, u32[]{:S(2)}, u32[]{:S(2)}) %collective-permute-start.34) | collective-permute-done | bytes 131104 | tf_op jit(solution)/shard_map/ppermute | solution.py:32
  324.1 1.6 collective-permute-start.37
  325.8 10.5 %shard_map.151 = (bf16[256,1408]{1,0:T(8,128)(2,1)S(1)}, bf16[256,1408]{1,0:T(8,128)(2,1)S(1)}, bf16[512,1408]{1,0:T(8,128)(2,1)S(1)}) custom-call(bf16[512,4096]{1,0:T(8,128)(2,1)S(1)} %shard_map.143.refs_0_.refs_2_.refs_4_.refs_6_.refs_8_, bf16[512,4096]{1,0:T(8,128)(2,1)S(1)} %collective-permute-done.29.refs_1_.refs_3_.refs_5_.refs_7_.refs_9_, ...), custom_call_target="tpu_custom_call" | custom-call | flops 1107296256 | tf_op jit(solution)/shard_map/pallas_call | solution.py:328
  336.3 1.8 convolution_convert_fusion.3
  338.9 2.1 collective-permute-done.37.got
  341.1 1.8 convolution_convert_fusion.2
  348.9 2.8 convolution_convert_fusion.1
  352.6 1.8 fusion.9
  354.4 6.7 %collective-permute-done.40 = bf16[256,1024]{1,0:T(8,128)(2,1)S(1)} collective-permute-done((bf16[256,1024]{1,0:T(8,128)(2,1)S(1)}, bf16[256,1024]{1,0:T(8,128)(2,1)S(1)}, u32[]{:S(2)}, u32[]{:S(2)}) %collective-permute-start.40) | collective-permute-done | bytes 524320 | tf_op jit(solution)/shard_map/ppermute | solution.py:32
  365.2 6.3 %collective-permute-start.44 = (bf16[256,1024]{1,0:T(8,128)(2,1)S(1)}, bf16[256,1024]{1,0:T(8,128)(2,1)}, u32[]{:S(2)}, u32[]{:S(2)}) collective-permute-start(bf16[256,1024]{1,0:T(8,128)(2,1)S(1)} %shard_map.153.refs_2_), channel_id=1, source_target_pairs={{0,1},{2,3},{4,5},{6,7},{8,9},{10,11},{12,13},{14,15},{17,16},{19,... | collective-permute-start | bytes 1572872 | tf_op jit(solution)/shard_map/ppermute | solution.py:850
  371.5 5.1 %convolution_convert_fusion = bf16[512,1024]{1,0:T(8,128)(2,1)} fusion(bf16[512,1408]{1,0:T(8,128)(2,1)} %copy-done.53, bf16[1024,1408]{1,0:T(8,128)(2,1)} %copy-done.33), kind=kOutput, calls=%fused_computation.3 | convolution fusion | flops 1476919296 | bytes 5373952 | tf_op jit(solution)/shard_map/dot_general | solution.py:53
  376.6 1.8 fusion.7.refs_1_
  381.9 3.3 fusion.10
  385.4 1.6 collective-permute-start.49
  387.5 2.1 fusion.6.refs_0_
  389.6 4.9 %shard_map.154 = (f32[512,1024]{1,0:T(8,128)S(1)}, bf16[512,1024]{1,0:T(8,128)(2,1)S(1)}) custom-call(bf16[1024,1408]{1,0:T(8,128)(2,1)S(1)} %copy-done, bf16[256,1408]{1,0:T(8,128)(2,1)S(1)} %copy-done.36, bf16[256,1408]{1,0:T(8,128)(2,1)S(1)} %copy-done.40, bf16[256,1408]{1,0:T(8,128)(2,1)S(1)} %copy-done.38, bf16[256,1408]{1,0:T(8,128)(2,1)S(1)} %copy-done.42), custom_call_target="tpu_custom_call" | custom-call | flops 738197504 | tf_op jit(solution)/shard_map/pallas_call | solution.py:469
  395.6 6.9 %collective-permute-done.47 = bf16[256,1024]{1,0:T(8,128)(2,1)S(1)} collective-permute-done((bf16[256,1024]{1,0:T(8,128)(2,1)S(1)}, bf16[256,1024]{1,0:T(8,128)(2,1)S(1)}, u32[]{:S(2)}, u32[]{:S(2)}) %collective-permute-start.47) | collective-permute-done | bytes 524320 | tf_op jit(solution)/shard_map/ppermute | solution.py:32
  403.1 3.1 collective-permute-start.53
  407.7 2.8 collective-permute-done.53
  410.5 1.8 collective-permute-done.54
  412.5 9.2 %collective-permute-done.50 = bf16[256,1024]{1,0:T(8,128)(2,1)S(1)} collective-permute-done((bf16[256,1024]{1,0:T(8,128)(2,1)S(1)}, bf16[256,1024]{1,0:T(8,128)(2,1)S(1)}, u32[]{:S(2)}, u32[]{:S(2)}) %collective-permute-start.50) | collective-permute-done | bytes 524320 | tf_op jit(solution)/shard_map/ppermute | solution.py:32
  424.1 2.1 fusion.4.refs_2_
  426.2 3.1 collective-permute-done.57
  429.4 5.8 %collective-permute-done.55.refs_7_ = bf16[256,1024]{1,0:T(8,128)(2,1)S(1)} collective-permute-done((bf16[256,1024]{1,0:T(8,128)(2,1)S(1)}, bf16[256,1024]{1,0:T(8,128)(2,1)S(1)}, u32[]{:S(2)}, u32[]{:S(2)}) %collective-permute-start.55) | collective-permute-done | bytes 524320 | tf_op jit(solution)/shard_map/ppermute | solution.py:36
  437.4 10.7 %collective-permute-done.58.refs_6_ = bf16[256,1024]{1,0:T(8,128)(2,1)S(1)} collective-permute-done((bf16[256,1024]{1,0:T(8,128)(2,1)S(1)}, bf16[256,1024]{1,0:T(8,128)(2,1)S(1)}, u32[]{:S(2)}, u32[]{:S(2)}) %collective-permute-start.58) | collective-permute-done | bytes 524320 | tf_op jit(solution)/shard_map/ppermute | solution.py:36
  448.4 3.4 collective-permute-start.62
  453.2 3.6 shard_map.159
  457.8 2.0 collective-permute-done.62.refs_7_
  459.8 4.1 collective-permute-done.61.refs_4_
  464.0 3.7 shard_map.158
  (333 shorter events, 79.8 us)
Async XLA Ops:
  3.4 3.6 collective-permute-start
  10.4 7.3 %collective-permute-start.1 = (bf16[256,2816]{1,0:T(8,128)(2,1)S(1)}, bf16[256,2816]{1,0:T(8,128)(2,1)S(1)}, u32[]{:S(2)}, u32[]{:S(2)}) collective-permute-start(bf16[256,2816]{1,0:T(8,128)(2,1)S(1)} %constant_dynamic-slice_fusion), channel_id=1, source_target_pairs={{0,2},{2,0},{4,6},{6,4},{8,10},{10,8},{12,14},{14,12},{16,18},{18,... | collective-permute-start | bytes 4325384 | tf_op jit(solution)/shard_map/ppermute | solution.py:32
  10.8 66.9 %collective-permute-start.3 = (bf16[512,1408]{1,0:T(8,128)(2,1)S(1)}, bf16[512,1408]{1,0:T(8,128)(2,1)}, u32[]{:S(2)}, u32[]{:S(2)}) collective-permute-start(bf16[512,1408]{1,0:T(8,128)(2,1)S(1)} %get-tuple-element.345.refs_0_.refs_7_.refs_9_), channel_id=1, source_target_pairs={{0,16},{2,18},{4,20},{6,22},{8,24},{10,26},{12,28},{14,30},{16,0},... | collective-permute-start | bytes 4325384 | tf_op jit(solution)/shard_map/ppermute | solution.py:32
  14.6 63.2 %collective-permute-start.4 = (bf16[512,1408]{1,0:T(8,128)(2,1)S(1)}, bf16[512,1408]{1,0:T(8,128)(2,1)S(1)}, u32[]{:S(2)}, u32[]{:S(2)}) collective-permute-start(bf16[512,1408]{1,0:T(8,128)(2,1)S(1)} %get-tuple-element.345.refs_0_.refs_7_.refs_9_), channel_id=1, source_target_pairs={{0,4},{2,6},{4,0},{6,2},{8,12},{10,14},{12,8},{14,10},{16,20},{18,... | collective-permute-start | bytes 4325384 | tf_op jit(solution)/shard_map/ppermute | solution.py:32
  16.1 63.3 %collective-permute-start.2 = (bf16[512,1408]{1,0:T(8,128)(2,1)}, bf16[512,1408]{1,0:T(8,128)(2,1)}, u32[]{:S(2)}, u32[]{:S(2)}) collective-permute-start(bf16[512,1408]{1,0:T(8,128)(2,1)} %get-tuple-element.311), channel_id=1, source_target_pairs={{0,8},{2,10},{4,12},{6,14},{8,0},{10,2},{12,4},{14,6},{16,24},{18,... | collective-permute-start | bytes 4325384 | tf_op jit(solution)/shard_map/ppermute | solution.py:32
  20.1 133.8 %copy-start.1 = (bf16[512,1408]{1,0:T(8,128)(2,1)}, bf16[512,1408]{1,0:T(8,128)(2,1)S(1)}, u32[]{:S(2)}) copy-start(bf16[512,1408]{1,0:T(8,128)(2,1)S(1)} %get-tuple-element.397.refs_0_.refs_2_.refs_10_.refs_12_) | copy-start | bytes 4325380
  20.1 59.3 %collective-permute-start.5 = (bf16[512,1408]{1,0:T(8,128)(2,1)S(1)}, bf16[512,1408]{1,0:T(8,128)(2,1)S(1)}, u32[]{:S(2)}, u32[]{:S(2)}) collective-permute-start(bf16[512,1408]{1,0:T(8,128)(2,1)S(1)} %get-tuple-element.397.refs_0_.refs_2_.refs_10_.refs_12_), channel_id=1, source_target_pairs={{0,4},{2,6},{4,0},{6,2},{8,12},{10,14},{12,8},{14,10},{16,20},{18,... | collective-permute-start | bytes 4325384 | tf_op jit(solution)/shard_map/ppermute | solution.py:32
  80.5 69.3 %collective-permute-start.10 = (bf16[256,4096]{1,0:T(8,128)(2,1)}, bf16[256,4096]{1,0:T(8,128)(2,1)}, u32[]{:S(2)}, u32[]{:S(2)}) collective-permute-start(bf16[256,4096]{1,0:T(8,128)(2,1)} %get-tuple-element.340.refs_1_), channel_id=1, source_target_pairs={{0,2},{2,0},{4,6},{6,4},{8,10},{10,8},{12,14},{14,12},{16,18},{18,... | collective-permute-start | bytes 6291464 | tf_op jit(solution)/shard_map/ppermute | solution.py:32
  80.5 37.1 %collective-permute-start.9 = (bf16[256,3072]{1,0:T(8,128)(2,1)}, bf16[256,3072]{1,0:T(8,128)(2,1)}, u32[]{:S(2)}, u32[]{:S(2)}) collective-permute-start(bf16[256,3072]{1,0:T(8,128)(2,1)} %get-tuple-element.313), channel_id=1, source_target_pairs={{0,8},{2,10},{4,12},{6,14},{8,0},{10,2},{12,4},{14,6},{16,24},{18,... | collective-permute-start | bytes 4718600 | tf_op jit(solution)/shard_map/ppermute | solution.py:32
  81.7 68.1 %collective-permute-start.6 = (bf16[512,1408]{1,0:T(8,128)(2,1)}, bf16[512,1408]{1,0:T(8,128)(2,1)}, u32[]{:S(2)}, u32[]{:S(2)}) collective-permute-start(bf16[512,1408]{1,0:T(8,128)(2,1)} %get-tuple-element.311), channel_id=1, source_target_pairs={{0,24},{2,26},{4,28},{6,30},{8,16},{10,18},{12,20},{14,22},{16,8},... | collective-permute-start | bytes 4325384 | tf_op jit(solution)/shard_map/ppermute | solution.py:32
  83.6 66.3 %collective-permute-start.7 = (bf16[512,1408]{1,0:T(8,128)(2,1)}, bf16[512,1408]{1,0:T(8,128)(2,1)}, u32[]{:S(2)}, u32[]{:S(2)}) collective-permute-start(bf16[512,1408]{1,0:T(8,128)(2,1)} %collective-permute-done.2.refs_0_.refs_11_.refs_13_), channel_id=1, source_target_pairs={{0,4},{2,6},{4,0},{6,2},{8,12},{10,14},{12,8},{14,10},{16,20},{18,... | collective-permute-start | bytes 4325384 | tf_op jit(solution)/shard_map/ppermute | solution.py:32
  85.0 64.8 %collective-permute-start.8 = (bf16[512,1408]{1,0:T(8,128)(2,1)}, bf16[512,1408]{1,0:T(8,128)(2,1)}, u32[]{:S(2)}, u32[]{:S(2)}) collective-permute-start(bf16[512,1408]{1,0:T(8,128)(2,1)} %collective-permute-done.3.refs_0_.refs_15_.refs_17_), channel_id=1, source_target_pairs={{0,4},{2,6},{4,0},{6,2},{8,12},{10,14},{12,8},{14,10},{16,20},{18,... | collective-permute-start | bytes 4325384 | tf_op jit(solution)/shard_map/ppermute | solution.py:32
  149.8 40.0 %collective-permute-start.12 = (bf16[512,1408]{1,0:T(8,128)(2,1)}, bf16[512,1408]{1,0:T(8,128)(2,1)S(1)}, u32[]{:S(2)}, u32[]{:S(2)}) collective-permute-start(bf16[512,1408]{1,0:T(8,128)(2,1)} %collective-permute-done.6.refs_19_.refs_21_.refs_0_), channel_id=1, source_target_pairs={{0,4},{2,6},{4,0},{6,2},{8,12},{10,14},{12,8},{14,10},{16,20},{18,... | collective-permute-start | bytes 4325384 | tf_op jit(solution)/shard_map/ppermute | solution.py:32
  151.3 38.5 %collective-permute-start.14 = (bf16[256,2048]{1,0:T(8,128)(2,1)S(1)}, bf16[256,2048]{1,0:T(8,128)(2,1)S(1)}, u32[]{:S(2)}, u32[]{:S(2)}) collective-permute-start(bf16[256,2048]{1,0:T(8,128)(2,1)S(1)} %slice.84.refs_2_), channel_id=1, source_target_pairs={{0,1},{1,0},{2,3},{3,2},{4,5},{5,4},{6,7},{7,6},{8,9},{9,8},{10,11... | collective-permute-start | bytes 3145736 | tf_op jit(solution)/shard_map/ppermute | solution.py:36
  152.8 37.0 %collective-permute-start.15 = (bf16[256,2048]{1,0:T(8,128)(2,1)S(1)}, bf16[256,2048]{1,0:T(8,128)(2,1)S(1)}, u32[]{:S(2)}, u32[]{:S(2)}) collective-permute-start(bf16[256,2048]{1,0:T(8,128)(2,1)S(1)} %slice.84.refs_2_), channel_id=1, source_target_pairs={{0,2},{2,0},{4,6},{6,4},{8,10},{10,8},{12,14},{14,12},{16,18},{18,... | collective-permute-start | bytes 3145736 | tf_op jit(solution)/shard_map/ppermute | solution.py:32
  152.8 22.7 %collective-permute-start.13 = (bf16[256,1024]{1,0:T(8,128)(2,1)S(1)}, bf16[256,1024]{1,0:T(8,128)(2,1)S(1)}, u32[]{:S(2)}, u32[]{:S(2)}) collective-permute-start(bf16[256,1024]{1,0:T(8,128)(2,1)S(1)} %copy-done.82), channel_id=1, source_target_pairs={{0,8},{2,10},{4,12},{6,14},{8,0},{10,2},{12,4},{14,6},{16,24},{18,... | collective-permute-start | bytes 1572872 | tf_op jit(solution)/shard_map/ppermute | solution.py:32
  154.9 34.9 %collective-permute-start.11 = (bf16[256,1408]{1,0:T(8,128)(2,1)S(1)}, bf16[256,1408]{1,0:T(8,128)(2,1)S(1)}, u32[]{:S(2)}, u32[]{:S(2)}) collective-permute-start(bf16[256,1408]{1,0:T(8,128)(2,1)S(1)} %get-tuple-element.581), channel_id=1, source_target_pairs={{0,16},{2,18},{4,20},{6,22},{8,24},{10,26},{12,28},{14,30},{16,0},... | collective-permute-start | bytes 2162696 | tf_op jit(solution)/shard_map/ppermute | solution.py:32
  190.9 4.8 %collective-permute-start.20 = (bf16[256,2048]{1,0:T(8,128)(2,1)S(1)}, bf16[256,2048]{1,0:T(8,128)(2,1)S(1)}, u32[]{:S(2)}, u32[]{:S(2)}) collective-permute-start(bf16[256,2048]{1,0:T(8,128)(2,1)S(1)} %collective-permute-done.14.refs_3_), channel_id=1, source_target_pairs={{0,2},{2,0},{4,6},{6,4},{8,10},{10,8},{12,14},{14,12},{16,18},{18,... | collective-permute-start | bytes 3145736 | tf_op jit(solution)/shard_map/ppermute | solution.py:32
  190.9 36.6 %collective-permute-start.19 = (bf16[256,2048]{1,0:T(8,128)(2,1)S(1)}, bf16[256,2048]{1,0:T(8,128)(2,1)S(1)}, u32[]{:S(2)}, u32[]{:S(2)}) collective-permute-start(bf16[256,2048]{1,0:T(8,128)(2,1)S(1)} %pad_maximum_fusion.part), channel_id=1, source_target_pairs={{0,1},{1,0},{2,3},{3,2},{4,5},{5,4},{6,7},{7,6},{8,9},{9,8},{10,11... | collective-permute-start | bytes 3145736 | tf_op jit(solution)/shard_map/ppermute | solution.py:36
  192.4 28.9 %collective-permute-start.16 = (bf16[256,1408]{1,0:T(8,128)(2,1)}, bf16[256,1408]{1,0:T(8,128)(2,1)}, u32[]{:S(2)}, u32[]{:S(2)}) collective-permute-start(bf16[256,1408]{1,0:T(8,128)(2,1)} %get-tuple-element.337), channel_id=1, source_target_pairs={{0,8},{2,10},{4,12},{6,14},{8,0},{10,2},{12,4},{14,6},{16,24},{18,... | collective-permute-start | bytes 2162696 | tf_op jit(solution)/shard_map/ppermute | solution.py:32
  192.4 34.2 %collective-permute-start.17 = (bf16[256,1408]{1,0:T(8,128)(2,1)}, bf16[256,1408]{1,0:T(8,128)(2,1)}, u32[]{:S(2)}, u32[]{:S(2)}) collective-permute-start(bf16[256,1408]{1,0:T(8,128)(2,1)} %get-tuple-element.337), channel_id=1, source_target_pairs={{0,24},{2,26},{4,28},{6,30},{8,16},{10,18},{12,20},{14,22},{16,8},... | collective-permute-start | bytes 2162696 | tf_op jit(solution)/shard_map/ppermute | solution.py:32
  194.2 32.4 %collective-permute-start.18 = (bf16[256,1408]{1,0:T(8,128)(2,1)S(1)}, bf16[256,1408]{1,0:T(8,128)(2,1)S(1)}, u32[]{:S(2)}, u32[]{:S(2)}) collective-permute-start(bf16[256,1408]{1,0:T(8,128)(2,1)S(1)} %collective-permute-done.11.refs_0_.refs_16_), channel_id=1, source_target_pairs={{0,4},{2,6},{4,0},{6,2},{8,12},{10,14},{12,8},{14,10},{16,20},{18,... | collective-permute-start | bytes 2162696 | tf_op jit(solution)/shard_map/ppermute | solution.py:32
  228.4 17.7 %collective-permute-start.25 = (bf16[64,2048]{1,0:T(8,128)(2,1)S(1)}, bf16[64,2048]{1,0:T(8,128)(2,1)}, u32[]{:S(2)}, u32[]{:S(2)}) collective-permute-start(bf16[64,2048]{1,0:T(8,128)(2,1)S(1)} %copy-done.90), channel_id=1, source_target_pairs={{0,2},{2,0},{4,6},{6,4},{8,10},{10,8},{12,14},{14,12},{16,18},{18,... | collective-permute-start | bytes 786440 | tf_op jit(solution)/shard_map/ppermute | solution.py:32
  228.4 33.4 %collective-permute-start.21 = (bf16[256,1408]{1,0:T(8,128)(2,1)}, bf16[256,1408]{1,0:T(8,128)(2,1)S(1)}, u32[]{:S(2)}, u32[]{:S(2)}) collective-permute-start(bf16[256,1408]{1,0:T(8,128)(2,1)} %get-tuple-element.388), channel_id=1, source_target_pairs={{0,8},{2,10},{4,12},{6,14},{8,0},{10,2},{12,4},{14,6},{16,24},{18,... | collective-permute-start | bytes 2162696 | tf_op jit(solution)/shard_map/ppermute | solution.py:32
  230.1 34.8 %collective-permute-start.22 = (bf16[256,1408]{1,0:T(8,128)(2,1)}, bf16[256,1408]{1,0:T(8,128)(2,1)S(1)}, u32[]{:S(2)}, u32[]{:S(2)}) collective-permute-start(bf16[256,1408]{1,0:T(8,128)(2,1)} %get-tuple-element.365), channel_id=1, source_target_pairs={{0,16},{2,18},{4,20},{6,22},{8,24},{10,26},{12,28},{14,30},{16,0},... | collective-permute-start | bytes 2162696 | tf_op jit(solution)/shard_map/ppermute | solution.py:32
  231.1 33.8 %collective-permute-start.23 = (bf16[256,1408]{1,0:T(8,128)(2,1)}, bf16[256,1408]{1,0:T(8,128)(2,1)S(1)}, u32[]{:S(2)}, u32[]{:S(2)}) collective-permute-start(bf16[256,1408]{1,0:T(8,128)(2,1)} %collective-permute-done.16.refs_14_.refs_0_), channel_id=1, source_target_pairs={{0,4},{2,6},{4,0},{6,2},{8,12},{10,14},{12,8},{14,10},{16,20},{18,... | collective-permute-start | bytes 2162696 | tf_op jit(solution)/shard_map/ppermute | solution.py:32
  231.7 33.2 %collective-permute-start.24 = (bf16[256,1408]{1,0:T(8,128)(2,1)}, bf16[256,1408]{1,0:T(8,128)(2,1)S(1)}, u32[]{:S(2)}, u32[]{:S(2)}) collective-permute-start(bf16[256,1408]{1,0:T(8,128)(2,1)} %collective-permute-done.17.refs_2_.refs_18_), channel_id=1, source_target_pairs={{0,4},{2,6},{4,0},{6,2},{8,12},{10,14},{12,8},{14,10},{16,20},{18,... | collective-permute-start | bytes 2162696 | tf_op jit(solution)/shard_map/ppermute | solution.py:32
  264.9 10.7 %collective-permute-start.29 = (bf16[512,4096]{1,0:T(8,128)(2,1)S(1)}, bf16[512,4096]{1,0:T(8,128)(2,1)S(1)}, u32[]{:S(2)}, u32[]{:S(2)}) collective-permute-start(bf16[512,4096]{1,0:T(8,128)(2,1)S(1)} %shard_map.143.refs_0_.refs_2_.refs_4_.refs_6_.refs_8_), channel_id=1, source_target_pairs={{0,2},{2,0},{4,6},{6,4},{8,10},{10,8},{12,14},{14,12},{16,18},{18,... | collective-permute-start | bytes 12582920 | tf_op jit(solution)/shard_map/ppermute | solution.py:32
  265.0 24.8 %collective-permute-start.26 = (bf16[256,1408]{1,0:T(8,128)(2,1)}, bf16[256,1408]{1,0:T(8,128)(2,1)S(1)}, u32[]{:S(2)}, u32[]{:S(2)}) collective-permute-start(bf16[256,1408]{1,0:T(8,128)(2,1)} %get-tuple-element.388), channel_id=1, source_target_pairs={{0,24},{2,26},{4,28},{6,30},{8,16},{10,18},{12,20},{14,22},{16,8},... | collective-permute-start | bytes 2162696 | tf_op jit(solution)/shard_map/ppermute | solution.py:32
  266.8 22.9 %collective-permute-start.27 = (bf16[256,1408]{1,0:T(8,128)(2,1)S(1)}, bf16[256,1408]{1,0:T(8,128)(2,1)S(1)}, u32[]{:S(2)}, u32[]{:S(2)}) collective-permute-start(bf16[256,1408]{1,0:T(8,128)(2,1)S(1)} %collective-permute-done.21.refs_2_.refs_6_), channel_id=1, source_target_pairs={{0,4},{2,6},{4,0},{6,2},{8,12},{10,14},{12,8},{14,10},{16,20},{18,... | collective-permute-start | bytes 2162696 | tf_op jit(solution)/shard_map/ppermute | solution.py:32
  267.4 33.1 %collective-permute-start.28 = (bf16[256,1408]{1,0:T(8,128)(2,1)S(1)}, bf16[256,1408]{1,0:T(8,128)(2,1)S(1)}, u32[]{:S(2)}, u32[]{:S(2)}) collective-permute-start(bf16[256,1408]{1,0:T(8,128)(2,1)S(1)} %collective-permute-done.22.refs_8_.refs_0_), channel_id=1, source_target_pairs={{0,4},{2,6},{4,0},{6,2},{8,12},{10,14},{12,8},{14,10},{16,20},{18,... | collective-permute-start | bytes 2162696 | tf_op jit(solution)/shard_map/ppermute | solution.py:32
  300.5 2.7 collective-permute-start.31
  300.5 21.4 %collective-permute-start.33 = (bf16[512,1024]{1,0:T(8,128)(2,1)S(1)}, bf16[512,1024]{1,0:T(8,128)(2,1)S(1)}, u32[]{:S(2)}, u32[]{:S(2)}) collective-permute-start(bf16[512,1024]{1,0:T(8,128)(2,1)S(1)} %get-tuple-element.414), channel_id=1, source_target_pairs={{0,2},{2,0},{4,6},{6,4},{8,10},{10,8},{12,14},{14,12},{16,18},{18,... | collective-permute-start | bytes 3145736 | tf_op jit(solution)/shard_map/ppermute | solution.py:32
  301.0 21.9 %collective-permute-start.30 = (bf16[256,1408]{1,0:T(8,128)(2,1)S(1)}, bf16[256,1408]{1,0:T(8,128)(2,1)S(1)}, u32[]{:S(2)}, u32[]{:S(2)}) collective-permute-start(bf16[256,1408]{1,0:T(8,128)(2,1)S(1)} %collective-permute-done.26.refs_10_.refs_2_), channel_id=1, source_target_pairs={{0,4},{2,6},{4,0},{6,2},{8,12},{10,14},{12,8},{14,10},{16,20},{18,... | collective-permute-start | bytes 2162696 | tf_op jit(solution)/shard_map/ppermute | solution.py:32
  301.6 20.3 %collective-permute-start.34 = (bf16[32,2048]{1,0:T(8,128)(2,1)S(1)}, bf16[32,2048]{1,0:T(8,128)(2,1)S(1)}, u32[]{:S(2)}, u32[]{:S(2)}) collective-permute-start(bf16[32,2048]{1,0:T(8,128)(2,1)S(1)} %select_convert_fusion.1), channel_id=1, source_target_pairs={{0,4},{2,6},{4,0},{6,2},{8,12},{10,14},{12,8},{14,10},{16,20},{18,... | collective-permute-start | bytes 393224 | tf_op jit(solution)/shard_map/ppermute | solution.py:32
  304.3 18.5 %collective-permute-start.32 = (bf16[256,1024]{1,0:T(8,128)(2,1)S(1)}, bf16[256,1024]{1,0:T(8,128)(2,1)S(1)}, u32[]{:S(2)}, u32[]{:S(2)}) collective-permute-start(bf16[256,1024]{1,0:T(8,128)(2,1)S(1)} %get-tuple-element.412), channel_id=1, source_target_pairs={{0,8},{2,10},{4,12},{6,14},{8,0},{10,2},{12,4},{14,6},{16,24},{18,... | collective-permute-start | bytes 1572872 | tf_op jit(solution)/shard_map/ppermute | solution.py:32
  322.9 18.1 %collective-permute-start.36 = (bf16[512,1024]{1,0:T(8,128)(2,1)}, bf16[512,1024]{1,0:T(8,128)(2,1)S(1)}, u32[]{:S(2)}, u32[]{:S(2)}) collective-permute-start(bf16[512,1024]{1,0:T(8,128)(2,1)} %get-tuple-element.435), channel_id=1, source_target_pairs={{0,2},{2,0},{4,6},{6,4},{8,10},{10,8},{12,14},{14,12},{16,18},{18,... | collective-permute-start | bytes 3145736 | tf_op jit(solution)/shard_map/ppermute | solution.py:32
  323.7 14.4 %collective-permute-start.35 = (bf16[32,2048]{1,0:T(8,128)(2,1)}, bf16[32,2048]{1,0:T(8,128)(2,1)S(1)}, u32[]{:S(2)}, u32[]{:S(2)}) collective-permute-start(bf16[32,2048]{1,0:T(8,128)(2,1)} %convert_element_type.110), channel_id=1, source_target_pairs={{0,8},{2,10},{4,12},{6,14},{8,0},{10,2},{12,4},{14,6},{16,24},{18,... | collective-permute-start | bytes 393224 | tf_op jit(solution)/shard_map/ppermute | solution.py:32
  324.1 16.9 %collective-permute-start.37 = (bf16[256,1024]{1,0:T(8,128)(2,1)}, bf16[256,1024]{1,0:T(8,128)(2,1)S(1)}, u32[]{:S(2)}, u32[]{:S(2)}) collective-permute-start(bf16[256,1024]{1,0:T(8,128)(2,1)} %get-tuple-element.436), channel_id=1, source_target_pairs={{0,8},{2,10},{4,12},{6,14},{8,0},{10,2},{12,4},{14,6},{16,24},{18,... | collective-permute-start | bytes 1572872 | tf_op jit(solution)/shard_map/ppermute | solution.py:32
  341.0 2.7 collective-permute-start.38
  344.8 7.8 %collective-permute-start.39 = (bf16[512,1024]{1,0:T(8,128)(2,1)S(1)}, bf16[512,1024]{1,0:T(8,128)(2,1)S(1)}, u32[]{:S(2)}, u32[]{:S(2)}) collective-permute-start(bf16[512,1024]{1,0:T(8,128)(2,1)S(1)} %convolution_convert_fusion.2), channel_id=1, source_target_pairs={{0,2},{2,0},{4,6},{6,4},{8,10},{10,8},{12,14},{14,12},{16,18},{18,... | collective-permute-start | bytes 3145736 | tf_op jit(solution)/shard_map/ppermute | solution.py:32
  347.1 14.0 %collective-permute-start.40 = (bf16[256,1024]{1,0:T(8,128)(2,1)S(1)}, bf16[256,1024]{1,0:T(8,128)(2,1)S(1)}, u32[]{:S(2)}, u32[]{:S(2)}) collective-permute-start(bf16[256,1024]{1,0:T(8,128)(2,1)S(1)} %fusion.8), channel_id=1, source_target_pairs={{0,8},{2,10},{4,12},{6,14},{8,0},{10,2},{12,4},{14,6},{16,24},{18,... | collective-permute-start | bytes 1572872 | tf_op jit(solution)/shard_map/ppermute | solution.py:32
  362.9 17.8 %collective-permute-start.45 = (f32[512,1]{1,0:T(8,128)}, f32[512,1]{1,0:T(8,128)}, u32[]{:S(2)}, u32[]{:S(2)}) collective-permute-start(f32[512,1]{1,0:T(8,128)} %copy.15), channel_id=1, source_target_pairs={{0,2},{2,0},{4,6},{6,4},{8,10},{10,8},{12,14},{14,12},{16,18},{18,... | collective-permute-start | bytes 6152 | tf_op jit(solution)/shard_map/ppermute | solution.py:32
  362.9 19.0 %collective-permute-start.41 = (bf16[512,1024]{1,0:T(8,128)(2,1)}, bf16[512,1024]{1,0:T(8,128)(2,1)}, u32[]{:S(2)}, u32[]{:S(2)}) collective-permute-start(bf16[512,1024]{1,0:T(8,128)(2,1)} %convolution_convert_fusion.1), channel_id=1, source_target_pairs={{0,2},{2,0},{4,6},{6,4},{8,10},{10,8},{12,14},{14,12},{16,18},{18,... | collective-permute-start | bytes 3145736 | tf_op jit(solution)/shard_map/ppermute | solution.py:32
  363.4 21.8 %collective-permute-start.42 = (bf16[256,1024]{1,0:T(8,128)(2,1)}, bf16[256,1024]{1,0:T(8,128)(2,1)}, u32[]{:S(2)}, u32[]{:S(2)}) collective-permute-start(bf16[256,1024]{1,0:T(8,128)(2,1)} %fusion.9), channel_id=1, source_target_pairs={{0,8},{2,10},{4,12},{6,14},{8,0},{10,2},{12,4},{14,6},{16,24},{18,... | collective-permute-start | bytes 1572872 | tf_op jit(solution)/shard_map/ppermute | solution.py:32
  363.8 21.4 %collective-permute-start.43 = (bf16[256,1024]{1,0:T(8,128)(2,1)}, bf16[256,1024]{1,0:T(8,128)(2,1)}, u32[]{:S(2)}, u32[]{:S(2)}) collective-permute-start(bf16[256,1024]{1,0:T(8,128)(2,1)} %copy-done.65), channel_id=1, source_target_pairs={{1,0},{3,2},{5,4},{7,6},{9,8},{11,10},{13,12},{15,14},{16,17},{18,... | collective-permute-start | bytes 1572872 | tf_op jit(solution)/shard_map/ppermute | solution.py:850
  365.2 20.0 %collective-permute-start.44 = (bf16[256,1024]{1,0:T(8,128)(2,1)S(1)}, bf16[256,1024]{1,0:T(8,128)(2,1)}, u32[]{:S(2)}, u32[]{:S(2)}) collective-permute-start(bf16[256,1024]{1,0:T(8,128)(2,1)S(1)} %shard_map.153.refs_2_), channel_id=1, source_target_pairs={{0,1},{2,3},{4,5},{6,7},{8,9},{10,11},{12,13},{14,15},{17,16},{19,... | collective-permute-start | bytes 1572872 | tf_op jit(solution)/shard_map/ppermute | solution.py:850
  385.3 9.3 %collective-permute-start.46 = (bf16[512,1024]{1,0:T(8,128)(2,1)S(1)}, bf16[512,1024]{1,0:T(8,128)(2,1)S(1)}, u32[]{:S(2)}, u32[]{:S(2)}) collective-permute-start(bf16[512,1024]{1,0:T(8,128)(2,1)S(1)} %copy-done.94), channel_id=1, source_target_pairs={{0,2},{2,0},{4,6},{6,4},{8,10},{10,8},{12,14},{14,12},{16,18},{18,... | collective-permute-start | bytes 3145736 | tf_op jit(solution)/shard_map/ppermute | solution.py:32
  385.4 9.2 %collective-permute-start.49 = (f32[256,1]{1,0:T(8,128)S(1)}, f32[256,1]{1,0:T(8,128)S(1)}, u32[]{:S(2)}, u32[]{:S(2)}) collective-permute-start(f32[256,1]{1,0:T(8,128)S(1)} %get-tuple-element.496), channel_id=1, source_target_pairs={{0,8},{2,10},{4,12},{6,14},{8,0},{10,2},{12,4},{14,6},{16,24},{18,... | collective-permute-start | bytes 3080 | tf_op jit(solution)/shard_map/ppermute | solution.py:32
  386.9 15.6 %collective-permute-start.47 = (bf16[256,1024]{1,0:T(8,128)(2,1)S(1)}, bf16[256,1024]{1,0:T(8,128)(2,1)S(1)}, u32[]{:S(2)}, u32[]{:S(2)}) collective-permute-start(bf16[256,1024]{1,0:T(8,128)(2,1)S(1)} %fusion.10), channel_id=1, source_target_pairs={{0,8},{2,10},{4,12},{6,14},{8,0},{10,2},{12,4},{14,6},{16,24},{18,... | collective-permute-start | bytes 1572872 | tf_op jit(solution)/shard_map/ppermute | solution.py:32
  387.5 15.1 %collective-permute-start.48 = (bf16[256,1024]{1,0:T(8,128)(2,1)S(1)}, bf16[256,1024]{1,0:T(8,128)(2,1)S(1)}, u32[]{:S(2)}, u32[]{:S(2)}) collective-permute-start(bf16[256,1024]{1,0:T(8,128)(2,1)S(1)} %copy-done.69), channel_id=1, source_target_pairs={{0,1},{1,0},{2,3},{3,2},{4,5},{5,4},{6,7},{7,6},{8,9},{9,8},{10,11... | collective-permute-start | bytes 1572872 | tf_op jit(solution)/shard_map/ppermute | solution.py:36
  402.5 9.8 %collective-permute-start.52 = (bf16[512,1024]{1,0:T(8,128)(2,1)S(1)}, bf16[512,1024]{1,0:T(8,128)(2,1)S(1)}, u32[]{:S(2)}, u32[]{:S(2)}) collective-permute-start(bf16[512,1024]{1,0:T(8,128)(2,1)S(1)} %get-tuple-element.508), channel_id=1, source_target_pairs={{0,2},{2,0},{4,6},{6,4},{8,10},{10,8},{12,14},{14,12},{16,18},{18,... | collective-permute-start | bytes 3145736 | tf_op jit(solution)/shard_map/ppermute | solution.py:32
  402.5 9.8 %collective-permute-start.54 = (bf16[32,2048]{1,0:T(8,128)(2,1)S(1)}, bf16[32,2048]{1,0:T(8,128)(2,1)S(1)}, u32[]{:S(2)}, u32[]{:S(2)}) collective-permute-start(bf16[32,2048]{1,0:T(8,128)(2,1)S(1)} %convert_element_type.135), channel_id=1, source_target_pairs={{0,16},{2,18},{4,20},{6,22},{8,24},{10,26},{12,28},{14,30},{16,0},... | collective-permute-start | bytes 393224 | tf_op jit(solution)/shard_map/ppermute | solution.py:32
  403.1 7.4 %collective-permute-start.53 = (f32[256,1]{1,0:T(8,128)S(1)}, f32[256,1]{1,0:T(8,128)S(1)}, u32[]{:S(2)}, u32[]{:S(2)}) collective-permute-start(f32[256,1]{1,0:T(8,128)S(1)} %add.83), channel_id=1, source_target_pairs={{0,1},{1,0},{2,3},{3,2},{4,5},{5,4},{6,7},{7,6},{8,9},{9,8},{10,11... | collective-permute-start | bytes 3080 | tf_op jit(solution)/shard_map/ppermute | solution.py:36
  406.2 15.5 %collective-permute-start.50 = (bf16[256,1024]{1,0:T(8,128)(2,1)S(1)}, bf16[256,1024]{1,0:T(8,128)(2,1)S(1)}, u32[]{:S(2)}, u32[]{:S(2)}) collective-permute-start(bf16[256,1024]{1,0:T(8,128)(2,1)S(1)} %fusion.11), channel_id=1, source_target_pairs={{0,8},{2,10},{4,12},{6,14},{8,0},{10,2},{12,4},{14,6},{16,24},{18,... | collective-permute-start | bytes 1572872 | tf_op jit(solution)/shard_map/ppermute | solution.py:32
  406.6 15.1 %collective-permute-start.51 = (bf16[256,1024]{1,0:T(8,128)(2,1)S(1)}, bf16[256,1024]{1,0:T(8,128)(2,1)S(1)}, u32[]{:S(2)}, u32[]{:S(2)}) collective-permute-start(bf16[256,1024]{1,0:T(8,128)(2,1)S(1)} %fusion.6.refs_0_), channel_id=1, source_target_pairs={{0,1},{1,0},{2,3},{3,2},{4,5},{5,4},{6,7},{7,6},{8,9},{9,8},{10,11... | collective-permute-start | bytes 1572872 | tf_op jit(solution)/shard_map/ppermute | solution.py:36
  421.7 7.5 %collective-permute-start.57 = (f32[32,2048]{1,0:T(8,128)S(1)}, f32[32,2048]{1,0:T(8,128)S(1)}, u32[]{:S(2)}, u32[]{:S(2)}) collective-permute-start(f32[32,2048]{1,0:T(8,128)S(1)} %convert_add_fusion.1), channel_id=1, source_target_pairs={{0,4},{2,6},{4,0},{6,2},{8,12},{10,14},{12,8},{14,10},{16,20},{18,... | collective-permute-start | bytes 786440 | tf_op jit(solution)/shard_map/ppermute | solution.py:32
  422.4 12.8 %collective-permute-start.55 = (bf16[256,1024]{1,0:T(8,128)(2,1)S(1)}, bf16[256,1024]{1,0:T(8,128)(2,1)S(1)}, u32[]{:S(2)}, u32[]{:S(2)}) collective-permute-start(bf16[256,1024]{1,0:T(8,128)(2,1)S(1)} %fusion.5.refs_3_), channel_id=1, source_target_pairs={{0,1},{1,0},{2,3},{3,2},{4,5},{5,4},{6,7},{7,6},{8,9},{9,8},{10,11... | collective-permute-start | bytes 1572872 | tf_op jit(solution)/shard_map/ppermute | solution.py:36
  423.7 12.6 %collective-permute-start.56 = (bf16[256,1024]{1,0:T(8,128)(2,1)S(1)}, bf16[256,1024]{1,0:T(8,128)(2,1)S(1)}, u32[]{:S(2)}, u32[]{:S(2)}) collective-permute-start(bf16[256,1024]{1,0:T(8,128)(2,1)S(1)} %copy-done.80), channel_id=1, source_target_pairs={{0,8},{2,10},{4,12},{6,14},{8,0},{10,2},{12,4},{14,6},{16,24},{18,... | collective-permute-start | bytes 1572872 | tf_op jit(solution)/shard_map/ppermute | solution.py:32
  436.3 11.7 %collective-permute-start.58 = (bf16[256,1024]{1,0:T(8,128)(2,1)S(1)}, bf16[256,1024]{1,0:T(8,128)(2,1)S(1)}, u32[]{:S(2)}, u32[]{:S(2)}) collective-permute-start(bf16[256,1024]{1,0:T(8,128)(2,1)S(1)} %fusion.4.refs_2_), channel_id=1, source_target_pairs={{0,1},{1,0},{2,3},{3,2},{4,5},{5,4},{6,7},{7,6},{8,9},{9,8},{10,11... | collective-permute-start | bytes 1572872 | tf_op jit(solution)/shard_map/ppermute | solution.py:36
  436.9 11.4 %collective-permute-start.59 = (bf16[256,1024]{1,0:T(8,128)(2,1)S(1)}, bf16[256,1024]{1,0:T(8,128)(2,1)S(1)}, u32[]{:S(2)}, u32[]{:S(2)}) collective-permute-start(bf16[256,1024]{1,0:T(8,128)(2,1)S(1)} %get-tuple-element.546), channel_id=1, source_target_pairs={{0,8},{2,10},{4,12},{6,14},{8,0},{10,2},{12,4},{14,6},{16,24},{18,... | collective-permute-start | bytes 1572872 | tf_op jit(solution)/shard_map/ppermute | solution.py:32
  437.3 11.1 %collective-permute-start.60 = (f32[64,2048]{1,0:T(8,128)S(1)}, f32[64,2048]{1,0:T(8,128)S(1)}, u32[]{:S(2)}, u32[]{:S(2)}) collective-permute-start(f32[64,2048]{1,0:T(8,128)S(1)} %pad_maximum_fusion.1), channel_id=1, source_target_pairs={{0,2},{2,0},{4,6},{6,4},{8,10},{10,8},{12,14},{14,12},{16,18},{18,... | collective-permute-start | bytes 1572872 | tf_op jit(solution)/shard_map/ppermute | solution.py:32
  448.4 11.4 %collective-permute-start.62 = (bf16[256,1024]{1,0:T(8,128)(2,1)S(1)}, bf16[256,1024]{1,0:T(8,128)(2,1)S(1)}, u32[]{:S(2)}, u32[]{:S(2)}) collective-permute-start(bf16[256,1024]{1,0:T(8,128)(2,1)S(1)} %shard_map.157.refs_3_), channel_id=1, source_target_pairs={{0,1},{2,3},{4,5},{6,7},{8,9},{10,11},{12,13},{14,15},{17,16},{19,... | collective-permute-start | bytes 1572872 | tf_op jit(solution)/shard_map/ppermute | solution.py:850
  451.8 12.1 %collective-permute-start.61 = (bf16[256,1024]{1,0:T(8,128)(2,1)S(1)}, bf16[256,1024]{1,0:T(8,128)(2,1)S(1)}, u32[]{:S(2)}, u32[]{:S(2)}) collective-permute-start(bf16[256,1024]{1,0:T(8,128)(2,1)S(1)} %shard_map.156.refs_0_), channel_id=1, source_target_pairs={{1,0},{3,2},{5,4},{7,6},{9,8},{11,10},{13,12},{15,14},{16,17},{18,... | collective-permute-start | bytes 1572872 | tf_op jit(solution)/shard_map/ppermute | solution.py:850
  (100 other events, 902.7 us)

commit v4 on v3

--- a/solution.py
+++ b/solution.py
@@ -55,7 +55,7 @@
     )
 
 
-def call(body, cost=FREE, room=24, **settings):
+def call(body, cost=FREE, room=16, **settings):
     params = pltpu.CompilerParams(vmem_limit_bytes=room * MIB)
     return pl.pallas_call(body, compiler_params=params, cost_estimate=cost, **settings)
 
@@ -265,7 +265,7 @@
     return call(
         functools.partial(hidden_body, units),
         cost=work(8 * count * columns * tokens[0].shape[1]),
-        room=56,
+        room=44,
         grid=(4,),
         in_specs=[SMEM]
         + [pl.BlockSpec(t.shape, lambda i: (0, 0)) for t in tokens]
@@ -330,7 +330,7 @@
             act_body, units, len(places), depth, len(extra), int(slope is not None)
         ),
         cost=work(4 * count * columns * depth * len(places)),
-        room=36,
+        room=26,
         grid=(4,),
         in_specs=sum([token_specs(count, depth, step, p) for p in places], [])
         + [ANY] * len(units)
@@ -534,7 +534,7 @@
 
 
 def first_body(blocks, at, upper, *refs):
-    sums, got, out = refs[:4], refs[4:8], refs[8]
+    sums, got, out = refs[:4], (refs[5], refs[4], refs[4], refs[5]), refs[6]
     me, rank = at[0], at[1]
     share = out.shape[1]
     chunk = share // 2
@@ -638,6 +638,8 @@
     down = by_parity(down_weight, hop(send_columns(down_weight), 1))
     dz[0] = down[0]
     dy[0] = hop(down[0], 2)
+    low_rows, high_rows = slice(0, rows), slice(rows, 2 * rows)
+    down_parts = [[d[part] for part in (low_rows, high_rows)] for d in down]
     (
         squashed,
         adapter_pre_grad,
@@ -661,11 +663,12 @@
         adapter_down.T,
         adapter_up,
     )
-    up, down, uz, uy, dz, dy, normed_own, first_send, second_send, adapter_pre_grad, squashed = (
-        together(
-            up, down, uz, uy, dz, dy, normed_own, first_send, second_send, adapter_pre_grad,
-            squashed,
-        )
+    (
+        up, down_parts, uz, uy, dz, dy, normed_own, first_send, second_send, adapter_pre_grad,
+        squashed,
+    ) = together(
+        up, down_parts, uz, uy, dz, dy, normed_own, first_send, second_send, adapter_pre_grad,
+        squashed,
     )
 
     for s in far:
@@ -690,16 +693,17 @@
     keep = jnp.where(is_core, up_grad_part, down_grad_part)
     give = jnp.where(is_core, down_grad_part, up_grad_part).astype(jnp.bfloat16)
     normed_part = first_part[:, :share_width]
-    uz, uy, normed_part, first_part, sibling_own, up_chunks, down, second_send, keep, give = (
-        together(
-            uz, uy, normed_part, first_part, sibling_own, up_chunks, down, second_send, keep, give
-        )
-    )
-
-    low_rows, high_rows = slice(0, rows), slice(rows, 2 * rows)
+    (
+        uz, uy, normed_part, first_part, sibling_own, up_chunks, down_parts, second_send, keep,
+        give,
+    ) = together(
+        uz, uy, normed_part, first_part, sibling_own, up_chunks, down_parts, second_send, keep,
+        give,
+    )
+
     dzp = [[None, None] for _ in range(layers)]
     dyp = [[None, None] for _ in range(layers)]
-    dzp[2][0] = hop(down[0][low_rows], 2 << 2)
+    dzp[2][0] = hop(down_parts[0][0], 2 << 2)
     second_part = hop(second_send, 4)
     carried_part = jnp.concatenate([first_part[:, share_width:], second_part], axis=1)
     for s in far:
@@ -707,18 +711,17 @@
     normed_other = swap_mp(normed_part) if groups == 2 else normed_part
     sibling_part = hop(normed_part, 1) if groups == 2 else normed_part
     up_chunks = up_chunks + [stack(*units_of(uz[s], uy[s])) for s in (1, 2)]
-    downs = [[down[0][high_rows]], [down[1][low_rows]], [down[1][high_rows]]]
     (
-        dzp, uz, uy, carried_part, normed_part, normed_other, sibling_own, sibling_part, downs,
+        dzp, uz, uy, carried_part, normed_part, normed_other, sibling_own, sibling_part, down_parts,
         normed_own, carried_own, keep, give, up_chunks,
     ) = together(
-        dzp, uz, uy, carried_part, normed_part, normed_other, sibling_own, sibling_part, downs,
+        dzp, uz, uy, carried_part, normed_part, normed_other, sibling_own, sibling_part, down_parts,
         normed_own, carried_own, keep, give, up_chunks,
     )
-    [mine_high], [other_low], [other_high] = downs
+    (mine_low, mine_high), (other_low, other_high) = down_parts
 
     for s in far:
-        dzp[s][0] = hop(other_low if s & 1 else down[0][low_rows], s << 2)
+        dzp[s][0] = hop(other_low if s & 1 else mine_low, s << 2)
     dzp[1][0] = hop(other_low, 1 << 2)
     dyp[2][0] = hop(dzp[2][0], 2)
     carried_other = swap_mp(carried_part) if groups == 2 else carried_part
@@ -840,14 +843,10 @@
         got_low, core_low,
     )
 
-    def to_holder(value, p):
-        if not paired:
-            return value
-        moves = []
-        for i in range(size):
-            holder = ((i >> 3) ^ p) & 1
-            moves.append((2 * i + 1 - holder, 2 * i + holder))
-        return lax.ppermute(value, ("dp", "mp"), moves)
+    holds_low = ((mp_rank ^ (me >> 3)) & 1) == 0
+
+    def swap_held(low, high):
+        return swap_mp(jnp.where(holds_low, high, low))
 
     from_core[0] = hop(to_core[0], 1)
     to_pair[0] = pair_product(0)
@@ -856,7 +855,7 @@
         from_core, to_pair, to_core, pre_own, pre_pair, pre_other
     )
     high, pair_one, core_high, got_zero, got_high = [None] * 5
-    sum_one, sum_zero, sum_high, sent_zero, sent_one, sent_low, sent_high = [None] * 7
+    sum_one, sum_zero, sum_high, sent_zero, sent_one = [None] * 5
     stat = other = half = None
     for step in range(layers + 3):
         if step < layers:
@@ -884,9 +883,8 @@
                 )
             ]
         if step == 1:
-            sent_one = to_holder(sum_one, 0)
             if paired:
-                sent_low = to_holder(sum_low, 1)
+                sent_one = swap_held(sum_one, sum_low)
             stat_got = hop(stat[2], 1)
             stat = [stat[0] + stat_got[:tokens], stat[1] + stat_got[tokens:]]
         if step == 2:
@@ -910,19 +908,18 @@
             sum_zero = pair_add(core_zero[0], got_zero)
             other = hop(half, 1)
         if step == layers + 2:
-            sent_zero = to_holder(sum_zero, 0)
             if paired:
                 sum_high = pair_add(core_high[0], got_high, swapped=True)
-                sent_high = to_holder(sum_high, 1)
+                sent_zero = swap_held(sum_zero, sum_high)
             break
         state = (
             to_core, from_core, to_pair, from_pair, grad_mine, grad_got, high, pair_one, sum_low, core_high,
-            got_zero, got_high, sum_one, sum_zero, sent_one, sent_low, stat, share, other, half,
+            got_zero, got_high, sum_one, sum_zero, sent_one, stat, share, other, half,
             pre_own, pre_pair, pre_other, hidden_pre, activated, core_zero,
         )
         (
             to_core, from_core, to_pair, from_pair, grad_mine, grad_got, high, pair_one, sum_low, core_high,
-            got_zero, got_high, sum_one, sum_zero, sent_one, sent_low, stat, share, other, half,
+            got_zero, got_high, sum_one, sum_zero, sent_one, stat, share, other, half,
             pre_own, pre_pair, pre_other, hidden_pre, activated, core_zero,
         ) = together(*state)
     adapter_down_grad = jnp.where(is_core, other, half).T
@@ -938,7 +935,7 @@
             size,
             upper_slice,
             [sum_zero, sum_one, sum_low, sum_high],
-            [sent_zero, sent_one, sent_low, sent_high],
+            [sent_one, sent_zero],
         )
     else:
         width = chunk // 2

time: 473 us -> 467 us (0.987)
  starting transfers between devices: 58.7 us -> 50.9 us
  Pallas kernels: 104 us -> 99 us
    ppermute x4 -> x0, starting transfers between devices: 12.4 us -> none  [to_holder(): return lax.ppermute(value, ('dp', 'mp'), moves)]
    ppermute x4 -> x0, waiting for transfers between devices: 6.14 us -> none  [to_holder(): return lax.ppermute(value, ('dp', 'mp'), moves)]
    ppermute x7 -> x9, waiting for transfers between devices: 19.3 us -> 23.6 us  [swap_mp(): return lax.ppermute(value, 'mp', [(0, 1), (1, 0)])]
    ppermute x7 -> x9, starting transfers between devices: 7.04 us -> 10.8 us  [swap_mp(): return lax.ppermute(value, 'mp', [(0, 1), (1, 0)])]
    unnamed x202 -> x204, local copies, waits for them, and re-layouts: 30.7 us -> 31.4 us
  transfers between devices with their start and end apart: 63 -> 61, of which waited for: 27 -> 25; matrix products, arithmetic and copies ran while one was open for 9% -> 11% of each run, Pallas kernels for 21% -> 20%
where the time goes in v4:
time: 467 us; the launch traced here: 461 us
  waiting for transfers between devices  225 us (48%)
  Pallas kernels  99 us (21%)
  starting transfers between devices  50.9 us (11%)
  local copies, waits for them, and re-layouts  41.7 us (9%)
  matrix products  31.4 us (7%)
  other arithmetic  11.4 us (2%)
    ppermute x52, waiting for transfers between devices, hop(): return lax.ppermute(value, 'dp', [(i, i ^ bits) for i in range(size)])  201 us
    ppermute x52, starting transfers between devices, hop(): return lax.ppermute(value, 'dp', [(i, i ^ bits) for i in range(size)])  40.1 us
    unnamed x204, local copies, waits for them, and re-layouts  31.4 us
    dot_general x12, matrix products, dot_t(): lax.dot_general(left, right, (((1,), (1,)), ((), ())), preferred_element_...  29.7 us
    pallas_call x1, Pallas kernels, hidden_kernel(): call(functools.partial(hidden_body, units), cost=work(8 * count * columns...  24.1 us
    ppermute x9, waiting for transfers between devices, swap_mp(): return lax.ppermute(value, 'mp', [(0, 1), (1, 0)])  23.6 us
    pallas_call x4, Pallas kernels, out_kernel(): call(functools.partial(out_body, units), cost=work(2 * count * columns *...  21.7 us
    pallas_call x2, Pallas kernels, act_kernel(): call(functools.partial(act_body, units, len(places), depth, len(extra), i...  21.4 us
  transfers between devices with their start and end apart: 61, of which 25 were waited for; matrix products, arithmetic and copies ran while one was open for 11% of the time, Pallas kernels for 20%

profile of v4, /device:TPU:0, one launch (start us, length us, event | category | flops | bytes accessed | tf_op | source)
XLA Modules:
  0.0 461.2 jit_solution(8557484260504069920)
XLA Ops:
  2.7 2.8 collective-permute-done.got
  5.5 1.8 copy-done.13
  7.3 2.2 shard_map.136
  10.1 3.7 collective-permute-start.3
  15.3 1.6 collective-permute-start.2
  21.0 9.8 %shard_map.138 = (bf16[256,64]{1,0:T(8,128)(2,1)S(1)}, bf16[256,64]{1,0:T(8,128)(2,1)S(1)}, f32[256,128]{1,0:T(8,128)S(1)}, bf16[256,4096]{1,0:T(8,128)(2,1)S(1)...) custom-call(s32[2]{0:T(128)S(1)} %pad_add_fusion.at.refs_0_, ...), custom_call_target="tpu_custom_call" | custom-call | tf_op jit(solution)/shard_map/pallas_call | solution.py:123
  31.5 1.8 fusion.14
  34.6 42.5 %collective-permute-done.3.refs_0_.refs_15_.refs_17_ = bf16[512,1408]{1,0:T(8,128)(2,1)} collective-permute-done((bf16[512,1408]{1,0:T(8,128)(2,1)S(1)}, bf16[512,1408]{1,0:T(8,128)(2,1)}, u32[]{:S(2)}, u32[]{:S(2)}) %collective-permute-start.3) | collective-permute-done | bytes 1441824 | tf_op jit(solution)/shard_map/ppermute | solution.py:32
  81.0 1.8 collective-permute-start.6
  86.5 2.4 shard_map.139
  91.4 25.5 %collective-permute-done.9 = bf16[256,3072]{1,0:T(8,128)(2,1)} collective-permute-done((bf16[256,3072]{1,0:T(8,128)(2,1)}, bf16[256,3072]{1,0:T(8,128)(2,1)}, u32[]{:S(2)}, u32[]{:S(2)}) %collective-permute-start.9) | collective-permute-done | bytes 1572896 | tf_op jit(solution)/shard_map/ppermute | solution.py:32
  118.3 30.8 %collective-permute-done.6.refs_19_.refs_21_.refs_0_ = bf16[512,1408]{1,0:T(8,128)(2,1)} collective-permute-done((bf16[512,1408]{1,0:T(8,128)(2,1)}, bf16[512,1408]{1,0:T(8,128)(2,1)}, u32[]{:S(2)}, u32[]{:S(2)}) %collective-permute-start.6) | collective-permute-done | bytes 1441824 | tf_op jit(solution)/shard_map/ppermute | solution.py:32
  152.1 2.4 collective-permute-start.11
  155.6 2.3 shard_map.141
  157.9 1.5 copy-done.22
  159.5 2.3 shard_map.140
  161.8 1.6 copy-done.30
  163.4 13.4 %collective-permute-done.13 = bf16[256,1024]{1,0:T(8,128)(2,1)S(1)} collective-permute-done((bf16[256,1024]{1,0:T(8,128)(2,1)S(1)}, bf16[256,1024]{1,0:T(8,128)(2,1)S(1)}, u32[]{:S(2)}, u32[]{:S(2)}) %collective-permute-start.13) | collective-permute-done | bytes 524320 | tf_op jit(solution)/shard_map/ppermute | solution.py:32
  176.9 10.2 %collective-permute-done.11.refs_0_.refs_16_ = bf16[256,1408]{1,0:T(8,128)(2,1)S(1)} collective-permute-done((bf16[256,1408]{1,0:T(8,128)(2,1)S(1)}, bf16[256,1408]{1,0:T(8,128)(2,1)S(1)}, u32[]{:S(2)}, u32[]{:S(2)}) %collective-permute-start.11) | collective-permute-done | bytes 720928 | tf_op jit(solution)/shard_map/ppermute | solution.py:32
  188.8 1.8 collective-permute-start.17
  192.0 24.1 %shard_map.142 = (f32[1024,1408]{1,0:T(8,128)}, f32[1024,1408]{1,0:T(8,128)}, bf16[1024,1408]{1,0:T(8,128)(2,1)}) custom-call(s32[2]{0:T(128)S(1)} %copy-done.83, bf16[256,4096]{1,0:T(8,128)(2,1)} %get-tuple-element.343.refs_1_, bf16[256,2048]{1,0:T(8,128)(2,1)S(1)} %slice.84.refs_2_, bf16[256,2048]{1,0:T(8,128)(2,1)S(1)} %collective-permute-done.14.refs_3_, ...), custom_call_target="tpu_custom_call" | custom-call | flops 2952790016 | tf_op jit(solution)/shard_map/pallas_call | solution.py:265
  216.1 6.6 %collective-permute-done.17.refs_2_.refs_18_ = bf16[256,1408]{1,0:T(8,128)(2,1)} collective-permute-done((bf16[256,1408]{1,0:T(8,128)(2,1)S(1)}, bf16[256,1408]{1,0:T(8,128)(2,1)}, u32[]{:S(2)}, u32[]{:S(2)}) %collective-permute-start.17) | collective-permute-done | bytes 720928 | tf_op jit(solution)/shard_map/ppermute | solution.py:32
  224.5 1.6 collective-permute-start.21
  230.5 2.5 shard_map.145
  236.8 4.8 %shard_map.144 = (f32[512,1024]{1,0:T(8,128)S(1)}, bf16[512,1024]{1,0:T(8,128)(2,1)S(1)}) custom-call(bf16[1024,1408]{1,0:T(8,128)(2,1)S(1)} %copy-done, bf16[512,1408]{1,0:T(8,128)(2,1)S(1)} %copy-done.2, bf16[512,1408]{1,0:T(8,128)(2,1)S(1)} %copy-done.4, bf16[512,1408]{1,0:T(8,128)(2,1)S(1)} %copy-done.2, bf16[512,1408]{1,0:T(8,128)(2,1)S(1)} %copy-done.4), custom_call_target="tpu_custom_call" | custom-call | flops 738197504 | tf_op jit(solution)/shard_map/pallas_call | solution.py:469
  242.9 15.1 %collective-permute-done.21.refs_2_.refs_6_ = bf16[256,1408]{1,0:T(8,128)(2,1)S(1)} collective-permute-done((bf16[256,1408]{1,0:T(8,128)(2,1)}, bf16[256,1408]{1,0:T(8,128)(2,1)S(1)}, u32[]{:S(2)}, u32[]{:S(2)}) %collective-permute-start.21) | collective-permute-done | bytes 720928 | tf_op jit(solution)/shard_map/ppermute | solution.py:32
  258.0 3.0 collective-permute-done.22.refs_8_.refs_0_
  261.1 1.9 collective-permute-start.26
  265.0 5.4 %shard_map.146 = (f32[512,1024]{1,0:T(8,128)S(1)}, bf16[512,1024]{1,0:T(8,128)(2,1)S(1)}) custom-call(bf16[1024,1408]{1,0:T(8,128)(2,1)S(1)} %copy-done, bf16[256,1408]{1,0:T(8,128)(2,1)S(1)} %copy-done.19, bf16[256,1408]{1,0:T(8,128)(2,1)S(1)} %copy-done.21, bf16[256,1408]{1,0:T(8,128)(2,1)} %collective-permute-done.17.refs_2_.refs_18_, ...), custom_call_target="tpu_custom_call" | custom-call | flops 738197504 | tf_op jit(solution)/shard_map/pallas_call | solution.py:469
  270.4 13.0 %shard_map.147.refs_12_ = f32[1024,1408]{1,0:T(8,128)S(1)} custom-call(bf16[512,4096]{1,0:T(8,128)(2,1)S(1)} %shard_map.143.refs_0_.refs_2_.refs_4_.refs_6_.refs_8_, bf16[512,4096]{1,0:T(8,128)(2,1)S(1)} %collective-permute-done.29.refs_1_.refs_3_.refs_5_.refs_7_.refs_9_, bf16[512,4096]{1,0:T(8,128)(2,1)S(1)} %shard_map.143.refs_0_.refs_2_.refs_4_.refs_6_.refs_8_, ...), custom_call_target="tpu_custom_call" | custom-call | flops 1845493760 | tf_op jit(solution)/shard_map/pallas_call | solution.py:328
  283.4 13.2 %collective-permute-done.28.refs_9_.refs_1_ = bf16[256,1408]{1,0:T(8,128)(2,1)S(1)} collective-permute-done((bf16[256,1408]{1,0:T(8,128)(2,1)S(1)}, bf16[256,1408]{1,0:T(8,128)(2,1)S(1)}, u32[]{:S(2)}, u32[]{:S(2)}) %collective-permute-start.28) | collective-permute-done | bytes 720928 | tf_op jit(solution)/shard_map/ppermute | solution.py:32
  300.8 6.4 %shard_map.150 = (f32[512,1024]{1,0:T(8,128)S(1)}, bf16[512,1024]{1,0:T(8,128)(2,1)}) custom-call(bf16[1024,1408]{1,0:T(8,128)(2,1)S(1)} %copy-done, bf16[256,1408]{1,0:T(8,128)(2,1)} %collective-permute-done.16.refs_14_.refs_0_, bf16[256,1408]{1,0:T(8,128)(2,1)S(1)} %collective-permute-done.23.refs_15_.refs_1_, ...), custom_call_target="tpu_custom_call" | custom-call | flops 738197504 | tf_op jit(solution)/shard_map/pallas_call | solution.py:469
  308.5 9.5 %collective-permute-done.34 = bf16[32,2048]{1,0:T(8,128)(2,1)S(1)} collective-permute-done((bf16[32,2048]{1,0:T(8,128)(2,1)S(1)}, bf16[32,2048]{1,0:T(8,128)(2,1)S(1)}, u32[]{:S(2)}, u32[]{:S(2)}) %collective-permute-start.34) | collective-permute-done | bytes 131104 | tf_op jit(solution)/shard_map/ppermute | solution.py:32
  320.5 1.7 collective-permute-start.37
  322.2 8.4 %shard_map.151 = (bf16[256,1408]{1,0:T(8,128)(2,1)S(1)}, bf16[256,1408]{1,0:T(8,128)(2,1)S(1)}, bf16[512,1408]{1,0:T(8,128)(2,1)S(1)}) custom-call(bf16[512,4096]{1,0:T(8,128)(2,1)S(1)} %shard_map.143.refs_0_.refs_2_.refs_4_.refs_6_.refs_8_, bf16[512,4096]{1,0:T(8,128)(2,1)S(1)} %collective-permute-done.29.refs_1_.refs_3_.refs_5_.refs_7_.refs_9_, ...), custom_call_target="tpu_custom_call" | custom-call | flops 1107296256 | tf_op jit(solution)/shard_map/pallas_call | solution.py:328
  330.6 1.8 convolution_convert_fusion.3
  333.2 4.1 collective-permute-done.37.got
  337.4 2.8 convolution_convert_fusion.2
  340.2 1.8 fusion.8
  350.8 2.4 multiply_reduce_fusion
  353.2 2.8 convolution_convert_fusion.1
  356.1 2.9 multiply_reduce_fusion.1
  359.0 2.9 fusion.9
  361.9 2.5 collective-permute-done.40
  366.2 2.5 collective-permute-start.43
  369.3 5.0 %convolution_convert_fusion = bf16[512,1024]{1,0:T(8,128)(2,1)} fusion(bf16[512,1408]{1,0:T(8,128)(2,1)} %copy-done.52, bf16[1024,1408]{1,0:T(8,128)(2,1)} %copy-done.28), kind=kOutput, calls=%fused_computation.3 | convolution fusion | flops 1476919296 | bytes 5373952 | tf_op jit(solution)/shard_map/dot_general | solution.py:53
  374.3 3.1 fusion.7.refs_1_
  380.8 3.3 fusion.10
  384.3 1.7 collective-permute-start.48
  386.9 2.1 fusion.6.refs_0_
  389.0 5.1 %shard_map.154 = (f32[512,1024]{1,0:T(8,128)S(1)}, bf16[512,1024]{1,0:T(8,128)(2,1)S(1)}) custom-call(bf16[1024,1408]{1,0:T(8,128)(2,1)S(1)} %copy-done, bf16[256,1408]{1,0:T(8,128)(2,1)S(1)} %copy-done.35, bf16[256,1408]{1,0:T(8,128)(2,1)S(1)} %copy-done.39, bf16[256,1408]{1,0:T(8,128)(2,1)S(1)} %copy-done.37, bf16[256,1408]{1,0:T(8,128)(2,1)S(1)} %copy-done.41), custom_call_target="tpu_custom_call" | custom-call | flops 738197504 | tf_op jit(solution)/shard_map/pallas_call | solution.py:469
  395.2 6.2 %collective-permute-done.46 = bf16[256,1024]{1,0:T(8,128)(2,1)S(1)} collective-permute-done((bf16[256,1024]{1,0:T(8,128)(2,1)S(1)}, bf16[256,1024]{1,0:T(8,128)(2,1)S(1)}, u32[]{:S(2)}, u32[]{:S(2)}) %collective-permute-start.46) | collective-permute-done | bytes 524320 | tf_op jit(solution)/shard_map/ppermute | solution.py:32
  402.7 1.6 collective-permute-start.52
  406.4 2.7 collective-permute-done.52
  409.1 2.2 collective-permute-done.53
  411.5 8.2 %collective-permute-done.49 = bf16[256,1024]{1,0:T(8,128)(2,1)S(1)} collective-permute-done((bf16[256,1024]{1,0:T(8,128)(2,1)S(1)}, bf16[256,1024]{1,0:T(8,128)(2,1)S(1)}, u32[]{:S(2)}, u32[]{:S(2)}) %collective-permute-start.49) | collective-permute-done | bytes 524320 | tf_op jit(solution)/shard_map/ppermute | solution.py:32
  422.1 2.1 fusion.4.refs_2_
  424.2 3.0 collective-permute-done.56
  427.3 5.9 %collective-permute-done.54.refs_7_ = bf16[256,1024]{1,0:T(8,128)(2,1)S(1)} collective-permute-done((bf16[256,1024]{1,0:T(8,128)(2,1)S(1)}, bf16[256,1024]{1,0:T(8,128)(2,1)S(1)}, u32[]{:S(2)}, u32[]{:S(2)}) %collective-permute-start.54) | collective-permute-done | bytes 524320 | tf_op jit(solution)/shard_map/ppermute | solution.py:36
  435.7 10.5 %collective-permute-done.57.refs_6_ = bf16[256,1024]{1,0:T(8,128)(2,1)S(1)} collective-permute-done((bf16[256,1024]{1,0:T(8,128)(2,1)S(1)}, bf16[256,1024]{1,0:T(8,128)(2,1)S(1)}, u32[]{:S(2)}, u32[]{:S(2)}) %collective-permute-start.57) | collective-permute-done | bytes 524320 | tf_op jit(solution)/shard_map/ppermute | solution.py:36
  446.7 1.5 collective-permute-start.60
  448.2 3.6 shard_map.159
  452.8 4.6 collective-permute-done.60.refs_5_
  457.4 3.5 shard_map.158
  (332 shorter events, 77.5 us)
Async XLA Ops:
  2.1 3.4 collective-permute-start
  9.7 7.3 %collective-permute-start.1 = (bf16[256,2816]{1,0:T(8,128)(2,1)S(1)}, bf16[256,2816]{1,0:T(8,128)(2,1)S(1)}, u32[]{:S(2)}, u32[]{:S(2)}) collective-permute-start(bf16[256,2816]{1,0:T(8,128)(2,1)S(1)} %constant_dynamic-slice_fusion), channel_id=1, source_target_pairs={{0,2},{2,0},{4,6},{6,4},{8,10},{10,8},{12,14},{14,12},{16,18},{18,... | collective-permute-start | bytes 4325384 | tf_op jit(solution)/shard_map/ppermute | solution.py:32
  10.1 66.9 %collective-permute-start.3 = (bf16[512,1408]{1,0:T(8,128)(2,1)S(1)}, bf16[512,1408]{1,0:T(8,128)(2,1)}, u32[]{:S(2)}, u32[]{:S(2)}) collective-permute-start(bf16[512,1408]{1,0:T(8,128)(2,1)S(1)} %get-tuple-element.348.refs_0_.refs_7_.refs_9_), channel_id=1, source_target_pairs={{0,16},{2,18},{4,20},{6,22},{8,24},{10,26},{12,28},{14,30},{16,0},... | collective-permute-start | bytes 4325384 | tf_op jit(solution)/shard_map/ppermute | solution.py:32
  13.8 63.2 %collective-permute-start.4 = (bf16[512,1408]{1,0:T(8,128)(2,1)S(1)}, bf16[512,1408]{1,0:T(8,128)(2,1)S(1)}, u32[]{:S(2)}, u32[]{:S(2)}) collective-permute-start(bf16[512,1408]{1,0:T(8,128)(2,1)S(1)} %get-tuple-element.348.refs_0_.refs_7_.refs_9_), channel_id=1, source_target_pairs={{0,4},{2,6},{4,0},{6,2},{8,12},{10,14},{12,8},{14,10},{16,20},{18,... | collective-permute-start | bytes 4325384 | tf_op jit(solution)/shard_map/ppermute | solution.py:32
  15.3 63.3 %collective-permute-start.2 = (bf16[512,1408]{1,0:T(8,128)(2,1)}, bf16[512,1408]{1,0:T(8,128)(2,1)}, u32[]{:S(2)}, u32[]{:S(2)}) collective-permute-start(bf16[512,1408]{1,0:T(8,128)(2,1)} %get-tuple-element.310), channel_id=1, source_target_pairs={{0,8},{2,10},{4,12},{6,14},{8,0},{10,2},{12,4},{14,6},{16,24},{18,... | collective-permute-start | bytes 4325384 | tf_op jit(solution)/shard_map/ppermute | solution.py:32
  18.3 60.4 %collective-permute-start.5 = (bf16[512,1408]{1,0:T(8,128)(2,1)S(1)}, bf16[512,1408]{1,0:T(8,128)(2,1)S(1)}, u32[]{:S(2)}, u32[]{:S(2)}) collective-permute-start(bf16[512,1408]{1,0:T(8,128)(2,1)S(1)} %get-tuple-element.400.refs_0_.refs_2_.refs_10_.refs_12_), channel_id=1, source_target_pairs={{0,4},{2,6},{4,0},{6,2},{8,12},{10,14},{12,8},{14,10},{16,20},{18,... | collective-permute-start | bytes 4325384 | tf_op jit(solution)/shard_map/ppermute | solution.py:32
  79.8 69.3 %collective-permute-start.10 = (bf16[256,4096]{1,0:T(8,128)(2,1)}, bf16[256,4096]{1,0:T(8,128)(2,1)}, u32[]{:S(2)}, u32[]{:S(2)}) collective-permute-start(bf16[256,4096]{1,0:T(8,128)(2,1)} %get-tuple-element.343.refs_1_), channel_id=1, source_target_pairs={{0,2},{2,0},{4,6},{6,4},{8,10},{10,8},{12,14},{14,12},{16,18},{18,... | collective-permute-start | bytes 6291464 | tf_op jit(solution)/shard_map/ppermute | solution.py:32
  79.8 37.1 %collective-permute-start.9 = (bf16[256,3072]{1,0:T(8,128)(2,1)}, bf16[256,3072]{1,0:T(8,128)(2,1)}, u32[]{:S(2)}, u32[]{:S(2)}) collective-permute-start(bf16[256,3072]{1,0:T(8,128)(2,1)} %get-tuple-element.312), channel_id=1, source_target_pairs={{0,8},{2,10},{4,12},{6,14},{8,0},{10,2},{12,4},{14,6},{16,24},{18,... | collective-permute-start | bytes 4718600 | tf_op jit(solution)/shard_map/ppermute | solution.py:32
  81.0 68.1 %collective-permute-start.6 = (bf16[512,1408]{1,0:T(8,128)(2,1)}, bf16[512,1408]{1,0:T(8,128)(2,1)}, u32[]{:S(2)}, u32[]{:S(2)}) collective-permute-start(bf16[512,1408]{1,0:T(8,128)(2,1)} %get-tuple-element.310), channel_id=1, source_target_pairs={{0,24},{2,26},{4,28},{6,30},{8,16},{10,18},{12,20},{14,22},{16,8},... | collective-permute-start | bytes 4325384 | tf_op jit(solution)/shard_map/ppermute | solution.py:32
  82.8 66.3 %collective-permute-start.7 = (bf16[512,1408]{1,0:T(8,128)(2,1)}, bf16[512,1408]{1,0:T(8,128)(2,1)}, u32[]{:S(2)}, u32[]{:S(2)}) collective-permute-start(bf16[512,1408]{1,0:T(8,128)(2,1)} %collective-permute-done.2.refs_0_.refs_11_.refs_13_), channel_id=1, source_target_pairs={{0,4},{2,6},{4,0},{6,2},{8,12},{10,14},{12,8},{14,10},{16,20},{18,... | collective-permute-start | bytes 4325384 | tf_op jit(solution)/shard_map/ppermute | solution.py:32
  84.3 64.8 %collective-permute-start.8 = (bf16[512,1408]{1,0:T(8,128)(2,1)}, bf16[512,1408]{1,0:T(8,128)(2,1)}, u32[]{:S(2)}, u32[]{:S(2)}) collective-permute-start(bf16[512,1408]{1,0:T(8,128)(2,1)} %collective-permute-done.3.refs_0_.refs_15_.refs_17_), channel_id=1, source_target_pairs={{0,4},{2,6},{4,0},{6,2},{8,12},{10,14},{12,8},{14,10},{16,20},{18,... | collective-permute-start | bytes 4325384 | tf_op jit(solution)/shard_map/ppermute | solution.py:32
  90.7 61.4 %copy-start.88 = (bf16[256,1024]{1,0:T(8,128)(2,1)S(1)}, bf16[256,1024]{1,0:T(8,128)(2,1)}, u32[]{:S(2)}) copy-start(bf16[256,1024]{1,0:T(8,128)(2,1)} %copy-done.87) | copy-start | bytes 1572868
  90.7 61.4 %copy-start.94 = (bf16[256,1408]{1,0:T(8,128)(2,1)S(1)}, bf16[256,1408]{1,0:T(8,128)(2,1)}, u32[]{:S(2)}) copy-start(bf16[256,1408]{1,0:T(8,128)(2,1)} %get-tuple-element.321) | copy-start | bytes 2162692
  149.1 38.0 %collective-permute-start.12 = (bf16[512,1408]{1,0:T(8,128)(2,1)}, bf16[512,1408]{1,0:T(8,128)(2,1)S(1)}, u32[]{:S(2)}, u32[]{:S(2)}) collective-permute-start(bf16[512,1408]{1,0:T(8,128)(2,1)} %collective-permute-done.6.refs_19_.refs_21_.refs_0_), channel_id=1, source_target_pairs={{0,4},{2,6},{4,0},{6,2},{8,12},{10,14},{12,8},{14,10},{16,20},{18,... | collective-permute-start | bytes 4325384 | tf_op jit(solution)/shard_map/ppermute | solution.py:32
  150.6 36.5 %collective-permute-start.14 = (bf16[256,2048]{1,0:T(8,128)(2,1)S(1)}, bf16[256,2048]{1,0:T(8,128)(2,1)S(1)}, u32[]{:S(2)}, u32[]{:S(2)}) collective-permute-start(bf16[256,2048]{1,0:T(8,128)(2,1)S(1)} %slice.84.refs_2_), channel_id=1, source_target_pairs={{0,1},{1,0},{2,3},{3,2},{4,5},{5,4},{6,7},{7,6},{8,9},{9,8},{10,11... | collective-permute-start | bytes 3145736 | tf_op jit(solution)/shard_map/ppermute | solution.py:36
  152.1 35.0 %collective-permute-start.15 = (bf16[256,2048]{1,0:T(8,128)(2,1)S(1)}, bf16[256,2048]{1,0:T(8,128)(2,1)S(1)}, u32[]{:S(2)}, u32[]{:S(2)}) collective-permute-start(bf16[256,2048]{1,0:T(8,128)(2,1)S(1)} %slice.84.refs_2_), channel_id=1, source_target_pairs={{0,2},{2,0},{4,6},{6,4},{8,10},{10,8},{12,14},{14,12},{16,18},{18,... | collective-permute-start | bytes 3145736 | tf_op jit(solution)/shard_map/ppermute | solution.py:32
  152.1 24.7 %collective-permute-start.13 = (bf16[256,1024]{1,0:T(8,128)(2,1)S(1)}, bf16[256,1024]{1,0:T(8,128)(2,1)S(1)}, u32[]{:S(2)}, u32[]{:S(2)}) collective-permute-start(bf16[256,1024]{1,0:T(8,128)(2,1)S(1)} %copy-done.88), channel_id=1, source_target_pairs={{0,8},{2,10},{4,12},{6,14},{8,0},{10,2},{12,4},{14,6},{16,24},{18,... | collective-permute-start | bytes 1572872 | tf_op jit(solution)/shard_map/ppermute | solution.py:32
  152.1 35.0 %collective-permute-start.11 = (bf16[256,1408]{1,0:T(8,128)(2,1)S(1)}, bf16[256,1408]{1,0:T(8,128)(2,1)S(1)}, u32[]{:S(2)}, u32[]{:S(2)}) collective-permute-start(bf16[256,1408]{1,0:T(8,128)(2,1)S(1)} %copy-done.94), channel_id=1, source_target_pairs={{0,16},{2,18},{4,20},{6,22},{8,24},{10,26},{12,28},{14,30},{16,0},... | collective-permute-start | bytes 2162696 | tf_op jit(solution)/shard_map/ppermute | solution.py:32
  187.1 4.9 %collective-permute-start.20 = (bf16[256,2048]{1,0:T(8,128)(2,1)S(1)}, bf16[256,2048]{1,0:T(8,128)(2,1)S(1)}, u32[]{:S(2)}, u32[]{:S(2)}) collective-permute-start(bf16[256,2048]{1,0:T(8,128)(2,1)S(1)} %collective-permute-done.14.refs_3_), channel_id=1, source_target_pairs={{0,2},{2,0},{4,6},{6,4},{8,10},{10,8},{12,14},{14,12},{16,18},{18,... | collective-permute-start | bytes 3145736 | tf_op jit(solution)/shard_map/ppermute | solution.py:32
  187.2 36.4 %collective-permute-start.19 = (bf16[256,2048]{1,0:T(8,128)(2,1)S(1)}, bf16[256,2048]{1,0:T(8,128)(2,1)S(1)}, u32[]{:S(2)}, u32[]{:S(2)}) collective-permute-start(bf16[256,2048]{1,0:T(8,128)(2,1)S(1)} %pad_maximum_fusion.part), channel_id=1, source_target_pairs={{0,1},{1,0},{2,3},{3,2},{4,5},{5,4},{6,7},{7,6},{8,9},{9,8},{10,11... | collective-permute-start | bytes 3145736 | tf_op jit(solution)/shard_map/ppermute | solution.py:36
  188.8 27.3 %collective-permute-start.16 = (bf16[256,1408]{1,0:T(8,128)(2,1)S(1)}, bf16[256,1408]{1,0:T(8,128)(2,1)}, u32[]{:S(2)}, u32[]{:S(2)}) collective-permute-start(bf16[256,1408]{1,0:T(8,128)(2,1)S(1)} %copy-done.93), channel_id=1, source_target_pairs={{0,8},{2,10},{4,12},{6,14},{8,0},{10,2},{12,4},{14,6},{16,24},{18,... | collective-permute-start | bytes 2162696 | tf_op jit(solution)/shard_map/ppermute | solution.py:32
  188.8 33.9 %collective-permute-start.17 = (bf16[256,1408]{1,0:T(8,128)(2,1)S(1)}, bf16[256,1408]{1,0:T(8,128)(2,1)}, u32[]{:S(2)}, u32[]{:S(2)}) collective-permute-start(bf16[256,1408]{1,0:T(8,128)(2,1)S(1)} %copy-done.93), channel_id=1, source_target_pairs={{0,24},{2,26},{4,28},{6,30},{8,16},{10,18},{12,20},{14,22},{16,8},... | collective-permute-start | bytes 2162696 | tf_op jit(solution)/shard_map/ppermute | solution.py:32
  190.6 32.1 %collective-permute-start.18 = (bf16[256,1408]{1,0:T(8,128)(2,1)S(1)}, bf16[256,1408]{1,0:T(8,128)(2,1)S(1)}, u32[]{:S(2)}, u32[]{:S(2)}) collective-permute-start(bf16[256,1408]{1,0:T(8,128)(2,1)S(1)} %collective-permute-done.11.refs_0_.refs_16_), channel_id=1, source_target_pairs={{0,4},{2,6},{4,0},{6,2},{8,12},{10,14},{12,8},{14,10},{16,20},{18,... | collective-permute-start | bytes 2162696 | tf_op jit(solution)/shard_map/ppermute | solution.py:32
  224.5 17.2 %collective-permute-start.25 = (bf16[64,2048]{1,0:T(8,128)(2,1)}, bf16[64,2048]{1,0:T(8,128)(2,1)}, u32[]{:S(2)}, u32[]{:S(2)}) collective-permute-start(bf16[64,2048]{1,0:T(8,128)(2,1)} %select_convert_fusion), channel_id=1, source_target_pairs={{0,2},{2,0},{4,6},{6,4},{8,10},{10,8},{12,14},{14,12},{16,18},{18,... | collective-permute-start | bytes 786440 | tf_op jit(solution)/shard_map/ppermute | solution.py:32
  224.5 33.4 %collective-permute-start.21 = (bf16[256,1408]{1,0:T(8,128)(2,1)}, bf16[256,1408]{1,0:T(8,128)(2,1)S(1)}, u32[]{:S(2)}, u32[]{:S(2)}) collective-permute-start(bf16[256,1408]{1,0:T(8,128)(2,1)} %get-tuple-element.391), channel_id=1, source_target_pairs={{0,8},{2,10},{4,12},{6,14},{8,0},{10,2},{12,4},{14,6},{16,24},{18,... | collective-permute-start | bytes 2162696 | tf_op jit(solution)/shard_map/ppermute | solution.py:32
  226.1 34.9 %collective-permute-start.22 = (bf16[256,1408]{1,0:T(8,128)(2,1)}, bf16[256,1408]{1,0:T(8,128)(2,1)S(1)}, u32[]{:S(2)}, u32[]{:S(2)}) collective-permute-start(bf16[256,1408]{1,0:T(8,128)(2,1)} %get-tuple-element.368), channel_id=1, source_target_pairs={{0,16},{2,18},{4,20},{6,22},{8,24},{10,26},{12,28},{14,30},{16,0},... | collective-permute-start | bytes 2162696 | tf_op jit(solution)/shard_map/ppermute | solution.py:32
  227.1 33.9 %collective-permute-start.23 = (bf16[256,1408]{1,0:T(8,128)(2,1)}, bf16[256,1408]{1,0:T(8,128)(2,1)S(1)}, u32[]{:S(2)}, u32[]{:S(2)}) collective-permute-start(bf16[256,1408]{1,0:T(8,128)(2,1)} %collective-permute-done.16.refs_14_.refs_0_), channel_id=1, source_target_pairs={{0,4},{2,6},{4,0},{6,2},{8,12},{10,14},{12,8},{14,10},{16,20},{18,... | collective-permute-start | bytes 2162696 | tf_op jit(solution)/shard_map/ppermute | solution.py:32
  227.7 33.3 %collective-permute-start.24 = (bf16[256,1408]{1,0:T(8,128)(2,1)}, bf16[256,1408]{1,0:T(8,128)(2,1)S(1)}, u32[]{:S(2)}, u32[]{:S(2)}) collective-permute-start(bf16[256,1408]{1,0:T(8,128)(2,1)} %collective-permute-done.17.refs_2_.refs_18_), channel_id=1, source_target_pairs={{0,4},{2,6},{4,0},{6,2},{8,12},{10,14},{12,8},{14,10},{16,20},{18,... | collective-permute-start | bytes 2162696 | tf_op jit(solution)/shard_map/ppermute | solution.py:32
  261.0 61.2 %copy-start.34 = (bf16[256,1408]{1,0:T(8,128)(2,1)}, bf16[256,1408]{1,0:T(8,128)(2,1)S(1)}, u32[]{:S(2)}) copy-start(bf16[256,1408]{1,0:T(8,128)(2,1)S(1)} %collective-permute-done.22.refs_8_.refs_0_) | copy-start | bytes 2162692
  261.0 9.4 %collective-permute-start.29 = (bf16[512,4096]{1,0:T(8,128)(2,1)S(1)}, bf16[512,4096]{1,0:T(8,128)(2,1)S(1)}, u32[]{:S(2)}, u32[]{:S(2)}) collective-permute-start(bf16[512,4096]{1,0:T(8,128)(2,1)S(1)} %shard_map.143.refs_0_.refs_2_.refs_4_.refs_6_.refs_8_), channel_id=1, source_target_pairs={{0,2},{2,0},{4,6},{6,4},{8,10},{10,8},{12,14},{14,12},{16,18},{18,... | collective-permute-start | bytes 12582920 | tf_op jit(solution)/shard_map/ppermute | solution.py:32
  261.1 22.3 %collective-permute-start.26 = (bf16[256,1408]{1,0:T(8,128)(2,1)}, bf16[256,1408]{1,0:T(8,128)(2,1)S(1)}, u32[]{:S(2)}, u32[]{:S(2)}) collective-permute-start(bf16[256,1408]{1,0:T(8,128)(2,1)} %get-tuple-element.391), channel_id=1, source_target_pairs={{0,24},{2,26},{4,28},{6,30},{8,16},{10,18},{12,20},{14,22},{16,8},... | collective-permute-start | bytes 2162696 | tf_op jit(solution)/shard_map/ppermute | solution.py:32
  263.0 20.5 %collective-permute-start.27 = (bf16[256,1408]{1,0:T(8,128)(2,1)S(1)}, bf16[256,1408]{1,0:T(8,128)(2,1)S(1)}, u32[]{:S(2)}, u32[]{:S(2)}) collective-permute-start(bf16[256,1408]{1,0:T(8,128)(2,1)S(1)} %collective-permute-done.21.refs_2_.refs_6_), channel_id=1, source_target_pairs={{0,4},{2,6},{4,0},{6,2},{8,12},{10,14},{12,8},{14,10},{16,20},{18,... | collective-permute-start | bytes 2162696 | tf_op jit(solution)/shard_map/ppermute | solution.py:32
  263.5 33.1 %collective-permute-start.28 = (bf16[256,1408]{1,0:T(8,128)(2,1)S(1)}, bf16[256,1408]{1,0:T(8,128)(2,1)S(1)}, u32[]{:S(2)}, u32[]{:S(2)}) collective-permute-start(bf16[256,1408]{1,0:T(8,128)(2,1)S(1)} %collective-permute-done.22.refs_8_.refs_0_), channel_id=1, source_target_pairs={{0,4},{2,6},{4,0},{6,2},{8,12},{10,14},{12,8},{14,10},{16,20},{18,... | collective-permute-start | bytes 2162696 | tf_op jit(solution)/shard_map/ppermute | solution.py:32
  296.6 2.7 collective-permute-start.31
  296.6 21.4 %collective-permute-start.33 = (bf16[512,1024]{1,0:T(8,128)(2,1)S(1)}, bf16[512,1024]{1,0:T(8,128)(2,1)S(1)}, u32[]{:S(2)}, u32[]{:S(2)}) collective-permute-start(bf16[512,1024]{1,0:T(8,128)(2,1)S(1)} %get-tuple-element.417), channel_id=1, source_target_pairs={{0,2},{2,0},{4,6},{6,4},{8,10},{10,8},{12,14},{14,12},{16,18},{18,... | collective-permute-start | bytes 3145736 | tf_op jit(solution)/shard_map/ppermute | solution.py:32
  297.1 22.1 %collective-permute-start.30 = (bf16[256,1408]{1,0:T(8,128)(2,1)S(1)}, bf16[256,1408]{1,0:T(8,128)(2,1)S(1)}, u32[]{:S(2)}, u32[]{:S(2)}) collective-permute-start(bf16[256,1408]{1,0:T(8,128)(2,1)S(1)} %collective-permute-done.26.refs_10_.refs_2_), channel_id=1, source_target_pairs={{0,4},{2,6},{4,0},{6,2},{8,12},{10,14},{12,8},{14,10},{16,20},{18,... | collective-permute-start | bytes 2162696 | tf_op jit(solution)/shard_map/ppermute | solution.py:32
  297.7 20.3 %collective-permute-start.34 = (bf16[32,2048]{1,0:T(8,128)(2,1)S(1)}, bf16[32,2048]{1,0:T(8,128)(2,1)S(1)}, u32[]{:S(2)}, u32[]{:S(2)}) collective-permute-start(bf16[32,2048]{1,0:T(8,128)(2,1)S(1)} %select_convert_fusion.1), channel_id=1, source_target_pairs={{0,4},{2,6},{4,0},{6,2},{8,12},{10,14},{12,8},{14,10},{16,20},{18,... | collective-permute-start | bytes 393224 | tf_op jit(solution)/shard_map/ppermute | solution.py:32
  300.4 18.8 %collective-permute-start.32 = (bf16[256,1024]{1,0:T(8,128)(2,1)S(1)}, bf16[256,1024]{1,0:T(8,128)(2,1)S(1)}, u32[]{:S(2)}, u32[]{:S(2)}) collective-permute-start(bf16[256,1024]{1,0:T(8,128)(2,1)S(1)} %get-tuple-element.415), channel_id=1, source_target_pairs={{0,8},{2,10},{4,12},{6,14},{8,0},{10,2},{12,4},{14,6},{16,24},{18,... | collective-permute-start | bytes 1572872 | tf_op jit(solution)/shard_map/ppermute | solution.py:32
  320.0 17.2 %collective-permute-start.36 = (bf16[512,1024]{1,0:T(8,128)(2,1)}, bf16[512,1024]{1,0:T(8,128)(2,1)S(1)}, u32[]{:S(2)}, u32[]{:S(2)}) collective-permute-start(bf16[512,1024]{1,0:T(8,128)(2,1)} %get-tuple-element.438), channel_id=1, source_target_pairs={{0,2},{2,0},{4,6},{6,4},{8,10},{10,8},{12,14},{14,12},{16,18},{18,... | collective-permute-start | bytes 3145736 | tf_op jit(solution)/shard_map/ppermute | solution.py:32
  320.1 12.4 %collective-permute-start.35 = (bf16[32,2048]{1,0:T(8,128)(2,1)S(1)}, bf16[32,2048]{1,0:T(8,128)(2,1)S(1)}, u32[]{:S(2)}, u32[]{:S(2)}) collective-permute-start(bf16[32,2048]{1,0:T(8,128)(2,1)S(1)} %convert_element_type.110), channel_id=1, source_target_pairs={{0,8},{2,10},{4,12},{6,14},{8,0},{10,2},{12,4},{14,6},{16,24},{18,... | collective-permute-start | bytes 393224 | tf_op jit(solution)/shard_map/ppermute | solution.py:32
  320.5 16.8 %collective-permute-start.37 = (bf16[256,1024]{1,0:T(8,128)(2,1)S(1)}, bf16[256,1024]{1,0:T(8,128)(2,1)S(1)}, u32[]{:S(2)}, u32[]{:S(2)}) collective-permute-start(bf16[256,1024]{1,0:T(8,128)(2,1)S(1)} %get-tuple-element.439), channel_id=1, source_target_pairs={{0,8},{2,10},{4,12},{6,14},{8,0},{10,2},{12,4},{14,6},{16,24},{18,... | collective-permute-start | bytes 1572872 | tf_op jit(solution)/shard_map/ppermute | solution.py:32
  337.3 2.9 collective-permute-start.38
  342.0 17.0 %collective-permute-start.39 = (bf16[512,1024]{1,0:T(8,128)(2,1)}, bf16[512,1024]{1,0:T(8,128)(2,1)}, u32[]{:S(2)}, u32[]{:S(2)}) collective-permute-start(bf16[512,1024]{1,0:T(8,128)(2,1)} %convolution_convert_fusion.2), channel_id=1, source_target_pairs={{0,2},{2,0},{4,6},{6,4},{8,10},{10,8},{12,14},{14,12},{16,18},{18,... | collective-permute-start | bytes 3145736 | tf_op jit(solution)/shard_map/ppermute | solution.py:32
  350.5 14.0 %collective-permute-start.40 = (bf16[256,1024]{1,0:T(8,128)(2,1)S(1)}, bf16[256,1024]{1,0:T(8,128)(2,1)}, u32[]{:S(2)}, u32[]{:S(2)}) collective-permute-start(bf16[256,1024]{1,0:T(8,128)(2,1)S(1)} %copy-done.99), channel_id=1, source_target_pairs={{0,8},{2,10},{4,12},{6,14},{8,0},{10,2},{12,4},{14,6},{16,24},{18,... | collective-permute-start | bytes 1572872 | tf_op jit(solution)/shard_map/ppermute | solution.py:32
  365.3 14.3 %collective-permute-start.44 = (f32[512,1]{1,0:T(8,128)}, f32[512,1]{1,0:T(8,128)}, u32[]{:S(2)}, u32[]{:S(2)}) collective-permute-start(f32[512,1]{1,0:T(8,128)} %copy.15), channel_id=1, source_target_pairs={{0,2},{2,0},{4,6},{6,4},{8,10},{10,8},{12,14},{14,12},{16,18},{18,... | collective-permute-start | bytes 6152 | tf_op jit(solution)/shard_map/ppermute | solution.py:32
  366.2 18.0 %collective-permute-start.43 = (bf16[256,1024]{1,0:T(8,128)(2,1)}, bf16[256,1024]{1,0:T(8,128)(2,1)}, u32[]{:S(2)}, u32[]{:S(2)}) collective-permute-start(bf16[256,1024]{1,0:T(8,128)(2,1)} %broadcast_select_fusion.1), channel_id=1, source_target_pairs={{0,1},{1,0},{2,3},{3,2},{4,5},{5,4},{6,7},{7,6},{8,9},{9,8},{10,11... | collective-permute-start | bytes 1572872 | tf_op jit(solution)/shard_map/ppermute | solution.py:36
  368.7 12.1 %collective-permute-start.41 = (bf16[512,1024]{1,0:T(8,128)(2,1)}, bf16[512,1024]{1,0:T(8,128)(2,1)}, u32[]{:S(2)}, u32[]{:S(2)}) collective-permute-start(bf16[512,1024]{1,0:T(8,128)(2,1)} %convolution_convert_fusion.1), channel_id=1, source_target_pairs={{0,2},{2,0},{4,6},{6,4},{8,10},{10,8},{12,14},{14,12},{16,18},{18,... | collective-permute-start | bytes 3145736 | tf_op jit(solution)/shard_map/ppermute | solution.py:32
  368.9 15.2 %collective-permute-start.42 = (bf16[256,1024]{1,0:T(8,128)(2,1)}, bf16[256,1024]{1,0:T(8,128)(2,1)}, u32[]{:S(2)}, u32[]{:S(2)}) collective-permute-start(bf16[256,1024]{1,0:T(8,128)(2,1)} %fusion.9), channel_id=1, source_target_pairs={{0,8},{2,10},{4,12},{6,14},{8,0},{10,2},{12,4},{14,6},{16,24},{18,... | collective-permute-start | bytes 1572872 | tf_op jit(solution)/shard_map/ppermute | solution.py:32
  384.2 10.0 %collective-permute-start.45 = (bf16[512,1024]{1,0:T(8,128)(2,1)S(1)}, bf16[512,1024]{1,0:T(8,128)(2,1)S(1)}, u32[]{:S(2)}, u32[]{:S(2)}) collective-permute-start(bf16[512,1024]{1,0:T(8,128)(2,1)S(1)} %copy-done.98), channel_id=1, source_target_pairs={{0,2},{2,0},{4,6},{6,4},{8,10},{10,8},{12,14},{14,12},{16,18},{18,... | collective-permute-start | bytes 3145736 | tf_op jit(solution)/shard_map/ppermute | solution.py:32
  384.3 9.8 %collective-permute-start.48 = (f32[256,1]{1,0:T(8,128)S(1)}, f32[256,1]{1,0:T(8,128)S(1)}, u32[]{:S(2)}, u32[]{:S(2)}) collective-permute-start(f32[256,1]{1,0:T(8,128)S(1)} %get-tuple-element.498), channel_id=1, source_target_pairs={{0,8},{2,10},{4,12},{6,14},{8,0},{10,2},{12,4},{14,6},{16,24},{18,... | collective-permute-start | bytes 3080 | tf_op jit(solution)/shard_map/ppermute | solution.py:32
  386.0 15.4 %collective-permute-start.46 = (bf16[256,1024]{1,0:T(8,128)(2,1)S(1)}, bf16[256,1024]{1,0:T(8,128)(2,1)S(1)}, u32[]{:S(2)}, u32[]{:S(2)}) collective-permute-start(bf16[256,1024]{1,0:T(8,128)(2,1)S(1)} %fusion.10), channel_id=1, source_target_pairs={{0,8},{2,10},{4,12},{6,14},{8,0},{10,2},{12,4},{14,6},{16,24},{18,... | collective-permute-start | bytes 1572872 | tf_op jit(solution)/shard_map/ppermute | solution.py:32
  386.4 15.1 %collective-permute-start.47 = (bf16[256,1024]{1,0:T(8,128)(2,1)S(1)}, bf16[256,1024]{1,0:T(8,128)(2,1)S(1)}, u32[]{:S(2)}, u32[]{:S(2)}) collective-permute-start(bf16[256,1024]{1,0:T(8,128)(2,1)S(1)} %copy-done.75), channel_id=1, source_target_pairs={{0,1},{1,0},{2,3},{3,2},{4,5},{5,4},{6,7},{7,6},{8,9},{9,8},{10,11... | collective-permute-start | bytes 1572872 | tf_op jit(solution)/shard_map/ppermute | solution.py:36
  401.4 9.8 %collective-permute-start.51 = (bf16[512,1024]{1,0:T(8,128)(2,1)S(1)}, bf16[512,1024]{1,0:T(8,128)(2,1)S(1)}, u32[]{:S(2)}, u32[]{:S(2)}) collective-permute-start(bf16[512,1024]{1,0:T(8,128)(2,1)S(1)} %get-tuple-element.510), channel_id=1, source_target_pairs={{0,2},{2,0},{4,6},{6,4},{8,10},{10,8},{12,14},{14,12},{16,18},{18,... | collective-permute-start | bytes 3145736 | tf_op jit(solution)/shard_map/ppermute | solution.py:32
  401.5 9.8 %collective-permute-start.53 = (bf16[32,2048]{1,0:T(8,128)(2,1)S(1)}, bf16[32,2048]{1,0:T(8,128)(2,1)S(1)}, u32[]{:S(2)}, u32[]{:S(2)}) collective-permute-start(bf16[32,2048]{1,0:T(8,128)(2,1)S(1)} %convert_element_type.135), channel_id=1, source_target_pairs={{0,16},{2,18},{4,20},{6,22},{8,24},{10,26},{12,28},{14,30},{16,0},... | collective-permute-start | bytes 393224 | tf_op jit(solution)/shard_map/ppermute | solution.py:32
  402.7 6.3 %collective-permute-start.52 = (f32[256,1]{1,0:T(8,128)S(1)}, f32[256,1]{1,0:T(8,128)S(1)}, u32[]{:S(2)}, u32[]{:S(2)}) collective-permute-start(f32[256,1]{1,0:T(8,128)S(1)} %add.83), channel_id=1, source_target_pairs={{0,1},{1,0},{2,3},{3,2},{4,5},{5,4},{6,7},{7,6},{8,9},{9,8},{10,11... | collective-permute-start | bytes 3080 | tf_op jit(solution)/shard_map/ppermute | solution.py:36
  404.3 15.4 %collective-permute-start.49 = (bf16[256,1024]{1,0:T(8,128)(2,1)S(1)}, bf16[256,1024]{1,0:T(8,128)(2,1)S(1)}, u32[]{:S(2)}, u32[]{:S(2)}) collective-permute-start(bf16[256,1024]{1,0:T(8,128)(2,1)S(1)} %fusion.11), channel_id=1, source_target_pairs={{0,8},{2,10},{4,12},{6,14},{8,0},{10,2},{12,4},{14,6},{16,24},{18,... | collective-permute-start | bytes 1572872 | tf_op jit(solution)/shard_map/ppermute | solution.py:32
  404.6 15.1 %collective-permute-start.50 = (bf16[256,1024]{1,0:T(8,128)(2,1)S(1)}, bf16[256,1024]{1,0:T(8,128)(2,1)S(1)}, u32[]{:S(2)}, u32[]{:S(2)}) collective-permute-start(bf16[256,1024]{1,0:T(8,128)(2,1)S(1)} %fusion.6.refs_0_), channel_id=1, source_target_pairs={{0,1},{1,0},{2,3},{3,2},{4,5},{5,4},{6,7},{7,6},{8,9},{9,8},{10,11... | collective-permute-start | bytes 1572872 | tf_op jit(solution)/shard_map/ppermute | solution.py:36
  419.7 7.5 %collective-permute-start.56 = (f32[32,2048]{1,0:T(8,128)S(1)}, f32[32,2048]{1,0:T(8,128)S(1)}, u32[]{:S(2)}, u32[]{:S(2)}) collective-permute-start(f32[32,2048]{1,0:T(8,128)S(1)} %convert_add_fusion.1), channel_id=1, source_target_pairs={{0,4},{2,6},{4,0},{6,2},{8,12},{10,14},{12,8},{14,10},{16,20},{18,... | collective-permute-start | bytes 786440 | tf_op jit(solution)/shard_map/ppermute | solution.py:32
  420.4 12.8 %collective-permute-start.54 = (bf16[256,1024]{1,0:T(8,128)(2,1)S(1)}, bf16[256,1024]{1,0:T(8,128)(2,1)S(1)}, u32[]{:S(2)}, u32[]{:S(2)}) collective-permute-start(bf16[256,1024]{1,0:T(8,128)(2,1)S(1)} %fusion.5.refs_3_), channel_id=1, source_target_pairs={{0,1},{1,0},{2,3},{3,2},{4,5},{5,4},{6,7},{7,6},{8,9},{9,8},{10,11... | collective-permute-start | bytes 1572872 | tf_op jit(solution)/shard_map/ppermute | solution.py:36
  421.8 12.7 %collective-permute-start.55 = (bf16[256,1024]{1,0:T(8,128)(2,1)S(1)}, bf16[256,1024]{1,0:T(8,128)(2,1)S(1)}, u32[]{:S(2)}, u32[]{:S(2)}) collective-permute-start(bf16[256,1024]{1,0:T(8,128)(2,1)S(1)} %copy-done.86), channel_id=1, source_target_pairs={{0,8},{2,10},{4,12},{6,14},{8,0},{10,2},{12,4},{14,6},{16,24},{18,... | collective-permute-start | bytes 1572872 | tf_op jit(solution)/shard_map/ppermute | solution.py:32
  434.4 11.7 %collective-permute-start.57 = (bf16[256,1024]{1,0:T(8,128)(2,1)S(1)}, bf16[256,1024]{1,0:T(8,128)(2,1)S(1)}, u32[]{:S(2)}, u32[]{:S(2)}) collective-permute-start(bf16[256,1024]{1,0:T(8,128)(2,1)S(1)} %fusion.4.refs_2_), channel_id=1, source_target_pairs={{0,1},{1,0},{2,3},{3,2},{4,5},{5,4},{6,7},{7,6},{8,9},{9,8},{10,11... | collective-permute-start | bytes 1572872 | tf_op jit(solution)/shard_map/ppermute | solution.py:36
  434.9 11.6 %collective-permute-start.58 = (bf16[256,1024]{1,0:T(8,128)(2,1)S(1)}, bf16[256,1024]{1,0:T(8,128)(2,1)S(1)}, u32[]{:S(2)}, u32[]{:S(2)}) collective-permute-start(bf16[256,1024]{1,0:T(8,128)(2,1)S(1)} %get-tuple-element.546), channel_id=1, source_target_pairs={{0,8},{2,10},{4,12},{6,14},{8,0},{10,2},{12,4},{14,6},{16,24},{18,... | collective-permute-start | bytes 1572872 | tf_op jit(solution)/shard_map/ppermute | solution.py:32
  435.5 10.9 %collective-permute-start.59 = (f32[64,2048]{1,0:T(8,128)S(1)}, f32[64,2048]{1,0:T(8,128)S(1)}, u32[]{:S(2)}, u32[]{:S(2)}) collective-permute-start(f32[64,2048]{1,0:T(8,128)S(1)} %pad_maximum_fusion.1), channel_id=1, source_target_pairs={{0,2},{2,0},{4,6},{6,4},{8,10},{10,8},{12,14},{14,12},{16,18},{18,... | collective-permute-start | bytes 1572872 | tf_op jit(solution)/shard_map/ppermute | solution.py:32
  446.7 10.8 %collective-permute-start.60 = (bf16[256,1024]{1,0:T(8,128)(2,1)S(1)}, bf16[256,1024]{1,0:T(8,128)(2,1)S(1)}, u32[]{:S(2)}, u32[]{:S(2)}) collective-permute-start(bf16[256,1024]{1,0:T(8,128)(2,1)S(1)} %broadcast_select_fusion), channel_id=1, source_target_pairs={{0,1},{1,0},{2,3},{3,2},{4,5},{5,4},{6,7},{7,6},{8,9},{9,8},{10,11... | collective-permute-start | bytes 1572872 | tf_op jit(solution)/shard_map/ppermute | solution.py:36
  (99 other events, 641.3 us)

commit v5 on v4

--- a/solution.py
+++ b/solution.py
@@ -299,14 +299,18 @@
         def _():
             left = jnp.concatenate([t[...] for t in tokens[which::2]], axis=1)
             total = dot(left, held[...])
-            if extras > slope_given:
+            if extras:
                 total = total + refs[count][...]
             if slope_given:
-                total = total * refs[count + extras - 1][...]
-            out[...] = total.astype(out.dtype)
-
-
-def act_kernel(tokens, spans, partial, slope=None):
+                total = total * refs[count + 1][...]
+            rounded = total.astype(out.dtype)
+            out[...] = rounded
+            if slope_given:
+                product = refs[count + 2][...] * rounded.astype(jnp.float32)
+                outs[-1][...] = jnp.sum(product, axis=1, keepdims=True)
+
+
+def act_kernel(tokens, spans, partial, slope=None, hidden=None):
     count, width = tokens[0].shape
     units = [u for _, us in spans for u in us]
     depth = 2 * units[0][2]
@@ -316,15 +320,17 @@
     columns = units[0][0].shape[1]
     step = count // 2
     out = pl.BlockSpec((step, columns), lambda i: (i, 0))
-    extra = [a for a in (partial, slope) if a is not None]
+    extra = [a for a in (partial, slope, hidden) if a is not None]
     if slope is None:
         out_specs, out_shape = out, jax.ShapeDtypeStruct((2 * count, columns), jnp.float32)
     else:
         own = pl.BlockSpec((step, columns), lambda i: (0, 0))
         out_specs = [own, own, token_specs(count, columns, step, 0)[1]]
+        out_specs.append(pl.BlockSpec((step, 1), lambda i: (i, 0)))
         out_shape = [
             jax.ShapeDtypeStruct((r, columns), jnp.bfloat16) for r in (step, step, count)
         ]
+        out_shape.append(jax.ShapeDtypeStruct((2 * count, 1), jnp.float32))
     return call(
         functools.partial(
             act_body, units, len(places), depth, len(extra), int(slope is not None)
@@ -800,11 +806,12 @@
         dyp, core_zero, got_one, core_low, out_one, share
     )
 
-    pre_own, pre_pair, pre_other = act_kernel(
+    pre_own, pre_pair, pre_other, stat = act_kernel(
         carried_both,
         [(s * chunk + chunk // 2, unit(s, 1)) for s in range(1, layers)],
         partial,
         slope,
+        hidden_pre,
     )
 
     def other_product(s):
@@ -836,10 +843,10 @@
     got_low = hop(core_low[1], 4)
     one_got = hop(out_one[1], 1)
     (
-        pre_own, pre_pair, pre_other, to_core, hidden_pre, share, activated, out_one, one_got,
+        pre_own, pre_pair, pre_other, to_core, stat, share, activated, out_one, one_got,
         got_low, core_low,
     ) = together(
-        pre_own, pre_pair, pre_other, to_core, hidden_pre, share, activated, out_one, one_got,
+        pre_own, pre_pair, pre_other, to_core, stat, share, activated, out_one, one_got,
         got_low, core_low,
     )
 
@@ -856,7 +863,7 @@
     )
     high, pair_one, core_high, got_zero, got_high = [None] * 5
     sum_one, sum_zero, sum_high, sent_zero, sent_one = [None] * 5
-    stat = other = half = None
+    other = half = None
     for step in range(layers + 3):
         if step < layers:
             from_pair[step ^ 1] = hop(to_pair[step], 4)
@@ -874,14 +881,7 @@
         if step == 0:
             sum_low = pair_add(core_low[0], got_low, swapped=True) if paired else None
             sum_one, pair_one = whole_add(out_one[0], one_got, got_one)
-            stat = [
-                jnp.sum(hidden_pre[first:last] * rows_of.astype(jnp.float32), axis=1)[:, None]
-                for first, last, rows_of in (
-                    (0, tokens, pre_own),
-                    (tokens, 2 * tokens, pre_pair),
-                    (2 * tokens, 4 * tokens, pre_other),
-                )
-            ]
+            stat = [stat[:tokens], stat[tokens : 2 * tokens], stat[2 * tokens :]]
         if step == 1:
             if paired:
                 sent_one = swap_held(sum_one, sum_low)
@@ -915,12 +915,12 @@
         state = (
             to_core, from_core, to_pair, from_pair, grad_mine, grad_got, high, pair_one, sum_low, core_high,
             got_zero, got_high, sum_one, sum_zero, sent_one, stat, share, other, half,
-            pre_own, pre_pair, pre_other, hidden_pre, activated, core_zero,
+            pre_own, pre_pair, pre_other, activated, core_zero,
         )
         (
             to_core, from_core, to_pair, from_pair, grad_mine, grad_got, high, pair_one, sum_low, core_high,
             got_zero, got_high, sum_one, sum_zero, sent_one, stat, share, other, half,
-            pre_own, pre_pair, pre_other, hidden_pre, activated, core_zero,
+            pre_own, pre_pair, pre_other, activated, core_zero,
         ) = together(*state)
     adapter_down_grad = jnp.where(is_core, other, half).T
     adapter_up_grad = jnp.where(is_core, half, other)

time: 467 us -> 458 us (0.981)
  waiting for transfers between devices: 225 us -> 235 us
  matrix products: 31.4 us -> 22.7 us
  other arithmetic: 11.4 us -> 4.21 us
    dot_general x12, matrix products: 29.7 us -> 21 us  [dot_t(): lax.dot_general(left, right, (((1,), (1,)), ((), ())), preferred_element_...]
    ppermute x52, waiting for transfers between devices: 201 us -> 206 us  [hop(): return lax.ppermute(value, 'dp', [(i, i ^ bits) for i in range(size)])]
    reduce_sum x2 -> x0, other arithmetic: 5.32 us -> none  [on_device(): jnp.sum(hidden_pre[first:last] * rows_of.astype(jnp.float32), axis=1)]
    ppermute x9, waiting for transfers between devices: 23.6 us -> 28.3 us  [swap_mp(): return lax.ppermute(value, 'mp', [(0, 1), (1, 0)])]
    unnamed x204 -> x176, local copies, waits for them, and re-layouts: 31.4 us -> 29.4 us
  transfers between devices with their start and end apart: 61 -> 61, of which waited for: 25 -> 27; matrix products, arithmetic and copies ran while one was open for 11% -> 7% of each run, Pallas kernels for 20% -> 21%
where the time goes in v5:
time: 458 us; the launch traced here: 453 us
  waiting for transfers between devices  235 us (51%)
  Pallas kernels  99.6 us (22%)
  starting transfers between devices  52 us (11%)
  local copies, waits for them, and re-layouts  37.6 us (8%)
  matrix products  22.7 us (5%)
    ppermute x52, waiting for transfers between devices, hop(): return lax.ppermute(value, 'dp', [(i, i ^ bits) for i in range(size)])  206 us
    ppermute x52, starting transfers between devices, hop(): return lax.ppermute(value, 'dp', [(i, i ^ bits) for i in range(size)])  42.6 us
    unnamed x176, local copies, waits for them, and re-layouts  29.4 us
    ppermute x9, waiting for transfers between devices, swap_mp(): return lax.ppermute(value, 'mp', [(0, 1), (1, 0)])  28.3 us
    pallas_call x1, Pallas kernels, hidden_kernel(): call(functools.partial(hidden_body, units), cost=work(8 * count * columns...  24 us
    pallas_call x2, Pallas kernels, act_kernel(): call(functools.partial(act_body, units, len(places), depth, len(extra), i...  23 us
    pallas_call x4, Pallas kernels, out_kernel(): call(functools.partial(out_body, units), cost=work(2 * count * columns *...  21.7 us
    dot_general x12, matrix products, dot_t(): lax.dot_general(left, right, (((1,), (1,)), ((), ())), preferred_element_...  21 us
  transfers between devices with their start and end apart: 61, of which 27 were waited for; matrix products, arithmetic and copies ran while one was open for 7% of the time, Pallas kernels for 21%

profile of v5, /device:TPU:0, one launch (start us, length us, event | category | flops | bytes accessed | tf_op | source)
XLA Modules:
  0.0 452.8 jit_solution(18380860219085971863)
XLA Ops:
  2.7 2.8 collective-permute-done.got
  5.5 1.8 copy-done.13
  7.3 2.2 shard_map.136
  10.1 3.7 collective-permute-start.3
  13.9 1.5 collective-permute-start.4
  15.4 1.6 collective-permute-start.2
  21.1 9.8 %shard_map.138 = (bf16[256,64]{1,0:T(8,128)(2,1)S(1)}, bf16[256,64]{1,0:T(8,128)(2,1)S(1)}, f32[256,128]{1,0:T(8,128)S(1)}, bf16[256,4096]{1,0:T(8,128)(2,1)S(1)...) custom-call(s32[2]{0:T(128)S(1)} %pad_add_fusion.at.refs_0_, ...), custom_call_target="tpu_custom_call" | custom-call | tf_op jit(solution)/shard_map/pallas_call | solution.py:123
  33.7 1.7 fusion.14
  36.0 41.1 %collective-permute-done.3.refs_0_.refs_15_.refs_17_ = bf16[512,1408]{1,0:T(8,128)(2,1)} collective-permute-done((bf16[512,1408]{1,0:T(8,128)(2,1)S(1)}, bf16[512,1408]{1,0:T(8,128)(2,1)}, u32[]{:S(2)}, u32[]{:S(2)}) %collective-permute-start.3) | collective-permute-done | bytes 1441824 | tf_op jit(solution)/shard_map/ppermute | solution.py:32
  81.1 1.8 collective-permute-start.6
  86.6 2.4 shard_map.139
  91.5 25.5 %collective-permute-done.9 = bf16[256,3072]{1,0:T(8,128)(2,1)} collective-permute-done((bf16[256,3072]{1,0:T(8,128)(2,1)}, bf16[256,3072]{1,0:T(8,128)(2,1)}, u32[]{:S(2)}, u32[]{:S(2)}) %collective-permute-start.9) | collective-permute-done | bytes 1572896 | tf_op jit(solution)/shard_map/ppermute | solution.py:32
  118.3 30.8 %collective-permute-done.6.refs_19_.refs_21_.refs_0_ = bf16[512,1408]{1,0:T(8,128)(2,1)} collective-permute-done((bf16[512,1408]{1,0:T(8,128)(2,1)}, bf16[512,1408]{1,0:T(8,128)(2,1)}, u32[]{:S(2)}, u32[]{:S(2)}) %collective-permute-start.6) | collective-permute-done | bytes 1441824 | tf_op jit(solution)/shard_map/ppermute | solution.py:32
  150.7 1.5 collective-permute-start.14
  152.2 2.4 collective-permute-start.11
  155.6 2.3 shard_map.141
  158.0 1.6 copy-done.22
  159.6 2.3 shard_map.140
  161.9 1.5 copy-done.27
  163.5 13.4 %collective-permute-done.13 = bf16[256,1024]{1,0:T(8,128)(2,1)S(1)} collective-permute-done((bf16[256,1024]{1,0:T(8,128)(2,1)S(1)}, bf16[256,1024]{1,0:T(8,128)(2,1)S(1)}, u32[]{:S(2)}, u32[]{:S(2)}) %collective-permute-start.13) | collective-permute-done | bytes 524320 | tf_op jit(solution)/shard_map/ppermute | solution.py:32
  177.0 10.2 %collective-permute-done.11.refs_0_.refs_16_ = bf16[256,1408]{1,0:T(8,128)(2,1)S(1)} collective-permute-done((bf16[256,1408]{1,0:T(8,128)(2,1)S(1)}, bf16[256,1408]{1,0:T(8,128)(2,1)S(1)}, u32[]{:S(2)}, u32[]{:S(2)}) %collective-permute-start.11) | collective-permute-done | bytes 720928 | tf_op jit(solution)/shard_map/ppermute | solution.py:32
  188.9 1.8 collective-permute-start.17
  192.1 24.0 %shard_map.142 = (f32[1024,1408]{1,0:T(8,128)}, f32[1024,1408]{1,0:T(8,128)}, bf16[1024,1408]{1,0:T(8,128)(2,1)}) custom-call(s32[2]{0:T(128)S(1)} %copy-done.69, bf16[256,4096]{1,0:T(8,128)(2,1)} %get-tuple-element.344.refs_1_, bf16[256,2048]{1,0:T(8,128)(2,1)S(1)} %slice.84.refs_2_, bf16[256,2048]{1,0:T(8,128)(2,1)S(1)} %collective-permute-done.14.refs_3_, ...), custom_call_target="tpu_custom_call" | custom-call | flops 2952790016 | tf_op jit(solution)/shard_map/pallas_call | solution.py:265
  216.1 6.7 %collective-permute-done.17.refs_2_.refs_18_ = bf16[256,1408]{1,0:T(8,128)(2,1)} collective-permute-done((bf16[256,1408]{1,0:T(8,128)(2,1)S(1)}, bf16[256,1408]{1,0:T(8,128)(2,1)}, u32[]{:S(2)}, u32[]{:S(2)}) %collective-permute-start.17) | collective-permute-done | bytes 720928 | tf_op jit(solution)/shard_map/ppermute | solution.py:32
  224.6 1.6 collective-permute-start.21
  230.6 2.5 shard_map.145
  236.9 4.9 %shard_map.144 = (f32[512,1024]{1,0:T(8,128)S(1)}, bf16[512,1024]{1,0:T(8,128)(2,1)S(1)}) custom-call(bf16[1024,1408]{1,0:T(8,128)(2,1)S(1)} %copy-done, bf16[512,1408]{1,0:T(8,128)(2,1)S(1)} %copy-done.2, bf16[512,1408]{1,0:T(8,128)(2,1)S(1)} %copy-done.4, bf16[512,1408]{1,0:T(8,128)(2,1)S(1)} %copy-done.2, bf16[512,1408]{1,0:T(8,128)(2,1)S(1)} %copy-done.4), custom_call_target="tpu_custom_call" | custom-call | flops 738197504 | tf_op jit(solution)/shard_map/pallas_call | solution.py:475
  243.0 15.1 %collective-permute-done.21.refs_2_.refs_6_ = bf16[256,1408]{1,0:T(8,128)(2,1)S(1)} collective-permute-done((bf16[256,1408]{1,0:T(8,128)(2,1)}, bf16[256,1408]{1,0:T(8,128)(2,1)S(1)}, u32[]{:S(2)}, u32[]{:S(2)}) %collective-permute-start.21) | collective-permute-done | bytes 720928 | tf_op jit(solution)/shard_map/ppermute | solution.py:32
  258.1 3.0 collective-permute-done.22.refs_8_.refs_0_
  261.2 1.9 collective-permute-start.26
  265.1 5.4 %shard_map.146 = (f32[512,1024]{1,0:T(8,128)S(1)}, bf16[512,1024]{1,0:T(8,128)(2,1)S(1)}) custom-call(bf16[1024,1408]{1,0:T(8,128)(2,1)S(1)} %copy-done, bf16[256,1408]{1,0:T(8,128)(2,1)S(1)} %copy-done.19, bf16[256,1408]{1,0:T(8,128)(2,1)S(1)} %copy-done.21, bf16[256,1408]{1,0:T(8,128)(2,1)} %collective-permute-done.17.refs_2_.refs_18_, ...), custom_call_target="tpu_custom_call" | custom-call | flops 738197504 | tf_op jit(solution)/shard_map/pallas_call | solution.py:475
  270.5 13.0 %shard_map.147.refs_12_ = f32[1024,1408]{1,0:T(8,128)S(1)} custom-call(bf16[512,4096]{1,0:T(8,128)(2,1)S(1)} %shard_map.143.refs_0_.refs_2_.refs_4_.refs_6_.refs_8_, bf16[512,4096]{1,0:T(8,128)(2,1)S(1)} %collective-permute-done.29.refs_1_.refs_3_.refs_5_.refs_7_.refs_9_, bf16[512,4096]{1,0:T(8,128)(2,1)S(1)} %shard_map.143.refs_0_.refs_2_.refs_4_.refs_6_.refs_8_, ...), custom_call_target="tpu_custom_call" | custom-call | flops 1845493760 | tf_op jit(solution)/shard_map/pallas_call | solution.py:334
  283.5 13.2 %collective-permute-done.28.refs_9_.refs_1_ = bf16[256,1408]{1,0:T(8,128)(2,1)S(1)} collective-permute-done((bf16[256,1408]{1,0:T(8,128)(2,1)S(1)}, bf16[256,1408]{1,0:T(8,128)(2,1)S(1)}, u32[]{:S(2)}, u32[]{:S(2)}) %collective-permute-start.28) | collective-permute-done | bytes 720928 | tf_op jit(solution)/shard_map/ppermute | solution.py:32
  300.9 6.4 %shard_map.150 = (f32[512,1024]{1,0:T(8,128)S(1)}, bf16[512,1024]{1,0:T(8,128)(2,1)}) custom-call(bf16[1024,1408]{1,0:T(8,128)(2,1)S(1)} %copy-done, bf16[256,1408]{1,0:T(8,128)(2,1)} %collective-permute-done.16.refs_14_.refs_0_, bf16[256,1408]{1,0:T(8,128)(2,1)S(1)} %collective-permute-done.23.refs_15_.refs_1_, ...), custom_call_target="tpu_custom_call" | custom-call | flops 738197504 | tf_op jit(solution)/shard_map/pallas_call | solution.py:475
  308.6 9.5 %collective-permute-done.34 = bf16[32,2048]{1,0:T(8,128)(2,1)S(1)} collective-permute-done((bf16[32,2048]{1,0:T(8,128)(2,1)S(1)}, bf16[32,2048]{1,0:T(8,128)(2,1)S(1)}, u32[]{:S(2)}, u32[]{:S(2)}) %collective-permute-start.34) | collective-permute-done | bytes 131104 | tf_op jit(solution)/shard_map/ppermute | solution.py:32
  319.8 1.7 collective-permute-start.37
  321.5 10.1 %shard_map.151 = (bf16[256,1408]{1,0:T(8,128)(2,1)S(1)}, bf16[256,1408]{1,0:T(8,128)(2,1)S(1)}, bf16[512,1408]{1,0:T(8,128)(2,1)S(1)}, f32[1024,1]{1,0:T(8,128)S(1)}) custom-call(bf16[512,4096]{1,0:T(8,128)(2,1)S(1)} %shard_map.143.refs_0_.refs_2_.refs_4_.refs_6_.refs_8_, ...), custom_call_target="tpu_custom_call" | custom-call | flops 1107296256 | tf_op jit(solution)/shard_map/pallas_call | solution.py:334
  331.7 1.8 convolution_convert_fusion.3
  334.2 2.4 collective-permute-done.37.got
  336.7 2.8 convolution_convert_fusion.2
  339.6 1.8 fusion.8
  348.7 3.3 convolution_convert_fusion.1
  352.1 2.2 fusion.9
  354.3 7.4 %collective-permute-done.40 = bf16[256,1024]{1,0:T(8,128)(2,1)S(1)} collective-permute-done((bf16[256,1024]{1,0:T(8,128)(2,1)S(1)}, bf16[256,1024]{1,0:T(8,128)(2,1)S(1)}, u32[]{:S(2)}, u32[]{:S(2)}) %collective-permute-start.40) | collective-permute-done | bytes 524320 | tf_op jit(solution)/shard_map/ppermute | solution.py:32
  361.7 1.6 collective-permute-start.43
  363.9 1.8 convolution_convert_fusion
  365.7 2.1 fusion.7.refs_1_
  368.9 7.2 %collective-permute-done.43.refs_4_ = bf16[256,1024]{1,0:T(8,128)(2,1)S(1)} collective-permute-done((bf16[256,1024]{1,0:T(8,128)(2,1)S(1)}, bf16[256,1024]{1,0:T(8,128)(2,1)S(1)}, u32[]{:S(2)}, u32[]{:S(2)}) %collective-permute-start.43) | collective-permute-done | bytes 524320 | tf_op jit(solution)/shard_map/ppermute | solution.py:36
  376.1 1.5 collective-permute-done.42
  378.1 1.7 collective-permute-start.46
  381.4 5.1 %shard_map.154 = (f32[512,1024]{1,0:T(8,128)S(1)}, bf16[512,1024]{1,0:T(8,128)(2,1)S(1)}) custom-call(bf16[1024,1408]{1,0:T(8,128)(2,1)S(1)} %copy-done, bf16[256,1408]{1,0:T(8,128)(2,1)S(1)} %copy-done.33, bf16[256,1408]{1,0:T(8,128)(2,1)S(1)} %copy-done.37, bf16[256,1408]{1,0:T(8,128)(2,1)S(1)} %copy-done.35, bf16[256,1408]{1,0:T(8,128)(2,1)S(1)} %copy-done.39), custom_call_target="tpu_custom_call" | custom-call | flops 738197504 | tf_op jit(solution)/shard_map/pallas_call | solution.py:475
  387.6 7.3 %collective-permute-done.46 = bf16[256,1024]{1,0:T(8,128)(2,1)S(1)} collective-permute-done((bf16[256,1024]{1,0:T(8,128)(2,1)S(1)}, bf16[256,1024]{1,0:T(8,128)(2,1)S(1)}, u32[]{:S(2)}, u32[]{:S(2)}) %collective-permute-start.46) | collective-permute-done | bytes 524320 | tf_op jit(solution)/shard_map/ppermute | solution.py:32
  396.3 1.7 collective-permute-start.49
  398.1 1.5 collective-permute-start.50
  400.6 1.5 collective-permute-done.52
  402.1 2.3 collective-permute-done.53
  404.7 8.2 %collective-permute-done.49 = bf16[256,1024]{1,0:T(8,128)(2,1)S(1)} collective-permute-done((bf16[256,1024]{1,0:T(8,128)(2,1)S(1)}, bf16[256,1024]{1,0:T(8,128)(2,1)S(1)}, u32[]{:S(2)}, u32[]{:S(2)}) %collective-permute-start.49) | collective-permute-done | bytes 524320 | tf_op jit(solution)/shard_map/ppermute | solution.py:32
  416.6 3.7 collective-permute-done.56
  420.4 5.9 %collective-permute-done.54.refs_7_ = bf16[256,1024]{1,0:T(8,128)(2,1)S(1)} collective-permute-done((bf16[256,1024]{1,0:T(8,128)(2,1)S(1)}, bf16[256,1024]{1,0:T(8,128)(2,1)S(1)}, u32[]{:S(2)}, u32[]{:S(2)}) %collective-permute-start.54) | collective-permute-done | bytes 524320 | tf_op jit(solution)/shard_map/ppermute | solution.py:36
  428.0 1.7 collective-permute-start.58
  429.9 8.8 %collective-permute-done.57.refs_6_ = bf16[256,1024]{1,0:T(8,128)(2,1)S(1)} collective-permute-done((bf16[256,1024]{1,0:T(8,128)(2,1)S(1)}, bf16[256,1024]{1,0:T(8,128)(2,1)S(1)}, u32[]{:S(2)}, u32[]{:S(2)}) %collective-permute-start.57) | collective-permute-done | bytes 524320 | tf_op jit(solution)/shard_map/ppermute | solution.py:36
  440.7 3.6 shard_map.159
  445.4 4.8 %collective-permute-done.60.refs_5_ = bf16[256,1024]{1,0:T(8,128)(2,1)S(1)} collective-permute-done((bf16[256,1024]{1,0:T(8,128)(2,1)S(1)}, bf16[256,1024]{1,0:T(8,128)(2,1)S(1)}, u32[]{:S(2)}, u32[]{:S(2)}) %collective-permute-start.60) | collective-permute-done | bytes 524320 | tf_op jit(solution)/shard_map/ppermute | solution.py:36
  450.2 2.4 shard_map.158
  (301 shorter events, 72.2 us)
Async XLA Ops:
  2.1 3.4 collective-permute-start
  9.7 7.3 %collective-permute-start.1 = (bf16[256,2816]{1,0:T(8,128)(2,1)S(1)}, bf16[256,2816]{1,0:T(8,128)(2,1)S(1)}, u32[]{:S(2)}, u32[]{:S(2)}) collective-permute-start(bf16[256,2816]{1,0:T(8,128)(2,1)S(1)} %constant_dynamic-slice_fusion), channel_id=1, source_target_pairs={{0,2},{2,0},{4,6},{6,4},{8,10},{10,8},{12,14},{14,12},{16,18},{18,... | collective-permute-start | bytes 4325384 | tf_op jit(solution)/shard_map/ppermute | solution.py:32
  10.1 66.9 %collective-permute-start.3 = (bf16[512,1408]{1,0:T(8,128)(2,1)S(1)}, bf16[512,1408]{1,0:T(8,128)(2,1)}, u32[]{:S(2)}, u32[]{:S(2)}) collective-permute-start(bf16[512,1408]{1,0:T(8,128)(2,1)S(1)} %get-tuple-element.349.refs_0_.refs_7_.refs_9_), channel_id=1, source_target_pairs={{0,16},{2,18},{4,20},{6,22},{8,24},{10,26},{12,28},{14,30},{16,0},... | collective-permute-start | bytes 4325384 | tf_op jit(solution)/shard_map/ppermute | solution.py:32
  13.9 63.2 %collective-permute-start.4 = (bf16[512,1408]{1,0:T(8,128)(2,1)S(1)}, bf16[512,1408]{1,0:T(8,128)(2,1)S(1)}, u32[]{:S(2)}, u32[]{:S(2)}) collective-permute-start(bf16[512,1408]{1,0:T(8,128)(2,1)S(1)} %get-tuple-element.349.refs_0_.refs_7_.refs_9_), channel_id=1, source_target_pairs={{0,4},{2,6},{4,0},{6,2},{8,12},{10,14},{12,8},{14,10},{16,20},{18,... | collective-permute-start | bytes 4325384 | tf_op jit(solution)/shard_map/ppermute | solution.py:32
  15.4 63.3 %collective-permute-start.2 = (bf16[512,1408]{1,0:T(8,128)(2,1)}, bf16[512,1408]{1,0:T(8,128)(2,1)}, u32[]{:S(2)}, u32[]{:S(2)}) collective-permute-start(bf16[512,1408]{1,0:T(8,128)(2,1)} %get-tuple-element.311), channel_id=1, source_target_pairs={{0,8},{2,10},{4,12},{6,14},{8,0},{10,2},{12,4},{14,6},{16,24},{18,... | collective-permute-start | bytes 4325384 | tf_op jit(solution)/shard_map/ppermute | solution.py:32
  18.3 60.4 %collective-permute-start.5 = (bf16[512,1408]{1,0:T(8,128)(2,1)S(1)}, bf16[512,1408]{1,0:T(8,128)(2,1)S(1)}, u32[]{:S(2)}, u32[]{:S(2)}) collective-permute-start(bf16[512,1408]{1,0:T(8,128)(2,1)S(1)} %get-tuple-element.401.refs_0_.refs_2_.refs_10_.refs_12_), channel_id=1, source_target_pairs={{0,4},{2,6},{4,0},{6,2},{8,12},{10,14},{12,8},{14,10},{16,20},{18,... | collective-permute-start | bytes 4325384 | tf_op jit(solution)/shard_map/ppermute | solution.py:32
  79.9 69.3 %collective-permute-start.10 = (bf16[256,4096]{1,0:T(8,128)(2,1)}, bf16[256,4096]{1,0:T(8,128)(2,1)}, u32[]{:S(2)}, u32[]{:S(2)}) collective-permute-start(bf16[256,4096]{1,0:T(8,128)(2,1)} %get-tuple-element.344.refs_1_), channel_id=1, source_target_pairs={{0,2},{2,0},{4,6},{6,4},{8,10},{10,8},{12,14},{14,12},{16,18},{18,... | collective-permute-start | bytes 6291464 | tf_op jit(solution)/shard_map/ppermute | solution.py:32
  79.9 37.1 %collective-permute-start.9 = (bf16[256,3072]{1,0:T(8,128)(2,1)}, bf16[256,3072]{1,0:T(8,128)(2,1)}, u32[]{:S(2)}, u32[]{:S(2)}) collective-permute-start(bf16[256,3072]{1,0:T(8,128)(2,1)} %get-tuple-element.313), channel_id=1, source_target_pairs={{0,8},{2,10},{4,12},{6,14},{8,0},{10,2},{12,4},{14,6},{16,24},{18,... | collective-permute-start | bytes 4718600 | tf_op jit(solution)/shard_map/ppermute | solution.py:32
  81.1 68.1 %collective-permute-start.6 = (bf16[512,1408]{1,0:T(8,128)(2,1)}, bf16[512,1408]{1,0:T(8,128)(2,1)}, u32[]{:S(2)}, u32[]{:S(2)}) collective-permute-start(bf16[512,1408]{1,0:T(8,128)(2,1)} %get-tuple-element.311), channel_id=1, source_target_pairs={{0,24},{2,26},{4,28},{6,30},{8,16},{10,18},{12,20},{14,22},{16,8},... | collective-permute-start | bytes 4325384 | tf_op jit(solution)/shard_map/ppermute | solution.py:32
  82.9 66.3 %collective-permute-start.7 = (bf16[512,1408]{1,0:T(8,128)(2,1)}, bf16[512,1408]{1,0:T(8,128)(2,1)}, u32[]{:S(2)}, u32[]{:S(2)}) collective-permute-start(bf16[512,1408]{1,0:T(8,128)(2,1)} %collective-permute-done.2.refs_0_.refs_11_.refs_13_), channel_id=1, source_target_pairs={{0,4},{2,6},{4,0},{6,2},{8,12},{10,14},{12,8},{14,10},{16,20},{18,... | collective-permute-start | bytes 4325384 | tf_op jit(solution)/shard_map/ppermute | solution.py:32
  84.4 64.8 %collective-permute-start.8 = (bf16[512,1408]{1,0:T(8,128)(2,1)}, bf16[512,1408]{1,0:T(8,128)(2,1)}, u32[]{:S(2)}, u32[]{:S(2)}) collective-permute-start(bf16[512,1408]{1,0:T(8,128)(2,1)} %collective-permute-done.3.refs_0_.refs_15_.refs_17_), channel_id=1, source_target_pairs={{0,4},{2,6},{4,0},{6,2},{8,12},{10,14},{12,8},{14,10},{16,20},{18,... | collective-permute-start | bytes 4325384 | tf_op jit(solution)/shard_map/ppermute | solution.py:32
  90.8 61.4 %copy-start.77 = (bf16[256,1024]{1,0:T(8,128)(2,1)S(1)}, bf16[256,1024]{1,0:T(8,128)(2,1)}, u32[]{:S(2)}) copy-start(bf16[256,1024]{1,0:T(8,128)(2,1)} %copy-done.76) | copy-start | bytes 1572868
  90.8 61.4 %copy-start.81 = (bf16[256,1408]{1,0:T(8,128)(2,1)S(1)}, bf16[256,1408]{1,0:T(8,128)(2,1)}, u32[]{:S(2)}) copy-start(bf16[256,1408]{1,0:T(8,128)(2,1)} %get-tuple-element.322) | copy-start | bytes 2162692
  149.2 38.0 %collective-permute-start.12 = (bf16[512,1408]{1,0:T(8,128)(2,1)}, bf16[512,1408]{1,0:T(8,128)(2,1)S(1)}, u32[]{:S(2)}, u32[]{:S(2)}) collective-permute-start(bf16[512,1408]{1,0:T(8,128)(2,1)} %collective-permute-done.6.refs_19_.refs_21_.refs_0_), channel_id=1, source_target_pairs={{0,4},{2,6},{4,0},{6,2},{8,12},{10,14},{12,8},{14,10},{16,20},{18,... | collective-permute-start | bytes 4325384 | tf_op jit(solution)/shard_map/ppermute | solution.py:32
  150.7 36.5 %collective-permute-start.14 = (bf16[256,2048]{1,0:T(8,128)(2,1)S(1)}, bf16[256,2048]{1,0:T(8,128)(2,1)S(1)}, u32[]{:S(2)}, u32[]{:S(2)}) collective-permute-start(bf16[256,2048]{1,0:T(8,128)(2,1)S(1)} %slice.84.refs_2_), channel_id=1, source_target_pairs={{0,1},{1,0},{2,3},{3,2},{4,5},{5,4},{6,7},{7,6},{8,9},{9,8},{10,11... | collective-permute-start | bytes 3145736 | tf_op jit(solution)/shard_map/ppermute | solution.py:36
  152.2 35.0 %collective-permute-start.15 = (bf16[256,2048]{1,0:T(8,128)(2,1)S(1)}, bf16[256,2048]{1,0:T(8,128)(2,1)S(1)}, u32[]{:S(2)}, u32[]{:S(2)}) collective-permute-start(bf16[256,2048]{1,0:T(8,128)(2,1)S(1)} %slice.84.refs_2_), channel_id=1, source_target_pairs={{0,2},{2,0},{4,6},{6,4},{8,10},{10,8},{12,14},{14,12},{16,18},{18,... | collective-permute-start | bytes 3145736 | tf_op jit(solution)/shard_map/ppermute | solution.py:32
  152.2 24.7 %collective-permute-start.13 = (bf16[256,1024]{1,0:T(8,128)(2,1)S(1)}, bf16[256,1024]{1,0:T(8,128)(2,1)S(1)}, u32[]{:S(2)}, u32[]{:S(2)}) collective-permute-start(bf16[256,1024]{1,0:T(8,128)(2,1)S(1)} %copy-done.77), channel_id=1, source_target_pairs={{0,8},{2,10},{4,12},{6,14},{8,0},{10,2},{12,4},{14,6},{16,24},{18,... | collective-permute-start | bytes 1572872 | tf_op jit(solution)/shard_map/ppermute | solution.py:32
  152.2 35.0 %collective-permute-start.11 = (bf16[256,1408]{1,0:T(8,128)(2,1)S(1)}, bf16[256,1408]{1,0:T(8,128)(2,1)S(1)}, u32[]{:S(2)}, u32[]{:S(2)}) collective-permute-start(bf16[256,1408]{1,0:T(8,128)(2,1)S(1)} %copy-done.81), channel_id=1, source_target_pairs={{0,16},{2,18},{4,20},{6,22},{8,24},{10,26},{12,28},{14,30},{16,0},... | collective-permute-start | bytes 2162696 | tf_op jit(solution)/shard_map/ppermute | solution.py:32
  187.2 4.9 %collective-permute-start.20 = (bf16[256,2048]{1,0:T(8,128)(2,1)S(1)}, bf16[256,2048]{1,0:T(8,128)(2,1)S(1)}, u32[]{:S(2)}, u32[]{:S(2)}) collective-permute-start(bf16[256,2048]{1,0:T(8,128)(2,1)S(1)} %collective-permute-done.14.refs_3_), channel_id=1, source_target_pairs={{0,2},{2,0},{4,6},{6,4},{8,10},{10,8},{12,14},{14,12},{16,18},{18,... | collective-permute-start | bytes 3145736 | tf_op jit(solution)/shard_map/ppermute | solution.py:32
  187.3 36.4 %collective-permute-start.19 = (bf16[256,2048]{1,0:T(8,128)(2,1)S(1)}, bf16[256,2048]{1,0:T(8,128)(2,1)S(1)}, u32[]{:S(2)}, u32[]{:S(2)}) collective-permute-start(bf16[256,2048]{1,0:T(8,128)(2,1)S(1)} %pad_maximum_fusion.part), channel_id=1, source_target_pairs={{0,1},{1,0},{2,3},{3,2},{4,5},{5,4},{6,7},{7,6},{8,9},{9,8},{10,11... | collective-permute-start | bytes 3145736 | tf_op jit(solution)/shard_map/ppermute | solution.py:36
  188.9 27.3 %collective-permute-start.16 = (bf16[256,1408]{1,0:T(8,128)(2,1)S(1)}, bf16[256,1408]{1,0:T(8,128)(2,1)}, u32[]{:S(2)}, u32[]{:S(2)}) collective-permute-start(bf16[256,1408]{1,0:T(8,128)(2,1)S(1)} %copy-done.80), channel_id=1, source_target_pairs={{0,8},{2,10},{4,12},{6,14},{8,0},{10,2},{12,4},{14,6},{16,24},{18,... | collective-permute-start | bytes 2162696 | tf_op jit(solution)/shard_map/ppermute | solution.py:32
  188.9 33.9 %collective-permute-start.17 = (bf16[256,1408]{1,0:T(8,128)(2,1)S(1)}, bf16[256,1408]{1,0:T(8,128)(2,1)}, u32[]{:S(2)}, u32[]{:S(2)}) collective-permute-start(bf16[256,1408]{1,0:T(8,128)(2,1)S(1)} %copy-done.80), channel_id=1, source_target_pairs={{0,24},{2,26},{4,28},{6,30},{8,16},{10,18},{12,20},{14,22},{16,8},... | collective-permute-start | bytes 2162696 | tf_op jit(solution)/shard_map/ppermute | solution.py:32
  190.7 32.1 %collective-permute-start.18 = (bf16[256,1408]{1,0:T(8,128)(2,1)S(1)}, bf16[256,1408]{1,0:T(8,128)(2,1)S(1)}, u32[]{:S(2)}, u32[]{:S(2)}) collective-permute-start(bf16[256,1408]{1,0:T(8,128)(2,1)S(1)} %collective-permute-done.11.refs_0_.refs_16_), channel_id=1, source_target_pairs={{0,4},{2,6},{4,0},{6,2},{8,12},{10,14},{12,8},{14,10},{16,20},{18,... | collective-permute-start | bytes 2162696 | tf_op jit(solution)/shard_map/ppermute | solution.py:32
  224.6 17.2 %collective-permute-start.25 = (bf16[64,2048]{1,0:T(8,128)(2,1)}, bf16[64,2048]{1,0:T(8,128)(2,1)}, u32[]{:S(2)}, u32[]{:S(2)}) collective-permute-start(bf16[64,2048]{1,0:T(8,128)(2,1)} %select_convert_fusion), channel_id=1, source_target_pairs={{0,2},{2,0},{4,6},{6,4},{8,10},{10,8},{12,14},{14,12},{16,18},{18,... | collective-permute-start | bytes 786440 | tf_op jit(solution)/shard_map/ppermute | solution.py:32
  224.6 33.4 %collective-permute-start.21 = (bf16[256,1408]{1,0:T(8,128)(2,1)}, bf16[256,1408]{1,0:T(8,128)(2,1)S(1)}, u32[]{:S(2)}, u32[]{:S(2)}) collective-permute-start(bf16[256,1408]{1,0:T(8,128)(2,1)} %get-tuple-element.392), channel_id=1, source_target_pairs={{0,8},{2,10},{4,12},{6,14},{8,0},{10,2},{12,4},{14,6},{16,24},{18,... | collective-permute-start | bytes 2162696 | tf_op jit(solution)/shard_map/ppermute | solution.py:32
  226.2 34.9 %collective-permute-start.22 = (bf16[256,1408]{1,0:T(8,128)(2,1)}, bf16[256,1408]{1,0:T(8,128)(2,1)S(1)}, u32[]{:S(2)}, u32[]{:S(2)}) collective-permute-start(bf16[256,1408]{1,0:T(8,128)(2,1)} %get-tuple-element.369), channel_id=1, source_target_pairs={{0,16},{2,18},{4,20},{6,22},{8,24},{10,26},{12,28},{14,30},{16,0},... | collective-permute-start | bytes 2162696 | tf_op jit(solution)/shard_map/ppermute | solution.py:32
  227.2 33.9 %collective-permute-start.23 = (bf16[256,1408]{1,0:T(8,128)(2,1)}, bf16[256,1408]{1,0:T(8,128)(2,1)S(1)}, u32[]{:S(2)}, u32[]{:S(2)}) collective-permute-start(bf16[256,1408]{1,0:T(8,128)(2,1)} %collective-permute-done.16.refs_14_.refs_0_), channel_id=1, source_target_pairs={{0,4},{2,6},{4,0},{6,2},{8,12},{10,14},{12,8},{14,10},{16,20},{18,... | collective-permute-start | bytes 2162696 | tf_op jit(solution)/shard_map/ppermute | solution.py:32
  227.8 33.3 %collective-permute-start.24 = (bf16[256,1408]{1,0:T(8,128)(2,1)}, bf16[256,1408]{1,0:T(8,128)(2,1)S(1)}, u32[]{:S(2)}, u32[]{:S(2)}) collective-permute-start(bf16[256,1408]{1,0:T(8,128)(2,1)} %collective-permute-done.17.refs_2_.refs_18_), channel_id=1, source_target_pairs={{0,4},{2,6},{4,0},{6,2},{8,12},{10,14},{12,8},{14,10},{16,20},{18,... | collective-permute-start | bytes 2162696 | tf_op jit(solution)/shard_map/ppermute | solution.py:32
  261.1 60.4 %copy-start.32 = (bf16[256,1408]{1,0:T(8,128)(2,1)}, bf16[256,1408]{1,0:T(8,128)(2,1)S(1)}, u32[]{:S(2)}) copy-start(bf16[256,1408]{1,0:T(8,128)(2,1)S(1)} %collective-permute-done.22.refs_8_.refs_0_) | copy-start | bytes 2162692
  261.1 9.4 %collective-permute-start.29 = (bf16[512,4096]{1,0:T(8,128)(2,1)S(1)}, bf16[512,4096]{1,0:T(8,128)(2,1)S(1)}, u32[]{:S(2)}, u32[]{:S(2)}) collective-permute-start(bf16[512,4096]{1,0:T(8,128)(2,1)S(1)} %shard_map.143.refs_0_.refs_2_.refs_4_.refs_6_.refs_8_), channel_id=1, source_target_pairs={{0,2},{2,0},{4,6},{6,4},{8,10},{10,8},{12,14},{14,12},{16,18},{18,... | collective-permute-start | bytes 12582920 | tf_op jit(solution)/shard_map/ppermute | solution.py:32
  261.2 22.3 %collective-permute-start.26 = (bf16[256,1408]{1,0:T(8,128)(2,1)}, bf16[256,1408]{1,0:T(8,128)(2,1)S(1)}, u32[]{:S(2)}, u32[]{:S(2)}) collective-permute-start(bf16[256,1408]{1,0:T(8,128)(2,1)} %get-tuple-element.392), channel_id=1, source_target_pairs={{0,24},{2,26},{4,28},{6,30},{8,16},{10,18},{12,20},{14,22},{16,8},... | collective-permute-start | bytes 2162696 | tf_op jit(solution)/shard_map/ppermute | solution.py:32
  263.1 20.5 %collective-permute-start.27 = (bf16[256,1408]{1,0:T(8,128)(2,1)S(1)}, bf16[256,1408]{1,0:T(8,128)(2,1)S(1)}, u32[]{:S(2)}, u32[]{:S(2)}) collective-permute-start(bf16[256,1408]{1,0:T(8,128)(2,1)S(1)} %collective-permute-done.21.refs_2_.refs_6_), channel_id=1, source_target_pairs={{0,4},{2,6},{4,0},{6,2},{8,12},{10,14},{12,8},{14,10},{16,20},{18,... | collective-permute-start | bytes 2162696 | tf_op jit(solution)/shard_map/ppermute | solution.py:32
  263.6 33.1 %collective-permute-start.28 = (bf16[256,1408]{1,0:T(8,128)(2,1)S(1)}, bf16[256,1408]{1,0:T(8,128)(2,1)S(1)}, u32[]{:S(2)}, u32[]{:S(2)}) collective-permute-start(bf16[256,1408]{1,0:T(8,128)(2,1)S(1)} %collective-permute-done.22.refs_8_.refs_0_), channel_id=1, source_target_pairs={{0,4},{2,6},{4,0},{6,2},{8,12},{10,14},{12,8},{14,10},{16,20},{18,... | collective-permute-start | bytes 2162696 | tf_op jit(solution)/shard_map/ppermute | solution.py:32
  296.7 2.7 collective-permute-start.31
  296.7 21.4 %collective-permute-start.33 = (bf16[512,1024]{1,0:T(8,128)(2,1)S(1)}, bf16[512,1024]{1,0:T(8,128)(2,1)S(1)}, u32[]{:S(2)}, u32[]{:S(2)}) collective-permute-start(bf16[512,1024]{1,0:T(8,128)(2,1)S(1)} %get-tuple-element.418), channel_id=1, source_target_pairs={{0,2},{2,0},{4,6},{6,4},{8,10},{10,8},{12,14},{14,12},{16,18},{18,... | collective-permute-start | bytes 3145736 | tf_op jit(solution)/shard_map/ppermute | solution.py:32
  297.2 22.1 %collective-permute-start.30 = (bf16[256,1408]{1,0:T(8,128)(2,1)S(1)}, bf16[256,1408]{1,0:T(8,128)(2,1)S(1)}, u32[]{:S(2)}, u32[]{:S(2)}) collective-permute-start(bf16[256,1408]{1,0:T(8,128)(2,1)S(1)} %collective-permute-done.26.refs_10_.refs_2_), channel_id=1, source_target_pairs={{0,4},{2,6},{4,0},{6,2},{8,12},{10,14},{12,8},{14,10},{16,20},{18,... | collective-permute-start | bytes 2162696 | tf_op jit(solution)/shard_map/ppermute | solution.py:32
  297.8 20.3 %collective-permute-start.34 = (bf16[32,2048]{1,0:T(8,128)(2,1)S(1)}, bf16[32,2048]{1,0:T(8,128)(2,1)S(1)}, u32[]{:S(2)}, u32[]{:S(2)}) collective-permute-start(bf16[32,2048]{1,0:T(8,128)(2,1)S(1)} %select_convert_fusion.1), channel_id=1, source_target_pairs={{0,4},{2,6},{4,0},{6,2},{8,12},{10,14},{12,8},{14,10},{16,20},{18,... | collective-permute-start | bytes 393224 | tf_op jit(solution)/shard_map/ppermute | solution.py:32
  300.5 18.8 %collective-permute-start.32 = (bf16[256,1024]{1,0:T(8,128)(2,1)S(1)}, bf16[256,1024]{1,0:T(8,128)(2,1)S(1)}, u32[]{:S(2)}, u32[]{:S(2)}) collective-permute-start(bf16[256,1024]{1,0:T(8,128)(2,1)S(1)} %get-tuple-element.416), channel_id=1, source_target_pairs={{0,8},{2,10},{4,12},{6,14},{8,0},{10,2},{12,4},{14,6},{16,24},{18,... | collective-permute-start | bytes 1572872 | tf_op jit(solution)/shard_map/ppermute | solution.py:32
  319.3 17.3 %collective-permute-start.36 = (bf16[512,1024]{1,0:T(8,128)(2,1)}, bf16[512,1024]{1,0:T(8,128)(2,1)S(1)}, u32[]{:S(2)}, u32[]{:S(2)}) collective-permute-start(bf16[512,1024]{1,0:T(8,128)(2,1)} %get-tuple-element.440), channel_id=1, source_target_pairs={{0,2},{2,0},{4,6},{6,4},{8,10},{10,8},{12,14},{14,12},{16,18},{18,... | collective-permute-start | bytes 3145736 | tf_op jit(solution)/shard_map/ppermute | solution.py:32
  319.4 14.1 %collective-permute-start.35 = (bf16[32,2048]{1,0:T(8,128)(2,1)S(1)}, bf16[32,2048]{1,0:T(8,128)(2,1)S(1)}, u32[]{:S(2)}, u32[]{:S(2)}) collective-permute-start(bf16[32,2048]{1,0:T(8,128)(2,1)S(1)} %convert_element_type.101), channel_id=1, source_target_pairs={{0,8},{2,10},{4,12},{6,14},{8,0},{10,2},{12,4},{14,6},{16,24},{18,... | collective-permute-start | bytes 393224 | tf_op jit(solution)/shard_map/ppermute | solution.py:32
  319.8 16.8 %collective-permute-start.37 = (bf16[256,1024]{1,0:T(8,128)(2,1)S(1)}, bf16[256,1024]{1,0:T(8,128)(2,1)S(1)}, u32[]{:S(2)}, u32[]{:S(2)}) collective-permute-start(bf16[256,1024]{1,0:T(8,128)(2,1)S(1)} %get-tuple-element.441), channel_id=1, source_target_pairs={{0,8},{2,10},{4,12},{6,14},{8,0},{10,2},{12,4},{14,6},{16,24},{18,... | collective-permute-start | bytes 1572872 | tf_op jit(solution)/shard_map/ppermute | solution.py:32
  336.6 2.9 collective-permute-start.38
  341.4 10.7 %collective-permute-start.39 = (bf16[512,1024]{1,0:T(8,128)(2,1)}, bf16[512,1024]{1,0:T(8,128)(2,1)}, u32[]{:S(2)}, u32[]{:S(2)}) collective-permute-start(bf16[512,1024]{1,0:T(8,128)(2,1)} %convolution_convert_fusion.2), channel_id=1, source_target_pairs={{0,2},{2,0},{4,6},{6,4},{8,10},{10,8},{12,14},{14,12},{16,18},{18,... | collective-permute-start | bytes 3145736 | tf_op jit(solution)/shard_map/ppermute | solution.py:32
  347.8 13.9 %collective-permute-start.40 = (bf16[256,1024]{1,0:T(8,128)(2,1)S(1)}, bf16[256,1024]{1,0:T(8,128)(2,1)S(1)}, u32[]{:S(2)}, u32[]{:S(2)}) collective-permute-start(bf16[256,1024]{1,0:T(8,128)(2,1)S(1)} %copy-done.85), channel_id=1, source_target_pairs={{0,8},{2,10},{4,12},{6,14},{8,0},{10,2},{12,4},{14,6},{16,24},{18,... | collective-permute-start | bytes 1572872 | tf_op jit(solution)/shard_map/ppermute | solution.py:32
  361.6 6.1 %collective-permute-start.44 = (f32[512,1]{1,0:T(8,128)S(1)}, f32[512,1]{1,0:T(8,128)S(1)}, u32[]{:S(2)}, u32[]{:S(2)}) collective-permute-start(f32[512,1]{1,0:T(8,128)S(1)} %slice.75), channel_id=1, source_target_pairs={{0,2},{2,0},{4,6},{6,4},{8,10},{10,8},{12,14},{14,12},{16,18},{18,... | collective-permute-start | bytes 6152 | tf_op jit(solution)/shard_map/ppermute | solution.py:32
  361.7 14.4 %collective-permute-start.43 = (bf16[256,1024]{1,0:T(8,128)(2,1)S(1)}, bf16[256,1024]{1,0:T(8,128)(2,1)S(1)}, u32[]{:S(2)}, u32[]{:S(2)}) collective-permute-start(bf16[256,1024]{1,0:T(8,128)(2,1)S(1)} %broadcast_select_fusion.1), channel_id=1, source_target_pairs={{0,1},{1,0},{2,3},{3,2},{4,5},{5,4},{6,7},{7,6},{8,9},{9,8},{10,11... | collective-permute-start | bytes 1572872 | tf_op jit(solution)/shard_map/ppermute | solution.py:36
  363.3 4.6 %collective-permute-start.41 = (bf16[512,1024]{1,0:T(8,128)(2,1)S(1)}, bf16[512,1024]{1,0:T(8,128)(2,1)S(1)}, u32[]{:S(2)}, u32[]{:S(2)}) collective-permute-start(bf16[512,1024]{1,0:T(8,128)(2,1)S(1)} %convolution_convert_fusion.1), channel_id=1, source_target_pairs={{0,2},{2,0},{4,6},{6,4},{8,10},{10,8},{12,14},{14,12},{16,18},{18,... | collective-permute-start | bytes 3145736 | tf_op jit(solution)/shard_map/ppermute | solution.py:32
  363.5 14.1 %collective-permute-start.42 = (bf16[256,1024]{1,0:T(8,128)(2,1)S(1)}, bf16[256,1024]{1,0:T(8,128)(2,1)S(1)}, u32[]{:S(2)}, u32[]{:S(2)}) collective-permute-start(bf16[256,1024]{1,0:T(8,128)(2,1)S(1)} %fusion.9), channel_id=1, source_target_pairs={{0,8},{2,10},{4,12},{6,14},{8,0},{10,2},{12,4},{14,6},{16,24},{18,... | collective-permute-start | bytes 1572872 | tf_op jit(solution)/shard_map/ppermute | solution.py:32
  377.6 8.9 %collective-permute-start.45 = (bf16[512,1024]{1,0:T(8,128)(2,1)S(1)}, bf16[512,1024]{1,0:T(8,128)(2,1)S(1)}, u32[]{:S(2)}, u32[]{:S(2)}) collective-permute-start(bf16[512,1024]{1,0:T(8,128)(2,1)S(1)} %convolution_convert_fusion), channel_id=1, source_target_pairs={{0,2},{2,0},{4,6},{6,4},{8,10},{10,8},{12,14},{14,12},{16,18},{18,... | collective-permute-start | bytes 3145736 | tf_op jit(solution)/shard_map/ppermute | solution.py:32
  377.7 8.8 %collective-permute-start.48 = (f32[256,1]{1,0:T(8,128)S(1)}, f32[256,1]{1,0:T(8,128)S(1)}, u32[]{:S(2)}, u32[]{:S(2)}) collective-permute-start(f32[256,1]{1,0:T(8,128)S(1)} %get-tuple-element.500), channel_id=1, source_target_pairs={{0,8},{2,10},{4,12},{6,14},{8,0},{10,2},{12,4},{14,6},{16,24},{18,... | collective-permute-start | bytes 3080 | tf_op jit(solution)/shard_map/ppermute | solution.py:32
  378.1 16.7 %collective-permute-start.46 = (bf16[256,1024]{1,0:T(8,128)(2,1)S(1)}, bf16[256,1024]{1,0:T(8,128)(2,1)S(1)}, u32[]{:S(2)}, u32[]{:S(2)}) collective-permute-start(bf16[256,1024]{1,0:T(8,128)(2,1)S(1)} %fusion.10), channel_id=1, source_target_pairs={{0,8},{2,10},{4,12},{6,14},{8,0},{10,2},{12,4},{14,6},{16,24},{18,... | collective-permute-start | bytes 1572872 | tf_op jit(solution)/shard_map/ppermute | solution.py:32
  379.8 15.1 %collective-permute-start.47 = (bf16[256,1024]{1,0:T(8,128)(2,1)S(1)}, bf16[256,1024]{1,0:T(8,128)(2,1)S(1)}, u32[]{:S(2)}, u32[]{:S(2)}) collective-permute-start(bf16[256,1024]{1,0:T(8,128)(2,1)S(1)} %fusion.7.refs_1_), channel_id=1, source_target_pairs={{0,1},{1,0},{2,3},{3,2},{4,5},{5,4},{6,7},{7,6},{8,9},{9,8},{10,11... | collective-permute-start | bytes 1572872 | tf_op jit(solution)/shard_map/ppermute | solution.py:36
  394.8 9.6 %collective-permute-start.51 = (bf16[512,1024]{1,0:T(8,128)(2,1)S(1)}, bf16[512,1024]{1,0:T(8,128)(2,1)S(1)}, u32[]{:S(2)}, u32[]{:S(2)}) collective-permute-start(bf16[512,1024]{1,0:T(8,128)(2,1)S(1)} %get-tuple-element.512), channel_id=1, source_target_pairs={{0,2},{2,0},{4,6},{6,4},{8,10},{10,8},{12,14},{14,12},{16,18},{18,... | collective-permute-start | bytes 3145736 | tf_op jit(solution)/shard_map/ppermute | solution.py:32
  394.9 9.6 %collective-permute-start.53 = (bf16[32,2048]{1,0:T(8,128)(2,1)S(1)}, bf16[32,2048]{1,0:T(8,128)(2,1)S(1)}, u32[]{:S(2)}, u32[]{:S(2)}) collective-permute-start(bf16[32,2048]{1,0:T(8,128)(2,1)S(1)} %convert_element_type.123), channel_id=1, source_target_pairs={{0,16},{2,18},{4,20},{6,22},{8,24},{10,26},{12,28},{14,30},{16,0},... | collective-permute-start | bytes 393224 | tf_op jit(solution)/shard_map/ppermute | solution.py:32
  395.8 6.3 %collective-permute-start.52 = (f32[256,1]{1,0:T(8,128)S(1)}, f32[256,1]{1,0:T(8,128)S(1)}, u32[]{:S(2)}, u32[]{:S(2)}) collective-permute-start(f32[256,1]{1,0:T(8,128)S(1)} %add.83), channel_id=1, source_target_pairs={{0,1},{1,0},{2,3},{3,2},{4,5},{5,4},{6,7},{7,6},{8,9},{9,8},{10,11... | collective-permute-start | bytes 3080 | tf_op jit(solution)/shard_map/ppermute | solution.py:36
  396.3 16.6 %collective-permute-start.49 = (bf16[256,1024]{1,0:T(8,128)(2,1)S(1)}, bf16[256,1024]{1,0:T(8,128)(2,1)S(1)}, u32[]{:S(2)}, u32[]{:S(2)}) collective-permute-start(bf16[256,1024]{1,0:T(8,128)(2,1)S(1)} %fusion.11), channel_id=1, source_target_pairs={{0,8},{2,10},{4,12},{6,14},{8,0},{10,2},{12,4},{14,6},{16,24},{18,... | collective-permute-start | bytes 1572872 | tf_op jit(solution)/shard_map/ppermute | solution.py:32
  398.1 14.8 %collective-permute-start.50 = (bf16[256,1024]{1,0:T(8,128)(2,1)S(1)}, bf16[256,1024]{1,0:T(8,128)(2,1)S(1)}, u32[]{:S(2)}, u32[]{:S(2)}) collective-permute-start(bf16[256,1024]{1,0:T(8,128)(2,1)S(1)} %fusion.6.refs_0_), channel_id=1, source_target_pairs={{0,1},{1,0},{2,3},{3,2},{4,5},{5,4},{6,7},{7,6},{8,9},{9,8},{10,11... | collective-permute-start | bytes 1572872 | tf_op jit(solution)/shard_map/ppermute | solution.py:36
  412.9 7.4 %collective-permute-start.56 = (f32[32,2048]{1,0:T(8,128)S(1)}, f32[32,2048]{1,0:T(8,128)S(1)}, u32[]{:S(2)}, u32[]{:S(2)}) collective-permute-start(f32[32,2048]{1,0:T(8,128)S(1)} %convert_add_fusion.1), channel_id=1, source_target_pairs={{0,4},{2,6},{4,0},{6,2},{8,12},{10,14},{12,8},{14,10},{16,20},{18,... | collective-permute-start | bytes 786440 | tf_op jit(solution)/shard_map/ppermute | solution.py:32
  413.5 12.7 %collective-permute-start.54 = (bf16[256,1024]{1,0:T(8,128)(2,1)S(1)}, bf16[256,1024]{1,0:T(8,128)(2,1)S(1)}, u32[]{:S(2)}, u32[]{:S(2)}) collective-permute-start(bf16[256,1024]{1,0:T(8,128)(2,1)S(1)} %fusion.5.refs_3_), channel_id=1, source_target_pairs={{0,1},{1,0},{2,3},{3,2},{4,5},{5,4},{6,7},{7,6},{8,9},{9,8},{10,11... | collective-permute-start | bytes 1572872 | tf_op jit(solution)/shard_map/ppermute | solution.py:36
  414.9 12.4 %collective-permute-start.55 = (bf16[256,1024]{1,0:T(8,128)(2,1)S(1)}, bf16[256,1024]{1,0:T(8,128)(2,1)S(1)}, u32[]{:S(2)}, u32[]{:S(2)}) collective-permute-start(bf16[256,1024]{1,0:T(8,128)(2,1)S(1)} %get-tuple-element.530), channel_id=1, source_target_pairs={{0,8},{2,10},{4,12},{6,14},{8,0},{10,2},{12,4},{14,6},{16,24},{18,... | collective-permute-start | bytes 1572872 | tf_op jit(solution)/shard_map/ppermute | solution.py:32
  427.3 11.4 %collective-permute-start.57 = (bf16[256,1024]{1,0:T(8,128)(2,1)S(1)}, bf16[256,1024]{1,0:T(8,128)(2,1)S(1)}, u32[]{:S(2)}, u32[]{:S(2)}) collective-permute-start(bf16[256,1024]{1,0:T(8,128)(2,1)S(1)} %fusion.4.refs_2_), channel_id=1, source_target_pairs={{0,1},{1,0},{2,3},{3,2},{4,5},{5,4},{6,7},{7,6},{8,9},{9,8},{10,11... | collective-permute-start | bytes 1572872 | tf_op jit(solution)/shard_map/ppermute | solution.py:36
  428.0 11.4 %collective-permute-start.58 = (bf16[256,1024]{1,0:T(8,128)(2,1)S(1)}, bf16[256,1024]{1,0:T(8,128)(2,1)S(1)}, u32[]{:S(2)}, u32[]{:S(2)}) collective-permute-start(bf16[256,1024]{1,0:T(8,128)(2,1)S(1)} %get-tuple-element.548), channel_id=1, source_target_pairs={{0,8},{2,10},{4,12},{6,14},{8,0},{10,2},{12,4},{14,6},{16,24},{18,... | collective-permute-start | bytes 1572872 | tf_op jit(solution)/shard_map/ppermute | solution.py:32
  429.7 9.7 %collective-permute-start.59 = (f32[64,2048]{1,0:T(8,128)S(1)}, f32[64,2048]{1,0:T(8,128)S(1)}, u32[]{:S(2)}, u32[]{:S(2)}) collective-permute-start(f32[64,2048]{1,0:T(8,128)S(1)} %pad_maximum_fusion.1), channel_id=1, source_target_pairs={{0,2},{2,0},{4,6},{6,4},{8,10},{10,8},{12,14},{14,12},{16,18},{18,... | collective-permute-start | bytes 1572872 | tf_op jit(solution)/shard_map/ppermute | solution.py:32
  439.6 10.6 %collective-permute-start.60 = (bf16[256,1024]{1,0:T(8,128)(2,1)S(1)}, bf16[256,1024]{1,0:T(8,128)(2,1)S(1)}, u32[]{:S(2)}, u32[]{:S(2)}) collective-permute-start(bf16[256,1024]{1,0:T(8,128)(2,1)S(1)} %broadcast_select_fusion), channel_id=1, source_target_pairs={{0,1},{1,0},{2,3},{3,2},{4,5},{5,4},{6,7},{7,6},{8,9},{9,8},{10,11... | collective-permute-start | bytes 1572872 | tf_op jit(solution)/shard_map/ppermute | solution.py:36
  (85 other events, 561.8 us)
